TPU v7x, 32 devices: a whole 2x2x4 slice. The times are simulated.
32 devices in a mesh: ctx: 16 (over z, y, core), wsh: 2 (over x).
Axes of the slice: x: 2, y: 2, z: 4, core: 2. Of those that a mesh axis runs over, the one named last changes fastest.
Arguments:
- tokens: bfloat16 [4, 2048, 1024], P('wsh', 'ctx'), may hold values from -6 to 6
- cotangent: bfloat16 [4, 2048, 1024], P('wsh', 'ctx'), may hold values from -6 to 6
- lengths: int32 [4, 4], P('wsh'), may hold values from 1 to 1536, as said below
- dealing: int32 [4, 16], P('wsh'), may hold values from 0 to 15, as said below
- gain_one: bfloat16 [1024], P('wsh'), may hold values from 0.099609375 to 1.8984375
- bias_one: bfloat16 [1024], P('wsh'), may hold values from -3 to 3
- gain_two: bfloat16 [1024], P('wsh'), may hold values from 0.099609375 to 1.8984375
- bias_two: bfloat16 [1024], P('wsh'), may hold values from -3 to 3
- w_qkv: bfloat16 [1024, 3072], P('wsh'), may hold values from -0.1875 to 0.1875
- w_out: bfloat16 [1024, 1024], P('wsh'), may hold values from -1.5 to 1.5
- w_up: bfloat16 [1024, 4096], P('wsh'), may hold values from -0.1875 to 0.1875
- w_down: bfloat16 [4096, 1024], P('wsh'), may hold values from -0.09375 to 0.09375
Outputs:
- out: bfloat16 [4, 2048, 1024], P('wsh', 'ctx')
- grad_tokens: float32 [4, 2048, 1024], P('wsh', 'ctx')
- grad_gain_one: float32 [1024], P(('ctx', 'wsh'))
- grad_bias_one: float32 [1024], P(('ctx', 'wsh'))
- grad_gain_two: float32 [1024], P(('ctx', 'wsh'))
- grad_bias_two: float32 [1024], P(('ctx', 'wsh'))
- grad_qkv: float32 [1024, 3072], P(('ctx', 'wsh'))
- grad_out: float32 [1024, 1024], P(('ctx', 'wsh'))
- grad_up: float32 [1024, 4096], P(('ctx', 'wsh'))
- grad_down: float32 [4096, 1024], P(('ctx', 'wsh'))
Inputs may be any that keep to these rules, and one draw needn't show every extreme that they name: Each row holds 4 lengths in packed order that sum to 2048; one of them is exactly 1536. Each row is a permutation of 0 to 15: dealt block j (dealt tokens j * 128 to (j + 1) * 128 - 1) holds packed block dealing[g, j].
All inputs are finite; a program needn't handle non-finite values.
Results may differ from a plain program's by a relative error of at most 0.015.
Values may be sent and summed in bfloat16 or wider, within the bound.
A program may use at most 512 MiB of HBM per device.

v0:
```python
import jax
import jax.numpy as jnp
from jax import lax
from jax.sharding import PartitionSpec as P

D = 1024
H = 16
HD = 64
ROT = 16
BLK = 128


EPSILON = 1e-05
MASKED = -1e30
WIDE = jnp.float32
NARROW = jnp.bfloat16


def norm_layer(values_in, scale_by, shift_by):
    average = jnp.mean(values_in, axis=-1, keepdims=True)
    centred = values_in - average
    variance = jnp.mean(centred * centred, axis=-1, keepdims=True)
    return centred * lax.rsqrt(variance + EPSILON) * scale_by + shift_by


def rotate(values_in, places):
    split_at = ROT // 2
    frequency = 10000.0 ** (-2.0 * jnp.arange(split_at, dtype=WIDE) / ROT)
    angles = places.astype(WIDE)[:, None] * frequency[None, :]
    cosine_table = jnp.cos(angles)[:, None, :]
    sine_table = jnp.sin(angles)[:, None, :]
    first_half = values_in[..., :split_at]
    second_half = values_in[..., split_at:ROT]
    return jnp.concatenate(
        [
            first_half * cosine_table - second_half * sine_table,
            second_half * cosine_table + first_half * sine_table,
            values_in[..., ROT:],
        ],
        axis=-1,
    )


def natural_rows(dealing_row, offset_row, row_count):
    ordinal = offset_row + jnp.arange(row_count, dtype=jnp.int32)
    table_ids = jnp.arange(dealing_row.shape[0], dtype=jnp.int32)
    picked = jnp.sum(
        jnp.where((ordinal // BLK)[:, None] == table_ids[None, :], dealing_row[None, :], 0), axis=1
    )
    return picked * BLK + ordinal % BLK


def sequence_openings(natural, lengths_row):
    openings = jnp.cumsum(lengths_row) - lengths_row
    return jnp.max(jnp.where(openings[None, :] <= natural[:, None], openings[None, :], 0), axis=1)


def score_block(queries, block_keys, offset_row, natural_q, opening_q, dealing_row):
    row_count = block_keys.shape[0]
    key_natural = natural_rows(dealing_row, offset_row, row_count)
    scores = jnp.einsum(
        "qhd,khd->hqk", queries, block_keys.reshape(row_count, H, HD), preferred_element_type=WIDE
    ) * HD ** (-0.5)
    allowed = (key_natural[None, :] <= natural_q[:, None]) & (
        key_natural[None, :] >= opening_q[:, None]
    )
    return (scores, allowed[None])


def fold_blocks(step_fn, state_in, arrays):
    row_count = arrays[0].shape[0]
    block_width = 1024
    stacked = tuple(
        (
            member.reshape((row_count // block_width, block_width) + member.shape[1:])
            for member in arrays
        )
    )
    offsets = jnp.arange(row_count // block_width, dtype=jnp.int32) * block_width

    def inner_step(state_now, block_item):
        return (step_fn(state_now, block_item[0], block_item[1]), None)

    state_out, _ = lax.scan(inner_step, state_in, (stacked, offsets))
    return state_out


def project(tokens_f, weights, places):
    w_qkv, w_out, w_up, w_down, gain_one, bias_one, gain_two, bias_two = weights
    all_rows = tokens_f.shape[0]
    normed_one = norm_layer(tokens_f, gain_one.astype(WIDE), bias_one.astype(WIDE)).astype(NARROW)
    normed_two = norm_layer(tokens_f, gain_two.astype(WIDE), bias_two.astype(WIDE)).astype(NARROW)
    mixed = jnp.dot(normed_one, w_qkv, preferred_element_type=WIDE).reshape(all_rows, 3, H, HD)
    queries = rotate(mixed[:, 0], places).astype(NARROW)
    keys_here = rotate(mixed[:, 1], places).astype(NARROW).reshape(all_rows, D)
    values_here = mixed[:, 2].astype(NARROW).reshape(all_rows, D)
    hidden = jnp.dot(normed_two, w_up, preferred_element_type=WIDE)
    activated = jax.nn.gelu(hidden, approximate=False).astype(NARROW)
    return (normed_one, normed_two, queries, keys_here, values_here, hidden, activated)


def attend(queries, keys_here, values_here, natural_q, opening_q, dealing_row):
    local_rows = queries.shape[0]

    def max_step(state_in, block_arrays, offset_row):
        row_top, row_total = state_in
        scores, allowed = score_block(
            queries, block_arrays[0], offset_row, natural_q, opening_q, dealing_row
        )
        new_top = jnp.maximum(row_top, jnp.max(jnp.where(allowed, scores, MASKED), axis=-1))
        kept_terms = jnp.where(allowed, jnp.exp(scores - new_top[..., None]), 0.0)
        return (new_top, row_total * jnp.exp(row_top - new_top) + jnp.sum(kept_terms, axis=-1))

    start_state = (jnp.full((H, local_rows), MASKED, WIDE), jnp.zeros((H, local_rows), WIDE))
    row_top, row_total = fold_blocks(
        max_step, start_state, (lax.all_gather(keys_here, "ctx", axis=0, tiled=True),)
    )
    log_total = row_top + jnp.log(row_total)

    def value_step(state_in, block_arrays, offset_row):
        scores, allowed = score_block(
            queries, block_arrays[0], offset_row, natural_q, opening_q, dealing_row
        )
        soft_probs = jnp.where(allowed, jnp.exp(scores - log_total[..., None]), 0.0).astype(NARROW)
        row_count = block_arrays[1].shape[0]
        return state_in + jnp.einsum(
            "hqk,khd->qhd",
            soft_probs,
            block_arrays[1].reshape(row_count, H, HD),
            preferred_element_type=WIDE,
        )

    attended = fold_blocks(
        value_step,
        jnp.zeros((local_rows, H, HD), WIDE),
        (
            lax.all_gather(keys_here, "ctx", axis=0, tiled=True),
            lax.all_gather(values_here, "ctx", axis=0, tiled=True),
        ),
    )
    return (attended, log_total)


def attention_back(
    queries,
    keys_here,
    values_here,
    g_attended,
    row_dot,
    log_total,
    natural_q,
    opening_q,
    dealing_row,
):
    local_rows = queries.shape[0]
    scale_factor = HD ** (-0.5)
    gathered_keys, gathered_values = (
        lax.all_gather(keys_here, "ctx", axis=0, tiled=True),
        lax.all_gather(values_here, "ctx", axis=0, tiled=True),
    )
    group_rows = gathered_keys.shape[0]
    key_span = 1024

    def key_block(state_in, block_item):
        block_keys, block_values, offset_row = block_item
        scores, allowed = score_block(
            queries, block_keys, offset_row, natural_q, opening_q, dealing_row
        )
        soft_probs = jnp.where(allowed, jnp.exp(scores - log_total[..., None]), 0.0)
        g_probs = jnp.einsum(
            "qhd,khd->hqk",
            g_attended,
            block_values.reshape(key_span, H, HD),
            preferred_element_type=WIDE,
        )
        g_scores = (soft_probs * (g_probs - row_dot[..., None])).astype(NARROW)
        state_out = (
            state_in
            + jnp.einsum(
                "hqk,khd->qhd",
                g_scores,
                block_keys.reshape(key_span, H, HD),
                preferred_element_type=WIDE,
            )
            * scale_factor
        )
        key_terms = (
            jnp.einsum("hqk,qhd->khd", g_scores, queries, preferred_element_type=WIDE)
            * scale_factor
        )
        value_terms = jnp.einsum(
            "hqk,qhd->khd", soft_probs.astype(NARROW), g_attended, preferred_element_type=WIDE
        )
        return (
            state_out,
            jnp.concatenate(
                [key_terms.reshape(key_span, D), value_terms.reshape(key_span, D)], axis=1
            ),
        )

    block_total = group_rows // key_span
    block_starts = jnp.arange(block_total, dtype=jnp.int32) * key_span
    stacked_blocks = (
        gathered_keys.reshape(block_total, key_span, D),
        gathered_values.reshape(block_total, key_span, D),
        block_starts,
    )
    g_queries, stacked_terms = lax.scan(
        key_block, jnp.zeros((local_rows, H, HD), WIDE), stacked_blocks
    )
    g_pairs = lax.psum_scatter(
        stacked_terms.reshape(group_rows, 2 * D), "ctx", scatter_dimension=0, tiled=True
    )
    g_keys = g_pairs[:, :D].reshape(local_rows, H, HD)
    g_values = g_pairs[:, D:].reshape(local_rows, H, HD)
    return (g_queries, g_keys, g_values)


def shards(
    tokens,
    cotangent,
    lengths,
    dealing,
    gain_one,
    bias_one,
    gain_two,
    bias_two,
    w_qkv,
    w_out,
    w_up,
    w_down,
):
    group_count = tokens.shape[0]
    local_rows = tokens.shape[1]
    all_rows = group_count * local_rows
    tokens_f = tokens.reshape(all_rows, D).astype(WIDE)
    first_row = lax.axis_index("ctx") * local_rows
    natural_list = [
        natural_rows(dealing[member], first_row, local_rows) for member in range(group_count)
    ]
    opening_list = [
        sequence_openings(natural_list[member], lengths[member]) for member in range(group_count)
    ]
    places = jnp.concatenate(
        [natural_list[member] - opening_list[member] for member in range(group_count)], axis=0
    )

    def forward():
        weights = (
            lax.all_gather(w_qkv, "wsh", axis=0, tiled=True),
            lax.all_gather(w_out, "wsh", axis=0, tiled=True),
            lax.all_gather(w_up, "wsh", axis=0, tiled=True),
            lax.all_gather(w_down, "wsh", axis=0, tiled=True),
            lax.all_gather(gain_one, "wsh", axis=0, tiled=True),
            lax.all_gather(bias_one, "wsh", axis=0, tiled=True),
            lax.all_gather(gain_two, "wsh", axis=0, tiled=True),
            lax.all_gather(bias_two, "wsh", axis=0, tiled=True),
        )
        local_parts = project(tokens_f, weights, places)
        attended_list = []
        total_list = []
        for member in range(group_count):
            rows_from = member * local_rows
            attended_one, total_one = attend(
                local_parts[2][rows_from : rows_from + local_rows],
                local_parts[3][rows_from : rows_from + local_rows],
                local_parts[4][rows_from : rows_from + local_rows],
                natural_list[member],
                opening_list[member],
                dealing[member],
            )
            attended_list.append(attended_one)
            total_list.append(total_one)
        return (weights, local_parts, jnp.concatenate(attended_list, axis=0), total_list)

    weights, local_parts, attended, total_list = forward()
    attended_low = attended.reshape(all_rows, D).astype(NARROW)
    mixed_out = (
        tokens_f
        + jnp.dot(attended_low, weights[1], preferred_element_type=WIDE)
        + jnp.dot(local_parts[6], weights[3], preferred_element_type=WIDE)
    )
    out = mixed_out.astype(NARROW)
    weights, local_parts, attended, total_list = forward()
    attended_low = attended.reshape(all_rows, D).astype(NARROW)
    w_qkv_all, w_out_all, w_up_all, w_down_all = (weights[0], weights[1], weights[2], weights[3])
    normed_one, normed_two, queries, keys_here, values_here, hidden, activated = local_parts
    grad_rows = cotangent.reshape(all_rows, D)
    grad_f = grad_rows.astype(WIDE)
    g_down = jnp.einsum("tf,td->fd", activated, grad_rows, preferred_element_type=WIDE)
    g_activated = jnp.einsum("td,fd->tf", grad_rows, w_down_all, preferred_element_type=WIDE)
    _, gelu_back = jax.vjp(lambda pre_act: jax.nn.gelu(pre_act, approximate=False), hidden)
    g_hidden = gelu_back(g_activated)[0].astype(NARROW)
    g_up = jnp.einsum("td,tf->df", normed_two, g_hidden, preferred_element_type=WIDE)
    g_normed_two = jnp.einsum("tf,df->td", g_hidden, w_up_all, preferred_element_type=WIDE)
    g_weight_out = jnp.einsum("te,td->ed", attended_low, grad_rows, preferred_element_type=WIDE)
    g_attended = (
        jnp.einsum("td,ed->te", grad_rows, w_out_all, preferred_element_type=WIDE)
        .astype(NARROW)
        .reshape(all_rows, H, HD)
    )
    row_dot = jnp.einsum("qhd,qhd->hq", g_attended.astype(WIDE), attended)
    query_grads = []
    key_grads = []
    value_grads = []
    for member in range(group_count):
        rows_from = member * local_rows
        rows_to = rows_from + local_rows
        g_q, g_k, g_v = attention_back(
            queries[rows_from:rows_to],
            keys_here[rows_from:rows_to],
            values_here[rows_from:rows_to],
            g_attended[rows_from:rows_to],
            row_dot[:, rows_from:rows_to],
            total_list[member],
            natural_list[member],
            opening_list[member],
            dealing[member],
        )
        query_grads.append(g_q)
        key_grads.append(g_k)
        value_grads.append(g_v)
    g_queries = jnp.concatenate(query_grads, axis=0)
    g_keys = jnp.concatenate(key_grads, axis=0)
    g_values = jnp.concatenate(value_grads, axis=0)
    _, rotate_back = jax.vjp(
        lambda pre_rot: rotate(pre_rot, places), jnp.zeros((all_rows, H, HD), WIDE)
    )
    g_queries_pre = rotate_back(g_queries)[0]
    g_keys_pre = rotate_back(g_keys)[0]
    g_mixed = (
        jnp.stack([g_queries_pre, g_keys_pre, g_values], axis=1)
        .reshape(all_rows, 3 * D)
        .astype(NARROW)
    )
    g_qkv = jnp.einsum("td,te->de", normed_one, g_mixed, preferred_element_type=WIDE)
    g_normed_one = jnp.einsum("te,de->td", g_mixed, w_qkv_all, preferred_element_type=WIDE)

    def both_norms(tokens_in, scale_one, shift_one, scale_two, shift_two):
        return (
            norm_layer(tokens_in, scale_one, shift_one),
            norm_layer(tokens_in, scale_two, shift_two),
        )

    _, norm_back = jax.vjp(
        both_norms,
        tokens_f,
        weights[4].astype(WIDE),
        weights[5].astype(WIDE),
        weights[6].astype(WIDE),
        weights[7].astype(WIDE),
    )
    g_tokens, g_scale_one, g_shift_one, g_scale_two, g_shift_two = norm_back(
        (g_normed_one, g_normed_two)
    )
    grad_tokens = g_tokens + grad_f
    summed = (
        lax.psum_scatter(g_qkv, ("ctx", "wsh"), scatter_dimension=0, tiled=True),
        lax.psum_scatter(g_weight_out, ("ctx", "wsh"), scatter_dimension=0, tiled=True),
        lax.psum_scatter(g_up, ("ctx", "wsh"), scatter_dimension=0, tiled=True),
        lax.psum_scatter(g_down, ("ctx", "wsh"), scatter_dimension=0, tiled=True),
        lax.psum_scatter(g_scale_one, ("ctx", "wsh"), scatter_dimension=0, tiled=True),
        lax.psum_scatter(g_shift_one, ("ctx", "wsh"), scatter_dimension=0, tiled=True),
        lax.psum_scatter(g_scale_two, ("ctx", "wsh"), scatter_dimension=0, tiled=True),
        lax.psum_scatter(g_shift_two, ("ctx", "wsh"), scatter_dimension=0, tiled=True),
    )
    return (
        out.reshape(group_count, local_rows, D),
        grad_tokens.reshape(group_count, local_rows, D),
        summed[4],
        summed[5],
        summed[6],
        summed[7],
        summed[0],
        summed[1],
        summed[2],
        summed[3],
    )


def solution(mesh):
    placed = (
        P("wsh", "ctx", None),
        P("wsh", "ctx", None),
        P("wsh", None),
        P("wsh", None),
        P("wsh"),
        P("wsh"),
        P("wsh"),
        P("wsh"),
        P("wsh", None),
        P("wsh", None),
        P("wsh", None),
        P("wsh", None),
    )
    return jax.shard_map(
        shards,
        mesh=mesh,
        in_specs=placed,
        out_specs=(
            P("wsh", "ctx", None),
            P("wsh", "ctx", None),
            P(("ctx", "wsh")),
            P(("ctx", "wsh")),
            P(("ctx", "wsh")),
            P(("ctx", "wsh")),
            P(("ctx", "wsh"), None),
            P(("ctx", "wsh"), None),
            P(("ctx", "wsh"), None),
            P(("ctx", "wsh"), None),
        ),
        check_vma=False,
    )
```

profile of v0, /device:TPU:0, one launch (start us, length us, event | category | flops | bytes accessed | tf_op | source)
XLA Modules:
  0.0 1940.8 jit_solution(146566531869979121)
XLA Ops:
  21.0 71.7 %all-gather.13.cloned.1.call-done = bf16[1024,3072]{1,0:T(8,128)(2,1)} async-done(((bf16[512,3072]{1,0:T(8,128)(2,1)}), bf16[1024,3072]{1,0:T(8,128)(2,1)}) %all-gather.13.cloned.1.call-update) | async-done | bytes 6291472 | tf_op jit(solution)/shard_map/all_gather | solution.py:250
  115.6 11.8 all-gather.23.cloned.1.call-done
  132.5 47.7 %all-gather.15.cloned.1.call-done = bf16[2048,1024]{1,0:T(8,128)(2,1)} async-done(((bf16[128,1024]{1,0:T(8,128)(2,1)}), bf16[2048,1024]{1,0:T(8,128)(2,1)}) %all-gather.15.cloned.1.call-update) | async-done | bytes 4194320 | tf_op jit(solution)/shard_map/all_gather | solution.py:138
  186.3 45.5 %all-gather.19.cloned.1.call-done = bf16[2048,1024]{1,0:T(8,128)(2,1)} async-done(((bf16[128,1024]{1,0:T(8,128)(2,1)}), bf16[2048,1024]{1,0:T(8,128)(2,1)}) %all-gather.19.cloned.1.call-update) | async-done | bytes 4194320 | tf_op jit(solution)/shard_map/all_gather | solution.py:138
  238.1 44.8 %all-gather.17.cloned.1.call-done = bf16[2048,1024]{1,0:T(8,128)(2,1)} async-done(((bf16[128,1024]{1,0:T(8,128)(2,1)}), bf16[2048,1024]{1,0:T(8,128)(2,1)}) %all-gather.17.cloned.1.call-update) | async-done | bytes 4194320 | tf_op jit(solution)/shard_map/all_gather | solution.py:137
  289.2 45.4 %all-gather.21.cloned.1.call-done = bf16[2048,1024]{1,0:T(8,128)(2,1)} async-done(((bf16[128,1024]{1,0:T(8,128)(2,1)}), bf16[2048,1024]{1,0:T(8,128)(2,1)}) %all-gather.21.cloned.1.call-update) | async-done | bytes 4194320 | tf_op jit(solution)/shard_map/all_gather | solution.py:137
  340.9 15.9 while.106
  356.9 23.0 %while.107 = (s32[]{:T(128)}, f32[128,16,64]{0,2,1:T(8,128)}, bf16[2,1024,1024]{1,2,0:T(8,128)(2,1)}, s32[2]{0:T(128)S(1)}, s32[1,16]{1,0:T(1,128)S(1)}, /*index...) while((s32[]{:T(128)}, f32[128,16,64]{0,2,1:T(8,128)}, ...), condition=%wide.region_23.24_spmd.clone, body=%wide.region_21.23_spmd.clone.sunk | while | flops 545993728 | bytes 14189791 | solution.py:84
  379.9 15.6 while.104
  395.6 23.1 %while.105 = (s32[]{:T(128)}, f32[128,16,64]{0,2,1:T(8,128)}, bf16[2,1024,1024]{1,2,0:T(8,128)(2,1)}, s32[2]{0:T(128)S(1)}, s32[1,16]{1,0:T(1,128)S(1)}, /*index...) while((s32[]{:T(128)}, f32[128,16,64]{0,2,1:T(8,128)}, ...), condition=%wide.region_15.16_spmd.clone, body=%wide.region_13.15_spmd.clone.sunk | while | flops 545993728 | bytes 14189791 | solution.py:84
  432.8 71.8 %while.109 = (s32[]{:T(128)}, f32[128,16,64]{0,2,1:T(8,128)S(1)}, f32[2,1024,2048]{2,1,0:T(8,128)}, bf16[2,1024,1024]{1,2,0:T(8,128)(2,1)}, s32[2]{0:T(128)S(1)}...) while((s32[]{:T(128)}, f32[128,16,64]{0,2,1:T(8,128)S(1)}, ...), condition=%wide.region_31.32_spmd.clone, body=%wide.region_29.31_spmd.clone.sunk | while | flops 1367159808 | bytes 113689840 | solution.py:208
  452.3 9.6 copy.172
  513.8 72.4 %while.108 = (s32[]{:T(128)}, f32[128,16,64]{0,2,1:T(8,128)S(1)}, f32[2,1024,2048]{2,1,0:T(8,128)}, bf16[2,1024,1024]{1,2,0:T(8,128)(2,1)}, s32[2]{0:T(128)S(1)}...) while((s32[]{:T(128)}, f32[128,16,64]{0,2,1:T(8,128)S(1)}, ...), condition=%wide.region_28.29_spmd.clone, body=%wide.region_26.28_spmd.clone.sunk | while | flops 1367159808 | bytes 113689840 | solution.py:208
  532.0 9.3 copy.171
  568.2 10.0 copy.171
  607.5 15.8 add_convert_fusion
  633.6 9.7 fusion.140
  645.5 81.6 %reduce-scatter.9.cloned.1.call-done = f32[128,2048]{1,0:T(8,128)} async-done(((f32[2048,2048]{1,0:T(8,128)}), f32[128,2048]{1,0:T(8,128)}) %reduce-scatter.9.cloned.1.call-update) | async-done | bytes 1048592 | tf_op jit(solution)/shard_map/reduce_scatter | solution.py:211
  730.2 178.3 %reduce-scatter.7.cloned.1.call-done = f32[128,2048]{1,0:T(8,128)} async-done(((f32[2048,2048]{1,0:T(8,128)}), f32[128,2048]{1,0:T(8,128)}) %reduce-scatter.7.cloned.1.call-update) | async-done | bytes 1048592 | tf_op jit(solution)/shard_map/reduce_scatter | solution.py:211
  938.1 39.9 %all-reduce.10 = (f32[1024]{0:T(1024)S(1)}, f32[1024]{0:T(1024)S(1)}, f32[1024]{0:T(1024)S(1)}, f32[1024]{0:T(1024)S(1)}) all-reduce(f32[1024]{0:T(1024)S(1)} %get-tuple-element.1373, f32[1024]{0:T(1024)S(1)} %get-tuple-element.1370, f32[1024]{0:T(1024)S(1)} %get-tuple-element.1364, ...), channel_id=4, replica_groups=mesh['ctx'=16,'wsh'=2] {'ctx','wsh'}, use_global_device_ids=true, to_apply=%region_37.38.clone | all-reduce | flops 4096 | bytes 32768
  983.5 68.8 %reduce-scatter.13.cloned.1.call-done = f32[32,1024]{1,0:T(8,128)} async-done(((f32[1024,1024]{1,0:T(8,128)}), f32[32,1024]{1,0:T(8,128)}) %reduce-scatter.13.cloned.1.call-update) | async-done | bytes 131088 | tf_op jit(solution)/shard_map/reduce_scatter | solution.py:359
  1052.4 356.8 %reduce-scatter.17.cloned.1.call-done = f32[128,1024]{1,0:T(8,128)} async-done(((f32[4096,1024]{1,0:T(8,128)}), f32[128,1024]{1,0:T(8,128)}) %reduce-scatter.17.cloned.1.call-update) | async-done | bytes 524304 | tf_op jit(solution)/shard_map/reduce_scatter | solution.py:361
  1409.2 361.5 %reduce-scatter.15.cloned.1.call-done = f32[32,4096]{1,0:T(8,128)} async-done(((f32[1024,4096]{1,0:T(8,128)}), f32[32,4096]{1,0:T(8,128)}) %reduce-scatter.15.cloned.1.call-update) | async-done | bytes 524304 | tf_op jit(solution)/shard_map/reduce_scatter | solution.py:360
  1770.7 163.2 %reduce-scatter.11.cloned.1.call-done = f32[32,3072]{1,0:T(8,128)} async-done(((f32[1024,3072]{1,0:T(8,128)}), f32[32,3072]{1,0:T(8,128)}) %reduce-scatter.11.cloned.1.call-update) | async-done | bytes 393232 | tf_op jit(solution)/shard_map/reduce_scatter | solution.py:358
  (367 shorter events, 352.8 us)
Async XLA Ops:
  7.2 85.5 %all-gather.13.cloned.1.call-start = ((), (), s32[]{:S(2)}) async-start(), calls=%async_computation.6 | async-start | bytes 9437184 | tf_op jit(solution)/shard_map/all_gather | solution.py:250
  7.9 119.4 %all-gather.23.cloned.1.call-start = ((), (), s32[]{:S(2)}) async-start(), calls=%async_computation.11 | async-start | bytes 3145728 | tf_op jit(solution)/shard_map/all_gather | solution.py:251
  8.7 171.5 %all-gather.15.cloned.1.call-start = ((), (), s32[]{:S(2)}) async-start(), calls=%async_computation.7 | async-start | bytes 4456448 | tf_op jit(solution)/shard_map/all_gather | solution.py:138
  109.4 122.5 %all-gather.19.cloned.1.call-start = ((), (), s32[]{:S(2)}) async-start(), calls=%async_computation.9 | async-start | bytes 4456448 | tf_op jit(solution)/shard_map/all_gather | solution.py:138
  110.3 172.6 %all-gather.17.cloned.1.call-start = ((), (), s32[]{:S(2)}) async-start(), calls=%async_computation.8 | async-start | bytes 4456448 | tf_op jit(solution)/shard_map/all_gather | solution.py:137
  112.9 221.7 %all-gather.21.cloned.1.call-start = ((), (), s32[]{:S(2)}) async-start(), calls=%async_computation.10 | async-start | bytes 4456448 | tf_op jit(solution)/shard_map/all_gather | solution.py:137
  113.8 13.6 copy-start.12
  113.8 486.0 %all-gather.25.cloned.1.call-start = ((), (), s32[]{:S(2)}) async-start(), calls=%async_computation.12 | async-start | bytes 12582912 | tf_op jit(solution)/shard_map/all_gather | solution.py:252
  114.5 492.9 %all-gather.27.cloned.1.call-start = ((), (), s32[]{:S(2)}) async-start(), calls=%async_computation.13 | async-start | bytes 12582912 | tf_op jit(solution)/shard_map/all_gather | solution.py:253
  115.3 611.7 %reduce-scatter.9.cloned.1.call-start = ((), (), s32[]{:S(2)}) async-start(), calls=%async_computation.15 | async-start | bytes 17825792 | tf_op jit(solution)/shard_map/reduce_scatter | solution.py:211
  418.6 14.1 copy-start
  418.6 14.1 copy-start.23
  418.6 14.1 copy-start.25
  418.6 14.1 copy-start.27
  418.6 14.1 copy-start.33
  505.4 403.2 %reduce-scatter.7.cloned.1.call-start = ((), (), s32[]{:S(2)}) async-start(), calls=%async_computation.14 | async-start | bytes 17825792 | tf_op jit(solution)/shard_map/reduce_scatter | solution.py:211
  586.2 466.2 %reduce-scatter.13.cloned.1.call-start = ((), (), s32[]{:S(2)}) async-start(), calls=%async_computation.17 | async-start | bytes 4325376 | tf_op jit(solution)/shard_map/reduce_scatter | solution.py:359
  590.1 819.1 %reduce-scatter.17.cloned.1.call-start = ((), (), s32[]{:S(2)}) async-start(), calls=%async_computation.19 | async-start | bytes 17301504 | tf_op jit(solution)/shard_map/reduce_scatter | solution.py:361
  607.5 15.8 copy-start.17
  633.5 1137.1 %reduce-scatter.15.cloned.1.call-start = ((), (), s32[]{:S(2)}) async-start(), calls=%async_computation.18 | async-start | bytes 17301504 | tf_op jit(solution)/shard_map/reduce_scatter | solution.py:360
  643.3 1290.5 %reduce-scatter.11.cloned.1.call-start = ((), (), s32[]{:S(2)}) async-start(), calls=%async_computation.16 | async-start | bytes 12976128 | tf_op jit(solution)/shard_map/reduce_scatter | solution.py:358
  728.1 184.1 %copy-start.30 = (f32[256,8]{0,1:T(8,128)S(1)}, f32[256,8]{0,1:T(8,128)}, u32[]{:S(2)}) copy-start(f32[256,8]{0,1:T(8,128)} %copy-done.29) | copy-start | bytes 24580
  728.1 184.1 %copy-start.32 = (f32[256,8]{0,1:T(8,128)S(1)}, f32[256,8]{0,1:T(8,128)}, u32[]{:S(2)}) copy-start(f32[256,8]{0,1:T(8,128)} %copy-done.31) | copy-start | bytes 24580
  920.6 14.4 slice-start
  (39 other events, 193.7 us)
Sparse Core Ops, SparseCore 0:
  9.6 83.0 all-gather.12
  94.2 33.1 all-gather.22
  129.6 50.5 all-gather.14
  182.7 49.0 all-gather.18
  233.8 49.0 all-gather.16
  285.5 49.0 all-gather.20
  336.1 102.4 all-gather.24
  440.2 104.0 all-gather.26
  548.4 178.5 reduce-scatter.8
  731.0 177.5 reduce-scatter.6
  911.4 140.9 reduce-scatter.12
  1055.1 354.0 reduce-scatter.16
  1412.0 358.6 reduce-scatter.14
  1777.1 156.6 reduce-scatter.10
where the time goes:
time: 1950 us; the launch traced here: 1940 us
  waiting for transfers between devices  1480 us (76%)
  local copies, waits for them, and re-layouts  185 us (9%)
  matrix products  139 us (7%)
  other arithmetic  61.1 us (3%)
  blocking collectives  58.1 us (3%)
    reduce_scatter x1, waiting for transfers between devices, shards(): lax.psum_scatter(g_up, ('ctx', 'wsh'), scatter_dimension=0, tiled=True)  362 us
    reduce_scatter x1, waiting for transfers between devices, shards(): lax.psum_scatter(g_down, ('ctx', 'wsh'), scatter_dimension=0, tiled=True)  357 us
    reduce_scatter x2, waiting for transfers between devices, attention_back(): lax.psum_scatter(stacked_terms.reshape(group_rows, 2 * D), 'ctx', scatter...  260 us
    reduce_scatter x1, waiting for transfers between devices, shards(): lax.psum_scatter(g_qkv, ('ctx', 'wsh'), scatter_dimension=0, tiled=True)  163 us
    all_gather x2, waiting for transfers between devices, attend(): lax.all_gather(values_here, 'ctx', axis=0, tiled=True)  93.2 us
    all_gather x2, waiting for transfers between devices, attend(): lax.all_gather(keys_here, 'ctx', axis=0, tiled=True)  90.2 us
    all_gather x1, waiting for transfers between devices, forward(): lax.all_gather(w_qkv, 'wsh', axis=0, tiled=True)  71.7 us
    dynamic_update_slice x8, local copies, waits for them, and re-layouts, attention_back(): lax.scan(key_block, jnp.zeros((local_rows, H, HD), WIDE), stacked_blocks)  69.3 us
  transfers between devices with their start and end apart: 14, of which 12 were waited for; matrix products, arithmetic and copies ran while one was open for 19% of the time, Pallas kernels for 0%

commit v1 on v0

--- a/solution.py
+++ b/solution.py
@@ -1,6 +1,10 @@
+import functools
+
 import jax
 import jax.numpy as jnp
 from jax import lax
+from jax.experimental import pallas as pl
+from jax.experimental.pallas import tpu as pltpu
 from jax.sharding import PartitionSpec as P
 
 D = 1024
@@ -378,6 +382,912 @@
     )
 
 
+MESH = pl.DeviceIdType.MESH
+NT = (((1,), (1,)), ((), ()))
+TN = (((0,), (0,)), ((), ()))
+VMEM_LIMIT = 60 * 1024 * 1024
+
+
+def dot(a, b, dims=(((1,), (0,)), ((), ()))):
+    return lax.dot_general(a, b, dims, preferred_element_type=WIDE)
+
+
+def pick(index, table):
+    result = jnp.int32(table[0])
+    for at in range(1, len(table)):
+        result = jnp.where(index == at, jnp.int32(table[at]), result)
+    return result
+
+
+def near_first(depth):
+    return [sorted(range(depth), key=lambda to, z=z: (abs(to - z), to)) for z in range(depth)]
+
+
+def pick2(row, column, table):
+    result = pick(column, table[0])
+    for at in range(1, len(table)):
+        result = jnp.where(row == at, pick(column, table[at]), result)
+    return result
+
+
+class Place:
+    def __init__(self, depth):
+        self.depth = depth
+        self.c = lax.axis_index("ctx")
+        self.x = lax.axis_index("wsh")
+        self.core = lax.rem(self.c, 2)
+        self.y = lax.rem(self.c // 2, 2)
+        self.z = self.c // 4
+        self.beside = (self.at(self.z, 1 - self.y, self.core), self.x)
+        self.twin = (self.at(self.z, self.y, 1 - self.core), self.x)
+        self.above = (self.at(self.z + 1, self.y, self.core), self.x)
+        self.below = (self.at(self.z - 1, self.y, self.core), self.x)
+        self.across = (self.c, 1 - self.x)
+        self.has_above = self.z < depth - 1
+        self.has_below = self.z > 0
+
+    def at(self, z, y, core):
+        return (z * 2 + y) * 2 + core
+
+    def greet(self):
+        barrier = pltpu.get_barrier_semaphore()
+
+        def hail(device):
+            pl.semaphore_signal(barrier, inc=1, device_id=device, device_id_type=MESH)
+
+        hail(self.beside)
+        hail(self.twin)
+        hail(self.across)
+
+        @pl.when(self.has_above)
+        def _():
+            hail(self.above)
+
+        @pl.when(self.has_below)
+        def _():
+            hail(self.below)
+
+        pl.semaphore_wait(
+            barrier, 3 + self.has_above.astype(jnp.int32) + self.has_below.astype(jnp.int32)
+        )
+
+
+def gather_kernel(
+    depth,
+    tok_ref,
+    cot_ref,
+    prm_ref,
+    turn_ref,
+    wqkv_ref,
+    wout_ref,
+    wup_ref,
+    wdown_ref,
+    heads_out,
+    units_out,
+    xhat_out,
+    cot_out,
+    g_up,
+    g_down,
+    g_sum,
+    wqkv_t,
+    wup_all,
+    wdown_part,
+    wout_part,
+    prm_all,
+    both,
+    xhat_all,
+    heads_buf,
+    units_buf,
+    wq_buf,
+    prm_buf,
+    in_sem,
+    w_sem,
+    wsend_sem,
+    wrecv_sem,
+    send_sem,
+    recv_sem,
+    out_sem,
+):
+    here = Place(depth)
+    c, x, y, z, core = here.c, here.x, here.y, here.z, here.core
+    count = depth * 4
+    rows = tok_ref.shape[0]
+    units = wup_all.shape[1]
+    half = prm_ref.shape[1]
+    order = near_first(depth)
+
+    own_in = (
+        pltpu.make_async_copy(tok_ref, both.at[c, pl.ds(0, rows)], in_sem.at[0]),
+        pltpu.make_async_copy(cot_ref, both.at[c, pl.ds(rows, rows)], in_sem.at[1]),
+    )
+    for copy in own_in:
+        copy.start()
+
+    pair = c // 2
+    per_half = count // 2
+    owner = c // per_half
+    inside = lax.rem(c, per_half)
+    shared = []
+    for part in range(3):
+        shared.append(
+            (
+                wqkv_ref.at[:, pl.ds(pl.multiple_of(part * D + pair * 128, 128), 128)],
+                wq_buf.at[x, part],
+            )
+        )
+    shared.append(
+        (
+            wup_ref.at[:, pl.ds(pl.multiple_of(c * units, 128), units)],
+            wup_all.at[pl.ds(pl.multiple_of(x * half, 128), half)],
+        )
+    )
+    shared.append((prm_ref, prm_buf.at[x]))
+    held = (
+        (wdown_ref.at[pl.ds(pl.multiple_of(inside * units, 128), units)], wdown_part),
+        (wout_ref.at[pl.ds(pl.multiple_of(inside * HD, HD), HD)], wout_part),
+    )
+    is_owner = owner == x
+    for at, (source, place) in enumerate(shared):
+        pltpu.make_async_copy(source, place, w_sem.at[at]).start()
+
+    @pl.when(is_owner)
+    def _():
+        for at, (source, place) in enumerate(held):
+            pltpu.make_async_copy(source, place, w_sem.at[5 + at]).start()
+
+    here.greet()
+
+    def remote(source, place, at):
+        return pltpu.make_async_remote_copy(
+            source,
+            place,
+            wsend_sem.at[at],
+            wrecv_sem.at[at],
+            device_id=here.across,
+            device_id_type=MESH,
+        )
+
+    for at, (source, place) in enumerate(shared):
+        remote(source, place, at).start()
+
+    @pl.when(is_owner)
+    def _():
+        for at, (source, place) in enumerate(held):
+            remote(source, place, 5 + at).start()
+
+    def passing(shard, way):
+        device = (here.beside, here.twin, here.above, here.below)[way]
+        return pltpu.make_async_remote_copy(
+            both.at[shard],
+            both.at[shard],
+            send_sem.at[way, shard],
+            recv_sem.at[shard],
+            device_id=device,
+            device_id_type=MESH,
+        )
+
+    for copy in own_in:
+        copy.wait()
+
+    def onward(shard, from_z):
+        passing(shard, 0).start()
+
+        @pl.when(jnp.logical_and(from_z <= z, here.has_above))
+        def _():
+            passing(shard, 2).start()
+
+        @pl.when(jnp.logical_and(from_z >= z, here.has_below))
+        def _():
+            passing(shard, 3).start()
+
+        passing(shard, 1).start()
+
+    onward(c, z)
+
+    for at, (source, place) in enumerate(shared):
+        pltpu.make_async_copy(source, place, w_sem.at[at]).wait()
+        remote(source, place, at).wait_recv()
+
+    @pl.when(is_owner)
+    def _():
+        for at, (source, place) in enumerate(held):
+            pltpu.make_async_copy(source, place, w_sem.at[5 + at]).wait()
+
+    @pl.when(jnp.logical_not(is_owner))
+    def _():
+        for at, (source, place) in enumerate(held):
+            remote(source, place, 5 + at).wait_recv()
+
+    odd = lax.rem(c, 2) == 1
+    for side in range(2):
+        prm_all[:, side * half : (side + 1) * half] = prm_buf[side]
+        for part in range(3):
+            turned = wq_buf[side, part].astype(WIDE).T
+            chosen = jnp.where(odd, turned[HD:], turned[:HD])
+            wqkv_t[part * HD : (part + 1) * HD, side * half : (side + 1) * half] = chosen.astype(
+                NARROW
+            )
+    g_up[...] = jnp.zeros_like(g_up)
+    g_down[...] = jnp.zeros_like(g_down)
+    g_sum[...] = jnp.zeros_like(g_sum)
+
+    def compute(shard):
+        tokens = both[shard, 0:rows, :].astype(WIDE)
+        average = jnp.mean(tokens, axis=-1, keepdims=True)
+        centred = tokens - average
+        variance = jnp.mean(centred * centred, axis=-1, keepdims=True)
+        xhat = centred * lax.rsqrt(variance + EPSILON)
+        xhat_low = xhat.astype(NARROW)
+        xhat_all[shard] = xhat_low
+        n_one = (xhat * prm_all[0:1, :] + prm_all[1:2, :]).astype(NARROW)
+        n_two = (xhat * prm_all[2:3, :] + prm_all[3:4, :]).astype(NARROW)
+        cotangent = both[shard, rows : 2 * rows, :]
+        mixed = dot(wqkv_t[...], n_one, NT)
+        turn = turn_ref[shard]
+        cosine, sine = turn[0:8], turn[8:16]
+        pieces = []
+        for base in (0, HD):
+            first, second = mixed[base : base + 8], mixed[base + 8 : base + 16]
+            pieces += [
+                first * cosine - second * sine,
+                second * cosine + first * sine,
+                mixed[base + 16 : base + HD],
+            ]
+        pieces.append(mixed[2 * HD : 3 * HD])
+        pieces.append(dot(wout_part[...], cotangent, NT))
+        heads_buf[shard] = jnp.concatenate(pieces, axis=0).astype(NARROW)
+        hidden = dot(n_two, wup_all[...])
+        spread = 0.5 * (1.0 + lax.erf(hidden * (0.5**0.5)))
+        activated = (hidden * spread).astype(NARROW)
+        slope = spread + hidden * (jnp.exp(hidden * hidden * -0.5) * 0.3989422804014327)
+        g_hidden_f = dot(cotangent, wdown_part[...], NT) * slope
+        g_hidden = g_hidden_f.astype(NARROW)
+        units_buf[shard, :, 0:units] = activated
+        units_buf[shard, :, units : 2 * units] = g_hidden
+        g_up[...] += dot(g_hidden, xhat_low, TN)
+        g_down[...] += dot(activated, cotangent, TN)
+        g_sum[...] += jnp.sum(g_hidden.astype(WIDE).reshape(rows // 8, 8, units), axis=0)
+        pltpu.make_async_copy(xhat_all.at[shard], xhat_out.at[shard], out_sem.at[0, shard]).start()
+        pltpu.make_async_copy(
+            both.at[shard, pl.ds(rows, rows)], cot_out.at[shard], out_sem.at[1, shard]
+        ).start()
+        pltpu.make_async_copy(
+            heads_buf.at[shard], heads_out.at[shard], out_sem.at[2, shard]
+        ).start()
+        pltpu.make_async_copy(
+            units_buf.at[shard], units_out.at[shard], out_sem.at[3, shard]
+        ).start()
+
+    inner = jnp.logical_and(here.has_above, here.has_below)
+
+    def step(at, carry):
+        turn_no = at // 4
+        kind = lax.rem(at, 4)
+        behind = jnp.where(kind >= 2, turn_no - 1, turn_no)
+        from_z = pick2(z, jnp.clip(behind, 0, depth - 1), order)
+        next_z = pick2(z, jnp.clip(turn_no + 1, 0, depth - 1), order)
+        shard_y = jnp.where(kind >= 2, 1 - y, y)
+        shard_core = jnp.where(lax.rem(kind, 2) == 1, 1 - core, core)
+        shard = here.at(from_z, shard_y, shard_core)
+        live = jnp.logical_and(behind >= 0, behind < depth)
+
+        early = jnp.logical_and(inner, turn_no == 2)
+        is_own = jnp.logical_and(kind == 0, turn_no == 0)
+
+        @pl.when(jnp.logical_and(live, jnp.logical_not(jnp.logical_or(is_own, jnp.logical_and(kind == 0, early)))))
+        def _():
+            passing(shard, 1).wait_recv()
+
+        @pl.when(
+            jnp.logical_and(
+                jnp.logical_and(kind == 0, live),
+                jnp.logical_not(jnp.logical_or(turn_no == 0, early)),
+            )
+        )
+        def _():
+            onward(shard, from_z)
+
+        @pl.when(jnp.logical_and(kind == 2, live))
+        def _():
+            passing(shard, 1).start()
+
+        @pl.when(jnp.logical_and(jnp.logical_and(kind == 1, turn_no == 1), inner))
+        def _():
+            following = here.at(next_z, y, core)
+            passing(following, 1).wait_recv()
+            onward(following, next_z)
+
+        @pl.when(live)
+        def _():
+            compute(shard)
+
+        return carry
+
+    lax.fori_loop(0, 4 * depth + 4, step, 0)
+
+    def finish(shard, carry):
+        shard_z = shard // 4
+        mine = lax.rem(shard, 2) == core
+        column = lax.rem(shard // 2, 2) == y
+
+        @pl.when(mine)
+        def _():
+            passing(shard, 1).wait_send()
+
+        @pl.when(jnp.logical_and(mine, column))
+        def _():
+            passing(shard, 0).wait_send()
+
+            @pl.when(jnp.logical_and(shard_z <= z, here.has_above))
+            def _():
+                passing(shard, 2).wait_send()
+
+            @pl.when(jnp.logical_and(shard_z >= z, here.has_below))
+            def _():
+                passing(shard, 3).wait_send()
+
+        pltpu.make_async_copy(xhat_all.at[shard], xhat_out.at[shard], out_sem.at[0, shard]).wait()
+        pltpu.make_async_copy(
+            both.at[shard, pl.ds(rows, rows)], cot_out.at[shard], out_sem.at[1, shard]
+        ).wait()
+        pltpu.make_async_copy(heads_buf.at[shard], heads_out.at[shard], out_sem.at[2, shard]).wait()
+        pltpu.make_async_copy(units_buf.at[shard], units_out.at[shard], out_sem.at[3, shard]).wait()
+        return carry
+
+    lax.fori_loop(0, count, finish, 0)
+    for at, (source, place) in enumerate(shared):
+        remote(source, place, at).wait_send()
+
+    @pl.when(is_owner)
+    def _():
+        for at, (source, place) in enumerate(held):
+            remote(source, place, 5 + at).wait_send()
+
+
+def gather_call(depth, tok, cot, prm, turn, w_qkv, w_out, w_up, w_down):
+    count = depth * 4
+    rows = tok.shape[0]
+    units = w_up.shape[1] // count
+    any_spec = pl.BlockSpec(memory_space=pl.ANY)
+    vmem = pl.BlockSpec(memory_space=pltpu.VMEM)
+    shape = jax.ShapeDtypeStruct
+    return pl.pallas_call(
+        functools.partial(gather_kernel, depth),
+        out_shape=(
+            shape((count, 4 * HD, rows), NARROW),
+            shape((count, rows, 2 * units), NARROW),
+            shape((count, rows, D), NARROW),
+            shape((count, rows, D), NARROW),
+            shape((units, D), WIDE),
+            shape((units, D), WIDE),
+            shape((8, units), WIDE),
+            shape((3 * HD, D), NARROW),
+            shape((D, units), NARROW),
+            shape((units, D), NARROW),
+            shape((HD, D), NARROW),
+            shape((8, D), WIDE),
+        ),
+        in_specs=[any_spec, any_spec, any_spec, vmem] + [any_spec] * 4,
+        out_specs=(any_spec,) * 4 + (vmem,) * 8,
+        scratch_shapes=[
+            pltpu.VMEM((count, 2 * rows, D), NARROW),
+            pltpu.VMEM((count, rows, D), NARROW),
+            pltpu.VMEM((count, 4 * HD, rows), NARROW),
+            pltpu.VMEM((count, rows, 2 * units), NARROW),
+            pltpu.VMEM((2, 3, D // 2, 128), NARROW),
+            pltpu.VMEM((2, 8, D // 2), WIDE),
+            pltpu.SemaphoreType.DMA((2,)),
+            pltpu.SemaphoreType.DMA((7,)),
+            pltpu.SemaphoreType.DMA((7,)),
+            pltpu.SemaphoreType.DMA((7,)),
+            pltpu.SemaphoreType.DMA((4, count)),
+            pltpu.SemaphoreType.DMA((count,)),
+            pltpu.SemaphoreType.DMA((4, count)),
+        ],
+        name="gather_and_units",
+        compiler_params=pltpu.CompilerParams(
+            collective_id=1, has_side_effects=True, vmem_limit_bytes=VMEM_LIMIT
+        ),
+    )(tok, cot, prm, turn, w_qkv, w_out, w_up, w_down)
+
+
+def attention_kernel(
+    lengths_ref,
+    dealing_ref,
+    heads_ref,
+    turn_ref,
+    turned_out,
+    tokens_out,
+    wide,
+    q_rows,
+    k_rows,
+    v_rows,
+    g_rows,
+    scores,
+    probs,
+    g_query,
+    attended,
+    g_key,
+    g_value,
+    turn_wide,
+    found,
+):
+    blocks = heads_ref.shape[0]
+    groups = heads_ref.shape[2] // BLK
+    spans = blocks // 2
+    span = 2 * BLK
+    scale = HD ** (-0.5)
+
+    for group in range(groups):
+        lanes = slice(group * BLK, (group + 1) * BLK)
+
+        def note(block, carry):
+            found[dealing_ref[group, block]] = block
+            return carry
+
+        lax.fori_loop(0, blocks, note, 0)
+        starts = [jnp.int32(0)]
+        for piece in range(lengths_ref.shape[1] - 1):
+            starts.append(starts[-1] + lengths_ref[group, piece])
+
+        def bring(at, carry):
+            for side in range(2):
+                source = found[2 * at + side]
+                part = heads_ref[source, :, lanes]
+                to = slice(side * BLK, (side + 1) * BLK)
+                wide[at, :, to] = part
+                turn_wide[at, :, to] = turn_ref[source, :, lanes]
+                part = part.astype(WIDE)
+                row = pl.ds(pl.multiple_of(side * BLK, BLK), BLK)
+                q_rows[at, row, :] = part[0:HD].T.astype(NARROW)
+                k_rows[at, row, :] = part[HD : 2 * HD].T.astype(NARROW)
+                v_rows[at, row, :] = part[2 * HD : 3 * HD].T.astype(NARROW)
+                g_rows[at, row, :] = part[3 * HD : 4 * HD].T.astype(NARROW)
+            g_key[at] = jnp.zeros((span, HD), WIDE)
+            g_value[at] = jnp.zeros((span, HD), WIDE)
+            return carry
+
+        lax.fori_loop(0, spans, bring, 0)
+
+        def one_span(at, carry):
+            natural = at * span + lax.broadcasted_iota(jnp.int32, (1, span), 1)
+            opening = jnp.zeros((1, span), jnp.int32)
+            first = jnp.int32(0)
+            for start in starts[1:]:
+                opening = jnp.where(natural >= start, start, opening)
+                first = jnp.where(at * span >= start, start, first)
+            low = first // span
+            queries_t = wide[at, 0:HD, :]
+            g_attended_t = wide[at, 3 * HD : 4 * HD, :]
+            key_in = lax.broadcasted_iota(jnp.int32, (span, span), 0)
+
+            def score(keys_at, top):
+                raw = dot(k_rows[keys_at], queries_t) * scale
+                place = key_in + keys_at * span
+                allowed = jnp.logical_and(place <= natural, place >= opening)
+                kept = jnp.where(allowed, raw, MASKED)
+                scores[keys_at] = kept
+                return jnp.maximum(top, jnp.max(kept.reshape(span // 8, 8, span), axis=0))
+
+            top = lax.fori_loop(low, at + 1, score, jnp.full((8, span), MASKED, WIDE))
+            top = jnp.max(top, axis=0, keepdims=True)
+
+            def power(keys_at, total):
+                risen = jnp.exp(scores[keys_at] - top)
+                scores[keys_at] = risen
+                return total + jnp.sum(risen.reshape(span // 8, 8, span), axis=0)
+
+            total = lax.fori_loop(low, at + 1, power, jnp.zeros((8, span), WIDE))
+            share = 1.0 / jnp.sum(total, axis=0, keepdims=True)
+            attended[...] = jnp.zeros_like(attended)
+            g_query[...] = jnp.zeros_like(g_query)
+
+            def weigh(keys_at, carry):
+                part = scores[keys_at] * share
+                scores[keys_at] = part
+                low_part = part.astype(NARROW)
+                probs[keys_at] = low_part
+                attended[...] += dot(wide[keys_at, 2 * HD : 3 * HD, :], low_part)
+                return carry
+
+            lax.fori_loop(low, at + 1, weigh, 0)
+            row_dot = jnp.sum(attended[...] * g_attended_t.astype(WIDE), axis=0, keepdims=True)
+
+            def back(keys_at, carry):
+                g_probs = dot(v_rows[keys_at], g_attended_t)
+                g_scores = (scores[keys_at] * (g_probs - row_dot)).astype(NARROW)
+                g_query[...] += dot(wide[keys_at, HD : 2 * HD, :], g_scores)
+                g_key[keys_at] += dot(g_scores, q_rows[at])
+                g_value[keys_at] += dot(probs[keys_at], g_rows[at])
+                return carry
+
+            lax.fori_loop(low, at + 1, back, 0)
+            wide[at, 0:HD, :] = (unturn(g_query[...] * scale, turn_wide[at])).astype(NARROW)
+            wide[at, 3 * HD : 4 * HD, :] = attended[...].astype(NARROW)
+            return carry
+
+        lax.fori_loop(0, spans, one_span, 0)
+
+        def give(at, carry):
+            keys_t = unturn(g_key[at].T * scale, turn_wide[at]).astype(NARROW)
+            values_t = g_value[at].T.astype(NARROW)
+            whole = jnp.concatenate(
+                [wide[at, 3 * HD : 4 * HD, :], wide[at, 0:HD, :], keys_t, values_t], axis=0
+            )
+            for side in range(2):
+                to = found[2 * at + side]
+                part = whole[:, side * BLK : (side + 1) * BLK]
+                turned_out[to, :, lanes] = part
+                tokens_out[to, lanes, :] = part.astype(WIDE).T.astype(NARROW)
+            return carry
+
+        lax.fori_loop(0, spans, give, 0)
+
+
+def unturn(rows, turn):
+    cosine, sine = turn[0:8], turn[8:16]
+    first, second = rows[0:8], rows[8:16]
+    return jnp.concatenate(
+        [first * cosine + second * sine, second * cosine - first * sine, rows[16:]], axis=0
+    )
+
+
+def attention_call(lengths, dealing, heads, turn):
+    blocks, _, rows = heads.shape
+    spans, span = blocks // 2, 2 * BLK
+    vmem = pl.BlockSpec(memory_space=pltpu.VMEM)
+    smem = pl.BlockSpec(memory_space=pltpu.SMEM)
+    shape = jax.ShapeDtypeStruct
+    return pl.pallas_call(
+        attention_kernel,
+        out_shape=(
+            shape((blocks, 4 * HD, rows), NARROW),
+            shape((blocks, rows, 4 * HD), NARROW),
+        ),
+        in_specs=[smem, smem, vmem, vmem],
+        out_specs=(vmem, vmem),
+        scratch_shapes=[
+            pltpu.VMEM((spans, 4 * HD, span), NARROW),
+            pltpu.VMEM((spans, span, HD), NARROW),
+            pltpu.VMEM((spans, span, HD), NARROW),
+            pltpu.VMEM((spans, span, HD), NARROW),
+            pltpu.VMEM((spans, span, HD), NARROW),
+            pltpu.VMEM((spans, span, span), WIDE),
+            pltpu.VMEM((spans, span, span), NARROW),
+            pltpu.VMEM((HD, span), WIDE),
+            pltpu.VMEM((HD, span), WIDE),
+            pltpu.VMEM((spans, span, HD), WIDE),
+            pltpu.VMEM((spans, span, HD), WIDE),
+            pltpu.VMEM((spans, 16, span), WIDE),
+            pltpu.SMEM((blocks,), jnp.int32),
+        ],
+        name="head_attention",
+        compiler_params=pltpu.CompilerParams(vmem_limit_bytes=VMEM_LIMIT),
+    )(lengths, dealing, heads, turn)
+
+
+def far_first(depth):
+    return [list(reversed(row)) for row in near_first(depth)]
+
+
+def reduce_kernel(
+    depth,
+    tokens_in,
+    units_in,
+    tok_ref,
+    cot_ref,
+    prm_all,
+    wqkv_t,
+    wup_all,
+    wdown_part,
+    wout_part,
+    out_ref,
+    grad_ref,
+    w_heads_out,
+    w_heads_back,
+    give_buf,
+    sum_buf,
+    beside_buf,
+    under_buf,
+    over_buf,
+    send_sem,
+    recv_twin,
+    recv_beside,
+    recv_z,
+):
+    here = Place(depth)
+    x, y, z, core = here.x, here.y, here.z, here.core
+    rows = tok_ref.shape[0]
+    units = wup_all.shape[1]
+    order = far_first(depth)
+    here.greet()
+    w_heads_out[0:HD, :] = wout_part[...]
+    w_heads_out[HD:, :] = jnp.zeros((3 * HD, D), NARROW)
+    w_heads_back[0:HD, :] = jnp.zeros((HD, D), NARROW)
+    w_heads_back[HD:, :] = wqkv_t[...]
+
+    def partial(shard):
+        heads = tokens_in[shard]
+        activated = units_in[shard, :, 0:units]
+        g_hidden = units_in[shard, :, units : 2 * units]
+        part_out = dot(heads, w_heads_out[...]) + dot(activated, wdown_part[...])
+        part_back = dot(heads, w_heads_back[...]) * prm_all[0:1, :] + dot(
+            g_hidden, wup_all[...], NT
+        ) * prm_all[2:3, :]
+        return part_out, part_back
+
+    def to_twin(slot):
+        return pltpu.make_async_remote_copy(
+            give_buf.at[slot],
+            sum_buf.at[slot],
+            send_sem.at[0, slot],
+            recv_twin.at[slot],
+            device_id=here.twin,
+            device_id_type=MESH,
+        )
+
+    def to_beside(to_z):
+        return pltpu.make_async_remote_copy(
+            sum_buf.at[to_z],
+            beside_buf.at[to_z],
+            send_sem.at[1, to_z],
+            recv_beside.at[to_z],
+            device_id=here.beside,
+            device_id_type=MESH,
+        )
+
+    def to_above(to_z):
+        return pltpu.make_async_remote_copy(
+            sum_buf.at[depth + to_z],
+            under_buf.at[to_z],
+            send_sem.at[2, to_z],
+            recv_z.at[0, to_z],
+            device_id=here.above,
+            device_id_type=MESH,
+        )
+
+    def to_below(to_z):
+        return pltpu.make_async_remote_copy(
+            sum_buf.at[depth + to_z],
+            over_buf.at[to_z],
+            send_sem.at[2, to_z],
+            recv_z.at[1, to_z],
+            device_id=here.below,
+            device_id_type=MESH,
+        )
+
+    def produce(at, carry):
+        to_z = pick2(z, at // 4, order)
+        kind = lax.rem(at, 4)
+        home = lax.rem(kind, 2)
+        to_y = jnp.where(home == 1, y, 1 - y)
+        slot = home * depth + to_z
+        to_core = jnp.where(kind < 2, 1 - core, core)
+        part_out, part_back = partial(here.at(to_z, to_y, to_core))
+
+        @pl.when(kind < 2)
+        def _():
+            give_buf[slot, 0:rows, :] = part_out.astype(NARROW)
+            give_buf[slot, rows : 2 * rows, :] = part_back.astype(NARROW)
+            to_twin(slot).start()
+
+        @pl.when(kind >= 2)
+        def _():
+            to_twin(slot).wait_recv()
+            sum_buf[slot, 0:rows, :] = (
+                part_out + sum_buf[slot, 0:rows, :].astype(WIDE)
+            ).astype(NARROW)
+            sum_buf[slot, rows : 2 * rows, :] = (
+                part_back + sum_buf[slot, rows : 2 * rows, :].astype(WIDE)
+            ).astype(NARROW)
+
+        @pl.when(kind == 2)
+        def _():
+            to_beside(to_z).start()
+
+        return carry
+
+    lax.fori_loop(0, 4 * depth, produce, 0)
+
+    def chain(at, carry):
+        to_z = pick2(z, at, order)
+        slot = depth + to_z
+        to_beside(to_z).wait_recv()
+
+        def add(incoming):
+            for part in range(4):
+                span = slice(part * rows // 2, (part + 1) * rows // 2)
+                total = sum_buf[slot, span, :].astype(WIDE) + beside_buf[to_z, span, :].astype(WIDE)
+                if incoming is not None:
+                    total = total + incoming[to_z, span, :].astype(WIDE)
+                sum_buf[slot, span, :] = total.astype(NARROW)
+
+        @pl.when(to_z > z)
+        def _():
+            @pl.when(here.has_below)
+            def _():
+                to_above(to_z).wait_recv()
+                add(under_buf)
+
+            @pl.when(jnp.logical_not(here.has_below))
+            def _():
+                add(None)
+
+            to_above(to_z).start()
+
+        @pl.when(to_z < z)
+        def _():
+            @pl.when(here.has_above)
+            def _():
+                to_below(to_z).wait_recv()
+                add(over_buf)
+
+            @pl.when(jnp.logical_not(here.has_above))
+            def _():
+                add(None)
+
+            to_below(to_z).start()
+
+        return carry
+
+    lax.fori_loop(0, depth, chain, 0)
+
+    @pl.when(here.has_below)
+    def _():
+        to_above(z).wait_recv()
+
+    @pl.when(jnp.logical_not(here.has_below))
+    def _():
+        under_buf[z] = jnp.zeros((2 * rows, D), NARROW)
+
+    @pl.when(here.has_above)
+    def _():
+        to_below(z).wait_recv()
+
+    @pl.when(jnp.logical_not(here.has_above))
+    def _():
+        over_buf[z] = jnp.zeros((2 * rows, D), NARROW)
+
+    def total(span):
+        return (
+            sum_buf[depth + z, span, :].astype(WIDE)
+            + beside_buf[z, span, :].astype(WIDE)
+            + under_buf[z, span, :].astype(WIDE)
+            + over_buf[z, span, :].astype(WIDE)
+        )
+
+    tokens = tok_ref[...].astype(WIDE)
+    out_ref[...] = (tokens + total(slice(0, rows))).astype(NARROW)
+    average = jnp.mean(tokens, axis=-1, keepdims=True)
+    centred = tokens - average
+    variance = jnp.mean(centred * centred, axis=-1, keepdims=True)
+    rise = lax.rsqrt(variance + EPSILON)
+    xhat = centred * rise
+    g_xhat = total(slice(rows, 2 * rows))
+    along = jnp.mean(g_xhat * xhat, axis=-1, keepdims=True)
+    level = jnp.mean(g_xhat, axis=-1, keepdims=True)
+    grad_ref[...] = cot_ref[...].astype(WIDE) + rise * (g_xhat - level - xhat * along)
+
+    def finish(to_z, carry):
+        to_twin(to_z).wait_send()
+        to_twin(depth + to_z).wait_send()
+        to_beside(to_z).wait_send()
+
+        @pl.when(to_z > z)
+        def _():
+            to_above(to_z).wait_send()
+
+        @pl.when(to_z < z)
+        def _():
+            to_below(to_z).wait_send()
+
+        return carry
+
+    lax.fori_loop(0, depth, finish, 0)
+
+
+def reduce_call(depth, tokens_in, units_in, tok, cot, prm_all, wqkv_t, wup_all, wdown_part, wout_part):
+    rows = tok.shape[0]
+    vmem = pl.BlockSpec(memory_space=pltpu.VMEM)
+    shape = jax.ShapeDtypeStruct
+    message = (2 * rows, D)
+    return pl.pallas_call(
+        functools.partial(reduce_kernel, depth),
+        out_shape=(shape((rows, D), NARROW), shape((rows, D), WIDE)),
+        in_specs=[vmem] * 9,
+        out_specs=(vmem, vmem),
+        scratch_shapes=[
+            pltpu.VMEM((4 * HD, D), NARROW),
+            pltpu.VMEM((4 * HD, D), NARROW),
+            pltpu.VMEM((2 * depth,) + message, NARROW),
+            pltpu.VMEM((2 * depth,) + message, NARROW),
+            pltpu.VMEM((depth,) + message, NARROW),
+            pltpu.VMEM((depth,) + message, NARROW),
+            pltpu.VMEM((depth,) + message, NARROW),
+            pltpu.SemaphoreType.DMA((3, 2 * depth)),
+            pltpu.SemaphoreType.DMA((2 * depth,)),
+            pltpu.SemaphoreType.DMA((depth,)),
+            pltpu.SemaphoreType.DMA((2, depth)),
+        ],
+        name="reduce_rows",
+        compiler_params=pltpu.CompilerParams(
+            collective_id=2, has_side_effects=True, vmem_limit_bytes=VMEM_LIMIT
+        ),
+    )(tokens_in, units_in, tok, cot, prm_all, wqkv_t, wup_all, wdown_part, wout_part)
+
+
+def fast_shards(depth, *arguments):
+    (tokens, cotangent, lengths, dealing, gain_one, bias_one, gain_two, bias_two) = arguments[:8]
+    w_qkv, w_out, w_up, w_down = arguments[8:]
+    groups, local_rows, _ = tokens.shape
+    rows = groups * local_rows
+    count = depth * 4
+    tok = tokens.reshape(rows, D)
+    cot = cotangent.reshape(rows, D)
+    prm = jnp.stack([gain_one, bias_one, gain_two, bias_two] * 2).astype(WIDE)
+
+    openings = jnp.cumsum(lengths, axis=1) - lengths
+    natural = (dealing.T[:, :, None] * BLK + jnp.arange(BLK, dtype=jnp.int32)[None, None, :]).reshape(
+        count, rows
+    )
+    start_rows = jnp.repeat(openings.T, BLK, axis=1)[:, None, :]
+    opening = jnp.max(jnp.where(start_rows <= natural[None], start_rows, 0), axis=0)
+    place = (natural - opening).astype(WIDE)
+    frequency = 10000.0 ** (-2.0 * jnp.arange(ROT // 2, dtype=WIDE) / ROT)
+    angles = place[:, None, :] * frequency[None, :, None]
+    turn = jnp.concatenate([jnp.cos(angles), jnp.sin(angles)], axis=1)
+
+    (heads, units, xhat, cot_all, g_up, g_down, g_sum, wqkv_t, wup_all, wdown_part, wout_part, prm_all) = (
+        gather_call(depth, tok, cot, prm, turn, w_qkv, w_out, w_up, w_down)
+    )
+    turned, by_token = attention_call(lengths, dealing, heads, turn)
+    out, grad_tokens = reduce_call(
+        depth, by_token, units, tok, cot, prm_all, wqkv_t, wup_all, wdown_part, wout_part
+    )
+
+    g_out = jnp.einsum("ser,srd->ed", turned[:, :HD], cot_all, preferred_element_type=WIDE)
+    g_one = jnp.einsum("ser,srd->ed", turned[:, HD:], xhat, preferred_element_type=WIDE)
+    sum_one = jnp.sum(turned[:, HD:].astype(WIDE), axis=(0, 2))[:, None]
+    sum_two = jnp.sum(g_sum, axis=0)[:, None]
+    gain_a, bias_a, gain_b, bias_b = prm_all[0:1], prm_all[1:2], prm_all[2:3], prm_all[3:4]
+    wide_qkv = wqkv_t.astype(WIDE)
+    wide_up = wup_all.astype(WIDE).T
+    vectors = jnp.stack(
+        [
+            jnp.sum(wide_qkv * g_one, axis=0),
+            jnp.sum(wide_qkv * sum_one, axis=0),
+            jnp.sum(wide_up * g_up, axis=0),
+            jnp.sum(wide_up * sum_two, axis=0),
+        ]
+    )
+    columns = jnp.concatenate(
+        [g_one * gain_a + bias_a * sum_one, g_up * gain_b + bias_b * sum_two, vectors], axis=0
+    )
+    width = columns.shape[0]
+    piece = D // (2 * count)
+    split = columns.reshape(width, count, 2, piece).transpose(2, 1, 0, 3)
+    split = lax.psum_scatter(split, "wsh", scatter_dimension=0, tiled=False)
+    split = lax.all_to_all(split, "ctx", split_axis=0, concat_axis=0, tiled=True)
+    units_count = g_up.shape[0]
+    qkv_part = split[:, : 3 * HD].reshape(count, 3, HD, piece).transpose(3, 1, 0, 2).reshape(piece, 3 * D)
+    up_part = split[:, 3 * HD : 3 * HD + units_count].transpose(2, 0, 1).reshape(piece, count * units_count)
+    vector_part = jnp.sum(split[:, 3 * HD + units_count :], axis=0)
+    out_part = lax.psum_scatter(g_out, "wsh", scatter_dimension=0, tiled=True)
+    down_part = lax.psum_scatter(g_down, "wsh", scatter_dimension=0, tiled=True)
+    return (
+        out.reshape(tokens.shape),
+        grad_tokens.reshape(tokens.shape),
+        vector_part[0],
+        vector_part[1],
+        vector_part[2],
+        vector_part[3],
+        qkv_part,
+        out_part,
+        up_part,
+        down_part,
+    )
+
+
 def solution(mesh):
     placed = (
         P("wsh", "ctx", None),
@@ -393,8 +1303,11 @@
         P("wsh", None),
         P("wsh", None),
     )
+    ctx_size = mesh.shape["ctx"]
+    by_heads = ctx_size == H and mesh.shape["wsh"] == 2
+    body = functools.partial(fast_shards, ctx_size // 4) if by_heads else shards
     return jax.shard_map(
-        shards,
+        body,
         mesh=mesh,
         in_specs=placed,
         out_specs=(

time: 1950 us -> 374 us (0.19)
  waiting for transfers between devices: 1480 us -> 27.9 us
  Pallas kernels: 0 us -> 290 us
  local copies, waits for them, and re-layouts: 185 us -> 17.8 us
  matrix products: 139 us -> 11.6 us
  blocking collectives: 58.1 us -> 0 us
  other arithmetic: 61.1 us -> 6.63 us
    reduce_scatter x6 -> x3, waiting for transfers between devices: 1210 us -> 27.2 us  [the longest x1 27.1 us: fast_shards(): split = lax.psum_scatter(split, 'wsh', scatter_dimension=0, tiled=False)]
    pallas_call x0 -> x3, Pallas kernels: none -> 290 us  [the longest x1 122 us: gather_call(): pl.pallas_call(functools.partial(gather_kernel, depth), out_shape=(shape(...]
    all_gather x8 -> x0, waiting for transfers between devices: 267 us -> none  [the longest x2 93.2 us: attend(): lax.all_gather(values_here, 'ctx', axis=0, tiled=True)]
    dot_general x40 -> x2, matrix products: 139 us -> 11.6 us  [the longest x1 5.85 us: fast_shards(): jnp.einsum('ser,srd->ed', turned[:, :HD], cot_all, preferred_element_type...]
    dynamic_update_slice x8 -> x0, local copies, waits for them, and re-layouts: 69.3 us -> none  [attention_back(): lax.scan(key_block, jnp.zeros((local_rows, H, HD), WIDE), stacked_blocks)]
    dynamic_slice x24 -> x0, local copies, waits for them, and re-layouts: 41.5 us -> none  [fold_blocks(): state_out, _ = lax.scan(inner_step, state_in, (stacked, offsets))]
    unnamed x1 -> x0, blocking collectives: 39.9 us -> none
    unnamed x112 -> x17, local copies, waits for them, and re-layouts: 35.7 us -> 2.06 us
  transfers between devices with their start and end apart: 14 -> 4, of which waited for: 12 -> 1; matrix products, arithmetic and copies ran while one was open for 19% -> 3% of each run, Pallas kernels for 0% -> 30%
where the time goes in v1:
time: 374 us
  Pallas kernels  290 us (78%)
  waiting for transfers between devices  27.9 us (7%)
  local copies, waits for them, and re-layouts  17.8 us (5%)
  between operations  14 us (4%)
  matrix products  11.6 us (3%)
  other arithmetic  6.63 us (2%)
  starting transfers between devices  5.73 us (2%)
    pallas_call x1, Pallas kernels, gather_call(): pl.pallas_call(functools.partial(gather_kernel, depth), out_shape=(shape(...  122 us
    pallas_call x1, Pallas kernels, reduce_call(): pl.pallas_call(functools.partial(reduce_kernel, depth), out_shape=(shape(...  114 us
    pallas_call x1, Pallas kernels, attention_call(): pl.pallas_call(attention_kernel, out_shape=(shape((blocks, 4 * HD, rows),...  53.7 us
    reduce_scatter x1, waiting for transfers between devices, fast_shards(): split = lax.psum_scatter(split, 'wsh', scatter_dimension=0, tiled=False)  27.1 us
  transfers between devices with their start and end apart: 4, of which 1 were waited for; matrix products, arithmetic and copies ran while one was open for 3% of the time, Pallas kernels for 30%

profile of v1, /device:TPU:0, one launch (start us, length us, event | category | flops | bytes accessed | tf_op | source)
XLA Modules:
  0.0 373.7 jit_solution(18146903966001969496)
XLA Ops:
  7.2 0.7 stack.10
  7.9 0.7 stack.11
  8.6 0.7 stack.12
  9.3 0.7 stack.26
  11.4 0.8 reduce_window_sum.11
  12.2 0.7 subtract_bitcast_fusion
  13.8 0.7 pad_maximum_fusion.turn_ref
  14.5 122.5 %gather_and_units.1 = (bf16[16,256,256]{2,1,0:T(8,128)(2,1)}, bf16[16,256,512]{2,1,0:T(8,128)(2,1)}, bf16[16,256,1024]{2,1,0:T(8,128)(2,1)}, bf16[16,256,1024]{2...) custom-call(bf16[256,1024]{1,0:T(8,128)(2,1)} %bitcast.54, ...), custom_call_target="tpu_custom_call" | custom-call | tf_op jit(solution)/shard_map/gather_and_units/pallas_call | solution.py:754
  137.0 53.7 %head_attention.1 = (bf16[16,256,256]{2,1,0:T(8,128)(2,1)}, bf16[16,256,256]{2,1,0:T(8,128)(2,1)}) custom-call(s32[2,4]{1,0:T(2,128)} %lengths_ref.1, s32[2,16]{1,0:T(2,128)} %dealing_ref.1, bf16[16,256,256]{2,1,0:T(8,128)(2,1)} %get-tuple-element.26.heads_ref, f32[16,16,256]{2,1,0:T(8,128)} %pad_maximum_fusion.turn_ref), custom_call_target="tpu_custom_call" | custom-call | tf_op jit(solution)/shard_map/head_attention/pallas_call | solution.py:941
  190.7 1.7 convert_reduce_fusion
  192.4 5.8 %fusion.8 = (f32[1024]{0:T(1024)S(1)}, f32[1024]{0:T(1024)S(1)}, f32[192,1024]{1,0:T(8,128)S(1)}) fusion(bf16[192,1024]{1,0:T(8,128)(2,1)S(1)} %copy-done.3, f32[192]{0:T(256)S(1)} %convert_reduce_fusion, f32[1024]{0:T(1024)S(1)} %bitcast.67, f32[1024]{0:T(1024)S(1)} %bitcast.68, bf16[16,256,1024]{2,1,0:T(8,128)(2,1)} %get-tuple-element.37, ...), kind=kOutput, calls=%fused_computation.13 | convolution fusion | flops 1612183552 | bytes 11158272 | tf_op jit(solution)/shard_map/ser,srd->ed/dot_general | solution.py:1249
  198.6 1.6 copy.83
  201.8 1.1 copy.89
  202.9 1.1 copy.90
  204.0 4.2 %concatenate.26 = f32[452,16,2,32]{0,3,1,2:T(8,128)} concatenate(f32[192,16,2,32]{0,3,1,2:T(8,128)S(1)} %copy.85, f32[256,16,2,32]{0,3,1,2:T(8,128)S(1)} %copy.86, f32[1,16,2,32]{0,3,1,2:T(8,128)S(1)} %copy.87, f32[1,16,2,32]{0,3,1,2:T(8,128)S(1)} %copy.88, f32[1,16,2,32]{0,3,1,2:T(8,128)} %copy.89, f32[1,16,2,32]{0,3,1,2:T(8,128)} %copy.90), dimensions={0} | concatenate | bytes 3702784 | tf_op jit(solution)/shard_map/concatenate | solution.py:1263
  208.3 5.8 %convolution_bitcast_fusion = f32[64,1024]{1,0:T(8,128)} fusion(bf16[16,256,1024]{2,1,0:T(8,128)(2,1)} %get-tuple-element.40, bf16[16,256,256]{2,1,0:T(8,128)(2,1)} %get-tuple-element.36), kind=kOutput, calls=%fused_computation.4 | convolution fusion | flops 536870912 | bytes 9175040 | tf_op jit(solution)/shard_map/ser,srd->ed/dot_general | solution.py:1248
  214.2 27.1 %reduce-scatter.4.cloned.1.call-done = f32[1,16,452,32]{2,3,1,0:T(8,128)} async-done(((f32[2,16,452,32]{2,3,1,0:T(8,128)}), f32[1,16,452,32]{2,3,1,0:T(8,128)}) %reduce-scatter.4.cloned.1.call-update) | async-done | bytes 925712 | tf_op jit(solution)/shard_map/reduce_scatter | solution.py:1269
  241.3 5.6 %all-to-all-start = ((f32[16,452,32]{1,2,0:T(8,128)}), f32[16,452,32]{1,2,0:T(8,128)S(1)}, u32[]{:S(2)}, u32[]{:S(2)}) async-start(f32[16,452,32]{1,2,0:T(8,128)} %bitcast.58), calls=%async_computation.1 | async-start | bytes 2097152 | tf_op jit(solution)/shard_map/all_to_all | solution.py:1270
  247.7 113.9 %reduce_rows.1 = (bf16[256,1024]{1,0:T(8,128)(2,1)}, f32[256,1024]{1,0:T(8,128)}) custom-call(bf16[16,256,256]{2,1,0:T(8,128)(2,1)} %get-tuple-element.27.tokens_in, bf16[16,256,512]{2,1,0:T(8,128)(2,1)} %get-tuple-element.28.units_in, bf16[256,1024]{1,0:T(8,128)(2,1)} %bitcast.55, bf16[256,1024]{1,0:T(8,128)(2,1)} %bitcast.57, ...), custom_call_target="tpu_custom_call" | custom-call | tf_op jit(solution)/shard_map/reduce_rows/pallas_call | solution.py:1194
  362.4 1.0 reshape.111
  363.6 0.8 copy.93
  364.6 0.7 slice_reduce_fusion.1
  365.4 0.8 copy.103
  366.2 1.0 copy.104
  (52 shorter events, 6.3 us)
Async XLA Ops:
  7.2 234.1 %reduce-scatter.4.cloned.1.call-start = ((), (), s32[]{:S(2)}) async-start(), calls=%async_computation.4 | async-start | bytes 3145728 | tf_op jit(solution)/shard_map/reduce_scatter | solution.py:1269
  137.0 55.4 %copy-start.4 = (f32[8,1024]{1,0:T(8,128)S(1)}, f32[8,1024]{1,0:T(8,128)}, u32[]{:S(2)}) copy-start(f32[8,1024]{1,0:T(8,128)} %get-tuple-element.29.prm_all) | copy-start | bytes 98308
  137.0 55.4 %copy-start.3 = (bf16[192,1024]{1,0:T(8,128)(2,1)S(1)}, bf16[192,1024]{1,0:T(8,128)(2,1)}, u32[]{:S(2)}) copy-start(bf16[192,1024]{1,0:T(8,128)(2,1)} %get-tuple-element.30.wqkv_t) | copy-start | bytes 1179652
  198.2 2.0 copy-start.5
  198.2 2.1 copy-start
  208.2 157.1 %reduce-scatter.6.cloned.1.call-start = ((), (), s32[]{:S(2)}) async-start(), calls=%async_computation.5 | async-start | bytes 393216 | tf_op jit(solution)/shard_map/reduce_scatter | solution.py:1275
  241.3 120.3 %all-to-all-start = ((f32[16,452,32]{1,2,0:T(8,128)}), f32[16,452,32]{1,2,0:T(8,128)S(1)}, u32[]{:S(2)}, u32[]{:S(2)}) async-start(f32[16,452,32]{1,2,0:T(8,128)} %bitcast.58), calls=%async_computation.1 | async-start | bytes 2097152 | tf_op jit(solution)/shard_map/all_to_all | solution.py:1270
  246.9 118.4 %reduce-scatter.8.cloned.1.call-start = ((), (), s32[]{:S(2)}) async-start(), calls=%async_computation.6 | async-start | bytes 1572864 | tf_op jit(solution)/shard_map/reduce_scatter | solution.py:1276
  361.6 3.7 %copy-start.2 = (bf16[256,1024]{1,0:T(8,128)(2,1)S(1)}, bf16[256,1024]{1,0:T(8,128)(2,1)}, u32[]{:S(2)}) copy-start(bf16[256,1024]{1,0:T(8,128)(2,1)} %get-tuple-element.34) | copy-start | bytes 1572868
  362.4 3.7 copy-start.1
Sparse Core Ops, SparseCore 0:
  208.4 32.9 reduce-scatter.3
  244.2 11.6 reduce-scatter.5
  258.7 20.3 reduce-scatter.7

commit v2 on v1

--- a/solution.py
+++ b/solution.py
@@ -450,6 +450,20 @@
         pl.semaphore_wait(
             barrier, 3 + self.has_above.astype(jnp.int32) + self.has_below.astype(jnp.int32)
         )
+
+
+    def greet_all(self):
+        barrier = pltpu.get_barrier_semaphore()
+        count = 4 * self.depth
+        pl.semaphore_signal(barrier, inc=1, device_id=self.across, device_id_type=MESH)
+
+        def hail(offset, carry):
+            device = (lax.rem(self.c + offset, count), self.x)
+            pl.semaphore_signal(barrier, inc=1, device_id=device, device_id_type=MESH)
+            return carry
+
+        lax.fori_loop(1, count, hail, 0)
+        pl.semaphore_wait(barrier, count)
 
 
 def gather_kernel(
@@ -973,6 +987,7 @@
 def reduce_kernel(
     depth,
     tokens_in,
+    turned_in,
     units_in,
     tok_ref,
     cot_ref,
@@ -981,32 +996,125 @@
     wup_all,
     wdown_part,
     wout_part,
+    g_up,
+    g_down,
+    g_sum,
+    xhat_in,
+    cot_in,
     out_ref,
     grad_ref,
+    qkv_ref,
+    wout_ref,
+    up_ref,
+    down_ref,
+    vec_ref,
     w_heads_out,
     w_heads_back,
     give_buf,
     sum_buf,
     beside_buf,
-    under_buf,
-    over_buf,
+    line_buf,
+    stream,
+    g_heads,
+    g_wout,
+    sum_heads,
+    vectors,
+    grads,
+    grads_in,
+    mail,
+    inbox,
+    wout_in,
+    down_in,
     send_sem,
     recv_twin,
     recv_beside,
     recv_z,
+    stream_sem,
+    across_send,
+    across_recv,
+    mail_send,
+    mail_recv,
 ):
     here = Place(depth)
-    x, y, z, core = here.x, here.y, here.z, here.core
+    c, x, y, z, core = here.c, here.x, here.y, here.z, here.core
     rows = tok_ref.shape[0]
     units = wup_all.shape[1]
+    count = 4 * depth
+    piece = D // (2 * count)
     order = far_first(depth)
-    here.greet()
+
+    def shard_of(at):
+        kind = lax.rem(at, 4)
+        to_y = jnp.where(lax.rem(kind, 2) == 1, y, 1 - y)
+        to_core = jnp.where(kind < 2, 1 - core, core)
+        return here.at(pick2(z, at // 4, order), to_y, to_core)
+
+    def load(at):
+        shard, slot = shard_of(at), lax.rem(at, 2)
+        return (
+            pltpu.make_async_copy(xhat_in.at[shard], stream.at[0, slot], stream_sem.at[0, slot]),
+            pltpu.make_async_copy(cot_in.at[shard], stream.at[1, slot], stream_sem.at[1, slot]),
+        )
+
+    for copy in load(0):
+        copy.start()
+    here.greet_all()
+
+    def crossing(source, place, at):
+        return pltpu.make_async_remote_copy(
+            source,
+            place,
+            across_send.at[at],
+            across_recv.at[at],
+            device_id=here.across,
+            device_id_type=MESH,
+        )
+
+    half_down = g_down.shape[0] // 2
+    half_wout = HD // 2
+    send_down = crossing(g_down.at[pl.ds((1 - x) * half_down, half_down)], down_in, 0)
+    send_wout = crossing(g_wout.at[pl.ds((1 - x) * half_wout, half_wout)], wout_in, 1)
+    send_grads = [crossing(grads.at[part, 1 - x], grads_in.at[part], 2 + part) for part in range(2)]
+    send_down.start()
+
     w_heads_out[0:HD, :] = wout_part[...]
     w_heads_out[HD:, :] = jnp.zeros((3 * HD, D), NARROW)
     w_heads_back[0:HD, :] = jnp.zeros((HD, D), NARROW)
     w_heads_back[HD:, :] = wqkv_t[...]
-
-    def partial(shard):
+    g_heads[...] = jnp.zeros_like(g_heads)
+    g_wout[...] = jnp.zeros_like(g_wout)
+    sum_heads[...] = jnp.zeros_like(sum_heads)
+    sum_units = jnp.sum(g_sum[...], axis=0, keepdims=True)
+
+    def settle(chunk, part, raw, weights, sums, column):
+        scaled = raw * column[:, 2 - 2 * part : 3 - 2 * part] + sums * column[:, 3 - 2 * part : 4 - 2 * part]
+        gain_sum = jnp.sum(weights * raw, axis=1, keepdims=True)
+        bias_sum = jnp.sum(weights * sums, axis=1, keepdims=True)
+        row = pl.ds(pl.multiple_of(chunk * 128, 128), 128)
+        if part == 0:
+            vectors[row, 0:1] = gain_sum
+            vectors[row, 1:2] = bias_sum
+        else:
+            lane = lax.broadcasted_iota(jnp.int32, scaled.shape, 1)
+            scaled = jnp.where(lane == 0, gain_sum, scaled)
+            scaled = jnp.where(lane == 1, bias_sum, scaled)
+            scaled = jnp.where(lane == 2, vectors[row, 0:1], scaled)
+            scaled = jnp.where(lane == 3, vectors[row, 1:2], scaled)
+        per = 128 // piece
+        for at in range(per):
+            grads[part, at % 2, chunk * (per // 2) + at // 2] = scaled[at * piece : (at + 1) * piece]
+
+    def settle_up(chunk, carry):
+        lanes = pl.ds(pl.multiple_of(chunk * 128, 128), 128)
+        weights = wup_all[lanes, :].astype(WIDE)
+        settle(chunk, 0, g_up[:, lanes].T, weights, sum_units, prm_all[:, lanes].T)
+        return carry
+
+    lax.fori_loop(0, D // 128, settle_up, 0)
+    send_grads[0].start()
+
+    def partial(at):
+        shard, slot = shard_of(at), lax.rem(at, 2)
         heads = tokens_in[shard]
         activated = units_in[shard, :, 0:units]
         g_hidden = units_in[shard, :, units : 2 * units]
@@ -1014,6 +1122,17 @@
         part_back = dot(heads, w_heads_back[...]) * prm_all[0:1, :] + dot(
             g_hidden, wup_all[...], NT
         ) * prm_all[2:3, :]
+
+        @pl.when(at + 1 < count)
+        def _():
+            for copy in load(at + 1):
+                copy.start()
+
+        for copy in load(at):
+            copy.wait()
+        g_wout[...] += dot(turned_in[shard, 0:HD, :], stream[1, slot])
+        g_heads[HD:, :] += dot(turned_in[shard, HD:, :], stream[0, slot])
+        sum_heads[...] += jnp.sum(heads.astype(WIDE).reshape(rows // 8, 8, 4 * HD), axis=0)
         return part_out, part_back
 
     def to_twin(slot):
@@ -1039,20 +1158,34 @@
     def to_above(to_z):
         return pltpu.make_async_remote_copy(
             sum_buf.at[depth + to_z],
-            under_buf.at[to_z],
+            line_buf.at[to_z],
             send_sem.at[2, to_z],
-            recv_z.at[0, to_z],
+            recv_z.at[to_z],
             device_id=here.above,
             device_id_type=MESH,
         )
+
+    def over_slot(to_z, at_z):
+        return jnp.where(to_z == at_z, depth, to_z)
 
     def to_below(to_z):
         return pltpu.make_async_remote_copy(
             sum_buf.at[depth + to_z],
-            over_buf.at[to_z],
+            line_buf.at[over_slot(to_z, z - 1)],
             send_sem.at[2, to_z],
-            recv_z.at[1, to_z],
+            recv_z.at[over_slot(to_z, z - 1)],
             device_id=here.below,
+            device_id_type=MESH,
+        )
+
+    def from_above(to_z):
+        slot = over_slot(to_z, z)
+        return pltpu.make_async_remote_copy(
+            sum_buf.at[depth + to_z],
+            line_buf.at[slot],
+            send_sem.at[2, to_z],
+            recv_z.at[slot],
+            device_id=here.above,
             device_id_type=MESH,
         )
 
@@ -1060,10 +1193,8 @@
         to_z = pick2(z, at // 4, order)
         kind = lax.rem(at, 4)
         home = lax.rem(kind, 2)
-        to_y = jnp.where(home == 1, y, 1 - y)
         slot = home * depth + to_z
-        to_core = jnp.where(kind < 2, 1 - core, core)
-        part_out, part_back = partial(here.at(to_z, to_y, to_core))
+        part_out, part_back = partial(at)
 
         @pl.when(kind < 2)
         def _():
@@ -1088,6 +1219,55 @@
         return carry
 
     lax.fori_loop(0, 4 * depth, produce, 0)
+    send_wout.start()
+    sum_row = jnp.sum(sum_heads[...], axis=0, keepdims=True)
+
+    def settle_qkv(chunk, carry):
+        lanes = pl.ds(pl.multiple_of(chunk * 128, 128), 128)
+        weights = w_heads_back[:, lanes].astype(WIDE).T
+        settle(chunk, 1, g_heads[:, lanes].T, weights, sum_row, prm_all[:, lanes].T)
+        return carry
+
+    lax.fori_loop(0, D // 128, settle_qkv, 0)
+    send_grads[1].start()
+
+    def post(part, to_c):
+        return pltpu.make_async_remote_copy(
+            mail.at[part, to_c],
+            inbox.at[part, c],
+            mail_send.at[part, to_c],
+            mail_recv.at[part, c],
+            device_id=(to_c, x),
+            device_id_type=MESH,
+        )
+
+    def collect(part, from_c):
+        return pltpu.make_async_remote_copy(
+            mail.at[part, from_c],
+            inbox.at[part, from_c],
+            mail_send.at[part, from_c],
+            mail_recv.at[part, from_c],
+            device_id=(from_c, x),
+            device_id_type=MESH,
+        )
+
+    def mail_out(part):
+        send_grads[part].wait_recv()
+
+        def fold(to_c, carry):
+            mail[part, to_c] = (grads[part, x, to_c] + grads_in[part, to_c]).astype(NARROW)
+            return carry
+
+        lax.fori_loop(0, count, fold, 0)
+
+        def start(offset, carry):
+            post(part, lax.rem(c + offset, count)).start()
+            return carry
+
+        lax.fori_loop(1, count, start, 0)
+        inbox[part, c] = mail[part, c]
+
+    mail_out(0)
 
     def chain(at, carry):
         to_z = pick2(z, at, order)
@@ -1098,8 +1278,8 @@
             for part in range(4):
                 span = slice(part * rows // 2, (part + 1) * rows // 2)
                 total = sum_buf[slot, span, :].astype(WIDE) + beside_buf[to_z, span, :].astype(WIDE)
-                if incoming is not None:
-                    total = total + incoming[to_z, span, :].astype(WIDE)
+                if incoming:
+                    total = total + line_buf[to_z, span, :].astype(WIDE)
                 sum_buf[slot, span, :] = total.astype(NARROW)
 
         @pl.when(to_z > z)
@@ -1107,11 +1287,11 @@
             @pl.when(here.has_below)
             def _():
                 to_above(to_z).wait_recv()
-                add(under_buf)
+                add(True)
 
             @pl.when(jnp.logical_not(here.has_below))
             def _():
-                add(None)
+                add(False)
 
             to_above(to_z).start()
 
@@ -1119,18 +1299,20 @@
         def _():
             @pl.when(here.has_above)
             def _():
-                to_below(to_z).wait_recv()
-                add(over_buf)
+                from_above(to_z).wait_recv()
+                add(True)
 
             @pl.when(jnp.logical_not(here.has_above))
             def _():
-                add(None)
+                add(False)
 
             to_below(to_z).start()
 
         return carry
 
-    lax.fori_loop(0, depth, chain, 0)
+    lax.fori_loop(0, 1, chain, 0)
+    mail_out(1)
+    lax.fori_loop(1, depth, chain, 0)
 
     @pl.when(here.has_below)
     def _():
@@ -1138,22 +1320,22 @@
 
     @pl.when(jnp.logical_not(here.has_below))
     def _():
-        under_buf[z] = jnp.zeros((2 * rows, D), NARROW)
+        line_buf[z] = jnp.zeros((2 * rows, D), NARROW)
 
     @pl.when(here.has_above)
     def _():
-        to_below(z).wait_recv()
+        from_above(z).wait_recv()
 
     @pl.when(jnp.logical_not(here.has_above))
     def _():
-        over_buf[z] = jnp.zeros((2 * rows, D), NARROW)
+        line_buf[depth] = jnp.zeros((2 * rows, D), NARROW)
 
     def total(span):
         return (
             sum_buf[depth + z, span, :].astype(WIDE)
             + beside_buf[z, span, :].astype(WIDE)
-            + under_buf[z, span, :].astype(WIDE)
-            + over_buf[z, span, :].astype(WIDE)
+            + line_buf[z, span, :].astype(WIDE)
+            + line_buf[depth, span, :].astype(WIDE)
         )
 
     tokens = tok_ref[...].astype(WIDE)
@@ -1185,35 +1367,90 @@
 
     lax.fori_loop(0, depth, finish, 0)
 
-
-def reduce_call(depth, tokens_in, units_in, tok, cot, prm_all, wqkv_t, wup_all, wdown_part, wout_part):
+    send_down.wait()
+    down_ref[...] = g_down[pl.ds(x * half_down, half_down), :] + down_in[...]
+    send_wout.wait()
+    wout_ref[...] = g_wout[pl.ds(x * half_wout, half_wout), :] + wout_in[...]
+
+    def close(offset, carry):
+        other = lax.rem(c + offset, count)
+        for part in range(2):
+            collect(part, other).wait_recv()
+            post(part, other).wait_send()
+        return carry
+
+    lax.fori_loop(1, count, close, 0)
+    for part in range(2):
+        send_grads[part].wait_send()
+    together = jnp.zeros((piece, 128), WIDE)
+    for from_c in range(count):
+        up_ref[:, from_c * units : (from_c + 1) * units] = inbox[0, from_c].astype(WIDE)
+        together = together + inbox[1, from_c, :, 0:128].astype(WIDE)
+    vec_ref[...] = together.T[0:8]
+    for pair in range(count // 2):
+        left = inbox[1, 2 * pair].astype(WIDE)
+        right = inbox[1, 2 * pair + 1].astype(WIDE)
+        for part in range(3):
+            lanes = slice((part + 1) * HD, (part + 2) * HD)
+            to = part * D + pair * 128
+            qkv_ref[:, to : to + 128] = jnp.concatenate([left[:, lanes], right[:, lanes]], axis=1)
+
+
+def reduce_call(depth, tokens_in, turned_in, units_in, tok, cot, rest, xhat, cot_all):
     rows = tok.shape[0]
+    count = depth * 4
+    piece = D // (2 * count)
+    units = rest[2].shape[1]
     vmem = pl.BlockSpec(memory_space=pltpu.VMEM)
+    any_spec = pl.BlockSpec(memory_space=pl.ANY)
     shape = jax.ShapeDtypeStruct
     message = (2 * rows, D)
     return pl.pallas_call(
         functools.partial(reduce_kernel, depth),
-        out_shape=(shape((rows, D), NARROW), shape((rows, D), WIDE)),
-        in_specs=[vmem] * 9,
-        out_specs=(vmem, vmem),
+        out_shape=(
+            shape((rows, D), NARROW),
+            shape((rows, D), WIDE),
+            shape((piece, 3 * D), WIDE),
+            shape((HD // 2, D), WIDE),
+            shape((piece, count * units), WIDE),
+            shape((units // 2, D), WIDE),
+            shape((8, piece), WIDE),
+        ),
+        in_specs=[vmem] * 13 + [any_spec] * 2,
+        out_specs=(vmem,) * 7,
         scratch_shapes=[
             pltpu.VMEM((4 * HD, D), NARROW),
             pltpu.VMEM((4 * HD, D), NARROW),
             pltpu.VMEM((2 * depth,) + message, NARROW),
             pltpu.VMEM((2 * depth,) + message, NARROW),
             pltpu.VMEM((depth,) + message, NARROW),
-            pltpu.VMEM((depth,) + message, NARROW),
-            pltpu.VMEM((depth,) + message, NARROW),
+            pltpu.VMEM((depth + 1,) + message, NARROW),
+            pltpu.VMEM((2, 2, rows, D), NARROW),
+            pltpu.VMEM((4 * HD, D), WIDE),
+            pltpu.VMEM((HD, D), WIDE),
+            pltpu.VMEM((8, 4 * HD), WIDE),
+            pltpu.VMEM((D, 128), WIDE),
+            pltpu.VMEM((2, 2, count, piece, 256), WIDE),
+            pltpu.VMEM((2, count, piece, 256), WIDE),
+            pltpu.VMEM((2, count, piece, 256), NARROW),
+            pltpu.VMEM((2, count, piece, 256), NARROW),
+            pltpu.VMEM((HD // 2, D), WIDE),
+            pltpu.VMEM((units // 2, D), WIDE),
             pltpu.SemaphoreType.DMA((3, 2 * depth)),
             pltpu.SemaphoreType.DMA((2 * depth,)),
             pltpu.SemaphoreType.DMA((depth,)),
-            pltpu.SemaphoreType.DMA((2, depth)),
+            pltpu.SemaphoreType.DMA((depth + 1,)),
+            pltpu.SemaphoreType.DMA((2, 2)),
+            pltpu.SemaphoreType.DMA((4,)),
+            pltpu.SemaphoreType.DMA((4,)),
+            pltpu.SemaphoreType.DMA((2, count)),
+            pltpu.SemaphoreType.DMA((2, count)),
         ],
         name="reduce_rows",
         compiler_params=pltpu.CompilerParams(
             collective_id=2, has_side_effects=True, vmem_limit_bytes=VMEM_LIMIT
         ),
-    )(tokens_in, units_in, tok, cot, prm_all, wqkv_t, wup_all, wdown_part, wout_part)
+    )(tokens_in, turned_in, units_in, tok, cot, *rest, xhat, cot_all)
 
 
 def fast_shards(depth, *arguments):
@@ -1241,39 +1478,10 @@
         gather_call(depth, tok, cot, prm, turn, w_qkv, w_out, w_up, w_down)
     )
     turned, by_token = attention_call(lengths, dealing, heads, turn)
-    out, grad_tokens = reduce_call(
-        depth, by_token, units, tok, cot, prm_all, wqkv_t, wup_all, wdown_part, wout_part
-    )
-
-    g_out = jnp.einsum("ser,srd->ed", turned[:, :HD], cot_all, preferred_element_type=WIDE)
-    g_one = jnp.einsum("ser,srd->ed", turned[:, HD:], xhat, preferred_element_type=WIDE)
-    sum_one = jnp.sum(turned[:, HD:].astype(WIDE), axis=(0, 2))[:, None]
-    sum_two = jnp.sum(g_sum, axis=0)[:, None]
-    gain_a, bias_a, gain_b, bias_b = prm_all[0:1], prm_all[1:2], prm_all[2:3], prm_all[3:4]
-    wide_qkv = wqkv_t.astype(WIDE)
-    wide_up = wup_all.astype(WIDE).T
-    vectors = jnp.stack(
-        [
-            jnp.sum(wide_qkv * g_one, axis=0),
-            jnp.sum(wide_qkv * sum_one, axis=0),
-            jnp.sum(wide_up * g_up, axis=0),
-            jnp.sum(wide_up * sum_two, axis=0),
-        ]
-    )
-    columns = jnp.concatenate(
-        [g_one * gain_a + bias_a * sum_one, g_up * gain_b + bias_b * sum_two, vectors], axis=0
-    )
-    width = columns.shape[0]
-    piece = D // (2 * count)
-    split = columns.reshape(width, count, 2, piece).transpose(2, 1, 0, 3)
-    split = lax.psum_scatter(split, "wsh", scatter_dimension=0, tiled=False)
-    split = lax.all_to_all(split, "ctx", split_axis=0, concat_axis=0, tiled=True)
-    units_count = g_up.shape[0]
-    qkv_part = split[:, : 3 * HD].reshape(count, 3, HD, piece).transpose(3, 1, 0, 2).reshape(piece, 3 * D)
-    up_part = split[:, 3 * HD : 3 * HD + units_count].transpose(2, 0, 1).reshape(piece, count * units_count)
-    vector_part = jnp.sum(split[:, 3 * HD + units_count :], axis=0)
-    out_part = lax.psum_scatter(g_out, "wsh", scatter_dimension=0, tiled=True)
-    down_part = lax.psum_scatter(g_down, "wsh", scatter_dimension=0, tiled=True)
+    rest = (prm_all, wqkv_t, wup_all, wdown_part, wout_part, g_up, g_down, g_sum)
+    out, grad_tokens, qkv_part, out_part, up_part, down_part, vector_part = reduce_call(
+        depth, by_token, turned, units, tok, cot, rest, xhat, cot_all
+    )
     return (
         out.reshape(tokens.shape),
         grad_tokens.reshape(tokens.shape),

time: 374 us -> 320 us (0.86)
  waiting for transfers between devices: 27.9 us -> 0 us
  between operations: 14 us -> 0.71 us
  Pallas kernels: 290 us -> 302 us
  matrix products: 11.6 us -> 0 us
  starting transfers between devices: 5.73 us -> 0 us
  local copies, waits for them, and re-layouts: 17.8 us -> 13.6 us
    reduce_scatter x3 -> x0, waiting for transfers between devices: 27.2 us -> none  [the longest x1 27.1 us: fast_shards(): split = lax.psum_scatter(split, 'wsh', scatter_dimension=0, tiled=False)]
    dot_general x2 -> x0, matrix products: 11.6 us -> none  [the longest x1 5.85 us: fast_shards(): jnp.einsum('ser,srd->ed', turned[:, :HD], cot_all, preferred_element_type...]
    pallas_call x1, Pallas kernels: 114 us -> 121 us  [reduce_call(): pl.pallas_call(functools.partial(reduce_kernel, depth), out_shape=(shape(...]
    concatenate x11 -> x0, local copies, waits for them, and re-layouts: 7.4 us -> none  [fast_shards(): jnp.concatenate([g_one * gain_a + bias_a * sum_one, g_up * gain_b + bias_...]
    unnamed x17 -> x12, local copies, waits for them, and re-layouts: 2.06 us -> 9.18 us
    all_to_all x1 -> x0, starting transfers between devices: 5.61 us -> none  [fast_shards(): lax.all_to_all(split, 'ctx', split_axis=0, concat_axis=0, tiled=True)]
    pallas_call x1, Pallas kernels: 53.7 us -> 58.2 us  [attention_call(): pl.pallas_call(attention_kernel, out_shape=(shape((blocks, 4 * HD, rows),...]
  transfers between devices with their start and end apart: 4 -> 0, of which waited for: 1 -> 0; matrix products, arithmetic and copies ran while one was open for 3% -> 0% of each run, Pallas kernels for 30% -> 0%
where the time goes in v2:
time: 320 us
  Pallas kernels  302 us (94%)
  local copies, waits for them, and re-layouts  13.6 us (4%)
  other arithmetic  4.13 us (1%)
    pallas_call x1, Pallas kernels, gather_call(): pl.pallas_call(functools.partial(gather_kernel, depth), out_shape=(shape(...  122 us
    pallas_call x1, Pallas kernels, reduce_call(): pl.pallas_call(functools.partial(reduce_kernel, depth), out_shape=(shape(...  121 us
    pallas_call x1, Pallas kernels, attention_call(): pl.pallas_call(attention_kernel, out_shape=(shape((blocks, 4 * HD, rows),...  58.2 us
    unnamed x12, local copies, waits for them, and re-layouts  9.18 us

profile of v2, /device:TPU:0, one launch (start us, length us, event | category | flops | bytes accessed | tf_op | source)
XLA Modules:
  0.0 320.5 jit_solution(14022300561730825724)
XLA Ops:
  0.7 0.7 multiply_bitcast_fusion
  1.4 0.8 reduce_window_sum.11
  2.2 0.7 subtract_bitcast_fusion
  2.9 0.1 copy.25
  3.0 0.1 broadcast_bitcast_fusion
  3.1 0.7 stack.19
  3.7 0.7 stack.20
  4.4 0.7 stack.21
  5.1 0.7 stack.22
  5.8 0.1 copy.24
  5.9 0.1 add.28
  6.0 0.6 convert_element_type.10.prm_ref
  6.6 0.5 multiply_cosine_fusion
  7.2 0.7 pad_maximum_fusion.turn_ref
  7.9 122.4 %gather_and_units.1 = (bf16[16,256,256]{2,1,0:T(8,128)(2,1)}, bf16[16,256,512]{2,1,0:T(8,128)(2,1)}, bf16[16,256,1024]{2,1,0:T(8,128)(2,1)}, bf16[16,256,1024]{2...) custom-call(bf16[256,1024]{1,0:T(8,128)(2,1)} %bitcast.28, ...), custom_call_target="tpu_custom_call" | custom-call | tf_op jit(solution)/shard_map/gather_and_units/pallas_call | solution.py:768
  130.3 58.2 %head_attention.1 = (bf16[16,256,256]{2,1,0:T(8,128)(2,1)}, bf16[16,256,256]{2,1,0:T(8,128)(2,1)}) custom-call(s32[2,4]{1,0:T(2,128)} %lengths_ref.1, s32[2,16]{1,0:T(2,128)} %dealing_ref.1, bf16[16,256,256]{2,1,0:T(8,128)(2,1)} %get-tuple-element.31.heads_ref, f32[16,16,256]{2,1,0:T(8,128)} %pad_maximum_fusion.turn_ref), custom_call_target="tpu_custom_call" | custom-call | tf_op jit(solution)/shard_map/head_attention/pallas_call | solution.py:955
  188.6 121.4 %reduce_rows.1 = (bf16[256,1024]{1,0:T(8,128)(2,1)}, f32[256,1024]{1,0:T(8,128)}, f32[32,3072]{1,0:T(8,128)}, f32[32,1024]{1,0:T(8,128)}, f32[32,4096]{1,0:T(8,1...) custom-call(bf16[16,256,256]{2,1,0:T(8,128)(2,1)} %get-tuple-element.32.tokens_in, ...), custom_call_target="tpu_custom_call" | custom-call | tf_op jit(solution)/shard_map/reduce_rows/pallas_call | solution.py:1408
  310.0 1.4 slice_bitcast_fusion
  311.4 1.9 copy.39
  313.3 2.3 copy.40
  315.6 1.8 copy.41
  317.3 1.6 copy.42
  318.9 0.8 copy.43
  319.7 0.8 copy.44
  (11 shorter events, 0.1 us)
Async XLA Ops:
  310.0 8.9 %copy-start.1 = (f32[32,4096]{1,0:T(8,128)S(1)}, f32[32,4096]{1,0:T(8,128)}, u32[]{:S(2)}) copy-start(f32[32,4096]{1,0:T(8,128)} %get-tuple-element.76) | copy-start | bytes 1572868
  310.0 9.7 %copy-start = (f32[128,1024]{1,0:T(8,128)S(1)}, f32[128,1024]{1,0:T(8,128)}, u32[]{:S(2)}) copy-start(f32[128,1024]{1,0:T(8,128)} %get-tuple-element.77) | copy-start | bytes 1572868

commit v3 on v2

--- a/solution.py
+++ b/solution.py
@@ -466,12 +466,58 @@
         pl.semaphore_wait(barrier, count)
 
 
+FREQUENCY = tuple(10000.0 ** (-2.0 * i / ROT) for i in range(ROT // 2))
+
+
+def turning(place):
+    row = lax.broadcasted_iota(jnp.int32, (ROT // 2, 1), 0)
+    frequency = jnp.full((ROT // 2, 1), FREQUENCY[0], WIDE)
+    for at in range(1, ROT // 2):
+        frequency = jnp.where(row == at, FREQUENCY[at], frequency)
+    angles = place.astype(WIDE) * frequency
+    return jnp.cos(angles), jnp.sin(angles)
+
+
+def starts_of(lengths_ref, group):
+    starts = []
+    so_far = jnp.int32(0)
+    for piece in range(lengths_ref.shape[1] - 1):
+        so_far = so_far + lengths_ref[group, piece]
+        starts.append(so_far)
+    return starts
+
+
+def opening_of(natural, starts):
+    opening = jnp.zeros(natural.shape, jnp.int32)
+    for start in starts:
+        opening = jnp.where(natural >= start, start, opening)
+    return opening
+
+
+def find_blocks(dealing_ref, found):
+    groups, blocks = dealing_ref.shape
+    for group in range(groups):
+
+        def look(block, carry):
+            where = jnp.int32(0)
+            for at in range(blocks):
+                where = jnp.where(dealing_ref[group, at] == block, jnp.int32(at), where)
+            found[group, block] = where
+            return carry
+
+        lax.fori_loop(0, blocks, look, 0)
+
+
 def gather_kernel(
     depth,
+    lengths_ref,
+    dealing_ref,
     tok_ref,
     cot_ref,
-    prm_ref,
-    turn_ref,
+    gain_one_ref,
+    bias_one_ref,
+    gain_two_ref,
+    bias_two_ref,
     wqkv_ref,
     wout_ref,
     wup_ref,
@@ -480,6 +526,8 @@
     units_out,
     xhat_out,
     cot_out,
+    attended_out,
+    total_out,
     g_up,
     g_down,
     g_sum,
@@ -492,8 +540,12 @@
     xhat_all,
     heads_buf,
     units_buf,
+    slope_buf,
+    wide,
+    k_rows,
     wq_buf,
     prm_buf,
+    found,
     in_sem,
     w_sem,
     wsend_sem,
@@ -506,16 +558,21 @@
     c, x, y, z, core = here.c, here.x, here.y, here.z, here.core
     count = depth * 4
     rows = tok_ref.shape[0]
+    groups = dealing_ref.shape[0]
     units = wup_all.shape[1]
-    half = prm_ref.shape[1]
+    half = prm_buf.shape[2]
     order = near_first(depth)
 
     own_in = (
-        pltpu.make_async_copy(tok_ref, both.at[c, pl.ds(0, rows)], in_sem.at[0]),
-        pltpu.make_async_copy(cot_ref, both.at[c, pl.ds(rows, rows)], in_sem.at[1]),
+        pltpu.make_async_copy(tok_ref, both.at[0, c], in_sem.at[0]),
+        pltpu.make_async_copy(cot_ref, both.at[1, c], in_sem.at[1]),
     )
     for copy in own_in:
         copy.start()
+    prm_rows = [
+        ref[...].astype(WIDE) for ref in (gain_one_ref, bias_one_ref, gain_two_ref, bias_two_ref)
+    ]
+    prm_buf[x] = jnp.concatenate(prm_rows + prm_rows, axis=0)
 
     pair = c // 2
     per_half = count // 2
@@ -535,7 +592,6 @@
             wup_all.at[pl.ds(pl.multiple_of(x * half, 128), half)],
         )
     )
-    shared.append((prm_ref, prm_buf.at[x]))
     held = (
         (wdown_ref.at[pl.ds(pl.multiple_of(inside * units, 128), units)], wdown_part),
         (wout_ref.at[pl.ds(pl.multiple_of(inside * HD, HD), HD)], wout_part),
@@ -561,6 +617,8 @@
             device_id_type=MESH,
         )
 
+    prm_copy = remote(prm_buf.at[x], prm_buf.at[x], 4)
+    prm_copy.start()
     for at, (source, place) in enumerate(shared):
         remote(source, place, at).start()
 
@@ -569,38 +627,39 @@
         for at, (source, place) in enumerate(held):
             remote(source, place, 5 + at).start()
 
-    def passing(shard, way):
+    def passing(what, shard, way):
         device = (here.beside, here.twin, here.above, here.below)[way]
         return pltpu.make_async_remote_copy(
-            both.at[shard],
-            both.at[shard],
-            send_sem.at[way, shard],
-            recv_sem.at[shard],
+            both.at[what, shard],
+            both.at[what, shard],
+            send_sem.at[what, way, shard],
+            recv_sem.at[what, shard],
             device_id=device,
             device_id_type=MESH,
         )
 
-    for copy in own_in:
-        copy.wait()
-
-    def onward(shard, from_z):
-        passing(shard, 0).start()
+    def onward(what, shard, from_z):
+        passing(what, shard, 0).start()
 
         @pl.when(jnp.logical_and(from_z <= z, here.has_above))
         def _():
-            passing(shard, 2).start()
+            passing(what, shard, 2).start()
 
         @pl.when(jnp.logical_and(from_z >= z, here.has_below))
         def _():
-            passing(shard, 3).start()
-
-        passing(shard, 1).start()
-
-    onward(c, z)
+            passing(what, shard, 3).start()
+
+        passing(what, shard, 1).start()
+
+    own_in[0].wait()
+    onward(0, c, z)
+    own_in[1].wait()
+    find_blocks(dealing_ref, found)
 
     for at, (source, place) in enumerate(shared):
         pltpu.make_async_copy(source, place, w_sem.at[at]).wait()
         remote(source, place, at).wait_recv()
+    prm_copy.wait_recv()
 
     @pl.when(is_owner)
     def _():
@@ -625,20 +684,32 @@
     g_down[...] = jnp.zeros_like(g_down)
     g_sum[...] = jnp.zeros_like(g_sum)
 
-    def compute(shard):
-        tokens = both[shard, 0:rows, :].astype(WIDE)
+    kept = (
+        (xhat_all, xhat_out),
+        (both.at[1], cot_out),
+        (heads_buf, heads_out),
+        (units_buf, units_out),
+    )
+
+    def copy_out(at, shard):
+        source, place = kept[at]
+        return pltpu.make_async_copy(source.at[shard], place.at[shard], out_sem.at[at, shard])
+
+    def ahead(shard):
+        tokens = both[0, shard].astype(WIDE)
         average = jnp.mean(tokens, axis=-1, keepdims=True)
         centred = tokens - average
         variance = jnp.mean(centred * centred, axis=-1, keepdims=True)
         xhat = centred * lax.rsqrt(variance + EPSILON)
-        xhat_low = xhat.astype(NARROW)
-        xhat_all[shard] = xhat_low
+        xhat_all[shard] = xhat.astype(NARROW)
         n_one = (xhat * prm_all[0:1, :] + prm_all[1:2, :]).astype(NARROW)
         n_two = (xhat * prm_all[2:3, :] + prm_all[3:4, :]).astype(NARROW)
-        cotangent = both[shard, rows : 2 * rows, :]
         mixed = dot(wqkv_t[...], n_one, NT)
-        turn = turn_ref[shard]
-        cosine, sine = turn[0:8], turn[8:16]
+        places = []
+        for group in range(groups):
+            natural = dealing_ref[group, shard] * BLK + lax.broadcasted_iota(jnp.int32, (1, BLK), 1)
+            places.append(natural - opening_of(natural, starts_of(lengths_ref, group)))
+        cosine, sine = turning(jnp.concatenate(places, axis=1))
         pieces = []
         for base in (0, HD):
             first, second = mixed[base : base + 8], mixed[base + 8 : base + 16]
@@ -648,109 +719,169 @@
                 mixed[base + 16 : base + HD],
             ]
         pieces.append(mixed[2 * HD : 3 * HD])
-        pieces.append(dot(wout_part[...], cotangent, NT))
-        heads_buf[shard] = jnp.concatenate(pieces, axis=0).astype(NARROW)
+        heads_buf[shard, 0 : 3 * HD, :] = jnp.concatenate(pieces, axis=0).astype(NARROW)
         hidden = dot(n_two, wup_all[...])
         spread = 0.5 * (1.0 + lax.erf(hidden * (0.5**0.5)))
-        activated = (hidden * spread).astype(NARROW)
-        slope = spread + hidden * (jnp.exp(hidden * hidden * -0.5) * 0.3989422804014327)
-        g_hidden_f = dot(cotangent, wdown_part[...], NT) * slope
-        g_hidden = g_hidden_f.astype(NARROW)
-        units_buf[shard, :, 0:units] = activated
+        units_buf[shard, :, 0:units] = (hidden * spread).astype(NARROW)
+        slope_buf[shard] = spread + hidden * (jnp.exp(hidden * hidden * -0.5) * 0.3989422804014327)
+        copy_out(0, shard).start()
+
+    def behind(shard):
+        cotangent = both[1, shard]
+        heads_buf[shard, 3 * HD : 4 * HD, :] = dot(wout_part[...], cotangent, NT).astype(NARROW)
+        g_hidden = (dot(cotangent, wdown_part[...], NT) * slope_buf[shard]).astype(NARROW)
         units_buf[shard, :, units : 2 * units] = g_hidden
-        g_up[...] += dot(g_hidden, xhat_low, TN)
-        g_down[...] += dot(activated, cotangent, TN)
+        g_up[...] += dot(g_hidden, xhat_all[shard], TN)
+        g_down[...] += dot(units_buf[shard, :, 0:units], cotangent, TN)
         g_sum[...] += jnp.sum(g_hidden.astype(WIDE).reshape(rows // 8, 8, units), axis=0)
-        pltpu.make_async_copy(xhat_all.at[shard], xhat_out.at[shard], out_sem.at[0, shard]).start()
-        pltpu.make_async_copy(
-            both.at[shard, pl.ds(rows, rows)], cot_out.at[shard], out_sem.at[1, shard]
-        ).start()
-        pltpu.make_async_copy(
-            heads_buf.at[shard], heads_out.at[shard], out_sem.at[2, shard]
-        ).start()
-        pltpu.make_async_copy(
-            units_buf.at[shard], units_out.at[shard], out_sem.at[3, shard]
-        ).start()
+        for at in (1, 2, 3):
+            copy_out(at, shard).start()
 
     inner = jnp.logical_and(here.has_above, here.has_below)
 
-    def step(at, carry):
-        turn_no = at // 4
-        kind = lax.rem(at, 4)
-        behind = jnp.where(kind >= 2, turn_no - 1, turn_no)
-        from_z = pick2(z, jnp.clip(behind, 0, depth - 1), order)
-        next_z = pick2(z, jnp.clip(turn_no + 1, 0, depth - 1), order)
-        shard_y = jnp.where(kind >= 2, 1 - y, y)
-        shard_core = jnp.where(lax.rem(kind, 2) == 1, 1 - core, core)
-        shard = here.at(from_z, shard_y, shard_core)
-        live = jnp.logical_and(behind >= 0, behind < depth)
-
-        early = jnp.logical_and(inner, turn_no == 2)
-        is_own = jnp.logical_and(kind == 0, turn_no == 0)
-
-        @pl.when(jnp.logical_and(live, jnp.logical_not(jnp.logical_or(is_own, jnp.logical_and(kind == 0, early)))))
+    def sweep(what, work, beside_work):
+        def step(at, carry):
+            turn_no = at // 4
+            kind = lax.rem(at, 4)
+            late = jnp.where(kind >= 2, turn_no - 1, turn_no)
+            from_z = pick2(z, jnp.clip(late, 0, depth - 1), order)
+            next_z = pick2(z, jnp.clip(turn_no + 1, 0, depth - 1), order)
+            shard_y = jnp.where(kind >= 2, 1 - y, y)
+            shard_core = jnp.where(lax.rem(kind, 2) == 1, 1 - core, core)
+            shard = here.at(from_z, shard_y, shard_core)
+            live = jnp.logical_and(late >= 0, late < depth)
+
+            early = jnp.logical_and(inner, turn_no == 2)
+            is_own = jnp.logical_and(kind == 0, turn_no == 0)
+            done = jnp.logical_or(is_own, jnp.logical_and(kind == 0, early))
+
+            @pl.when(jnp.logical_and(live, jnp.logical_not(done)))
+            def _():
+                passing(what, shard, 1).wait_recv()
+
+            @pl.when(jnp.logical_and(jnp.logical_and(kind == 0, live), jnp.logical_not(done)))
+            def _():
+                onward(what, shard, from_z)
+
+            @pl.when(jnp.logical_and(kind == 2, live))
+            def _():
+                passing(what, shard, 1).start()
+
+            @pl.when(jnp.logical_and(jnp.logical_and(kind == 1, turn_no == 1), inner))
+            def _():
+                following = here.at(next_z, y, core)
+                passing(what, following, 1).wait_recv()
+                onward(what, following, next_z)
+
+            beside_work(at)
+
+            @pl.when(live)
+            def _():
+                work(shard)
+
+            return carry
+
+        lax.fori_loop(0, 4 * depth + 4, step, 0)
+
+    def cotangent_too(at):
+        @pl.when(at == 4 * (depth - 1) + 1)
         def _():
-            passing(shard, 1).wait_recv()
-
-        @pl.when(
-            jnp.logical_and(
-                jnp.logical_and(kind == 0, live),
-                jnp.logical_not(jnp.logical_or(turn_no == 0, early)),
-            )
-        )
+            onward(1, c, z)
+
+    sweep(0, ahead, cotangent_too)
+
+    spans = count // 2
+    span = 2 * BLK
+
+    def bring(at, carry):
+        for group in range(groups):
+            lanes = slice(group * BLK, (group + 1) * BLK)
+            for side in range(2):
+                source = found[group, 2 * at + side]
+                part = heads_buf[source, 0 : 3 * HD, lanes]
+                to = slice(side * BLK, (side + 1) * BLK)
+                wide[group, at, 0:HD, to] = (part[0:HD].astype(WIDE) * HD ** (-0.5)).astype(NARROW)
+                wide[group, at, HD : 2 * HD, to] = part[2 * HD : 3 * HD]
+                k_rows[group, at, to, :] = part[HD : 2 * HD].astype(WIDE).T.astype(NARROW)
+        return carry
+
+    lax.fori_loop(0, spans, bring, 0)
+    openings = [starts_of(lengths_ref, group) for group in range(groups)]
+
+    def attend(at):
+        group = lax.rem(at, groups)
+        turn_no = at // groups
+        mine = jnp.where(lax.rem(turn_no, 2) == 0, spans - 1 - turn_no // 2, turn_no // 2)
+        natural = mine * span + lax.broadcasted_iota(jnp.int32, (1, span), 1)
+        opening = opening_of(natural, [jnp.where(group == 0, *pair) for pair in zip(*openings)])
+        key_in = lax.broadcasted_iota(jnp.int32, (span, span), 0)
+        queries = wide[group, mine, 0:HD, :]
+
+        def add(keys_at, state, allowed):
+            top, total, so_far = state
+            raw = jnp.where(allowed, dot(k_rows[group, keys_at], queries), MASKED)
+            new_top = jnp.maximum(top, jnp.max(raw, axis=0, keepdims=True))
+            risen = jnp.exp(raw - new_top)
+            fade = jnp.exp(top - new_top)
+            total = total * fade + jnp.sum(risen, axis=0, keepdims=True)
+            values = wide[group, keys_at, HD : 2 * HD, :]
+            return new_top, total, so_far * fade + dot(values, risen.astype(NARROW))
+
+        state = (
+            jnp.full((1, span), MASKED, WIDE),
+            jnp.zeros((1, span), WIDE),
+            jnp.zeros((HD, span), WIDE),
+        )
+        place = key_in + mine * span
+        state = add(mine, state, jnp.logical_and(place <= natural, place >= opening))
+
+        def earlier(back, state):
+            keys_at = mine - 1 - back
+            return add(keys_at, state, key_in >= opening - keys_at * span)
+
+        top, total, so_far = lax.fori_loop(0, mine, earlier, state)
+        attended = so_far / total
+        for side in range(2):
+            attended_out[group, 2 * mine + side] = attended[:, side * BLK : (side + 1) * BLK]
+        total_out[group, mine] = jnp.broadcast_to(top + jnp.log(total), (8, span))
+
+    def attend_too(at):
+        @pl.when(at < groups * spans)
         def _():
-            onward(shard, from_z)
-
-        @pl.when(jnp.logical_and(kind == 2, live))
-        def _():
-            passing(shard, 1).start()
-
-        @pl.when(jnp.logical_and(jnp.logical_and(kind == 1, turn_no == 1), inner))
-        def _():
-            following = here.at(next_z, y, core)
-            passing(following, 1).wait_recv()
-            onward(following, next_z)
-
-        @pl.when(live)
-        def _():
-            compute(shard)
-
-        return carry
-
-    lax.fori_loop(0, 4 * depth + 4, step, 0)
+            attend(at)
+
+    sweep(1, behind, attend_too)
 
     def finish(shard, carry):
         shard_z = shard // 4
         mine = lax.rem(shard, 2) == core
         column = lax.rem(shard // 2, 2) == y
-
-        @pl.when(mine)
-        def _():
-            passing(shard, 1).wait_send()
-
-        @pl.when(jnp.logical_and(mine, column))
-        def _():
-            passing(shard, 0).wait_send()
-
-            @pl.when(jnp.logical_and(shard_z <= z, here.has_above))
+        for what in range(2):
+
+            @pl.when(mine)
             def _():
-                passing(shard, 2).wait_send()
-
-            @pl.when(jnp.logical_and(shard_z >= z, here.has_below))
+                passing(what, shard, 1).wait_send()
+
+            @pl.when(jnp.logical_and(mine, column))
             def _():
-                passing(shard, 3).wait_send()
-
-        pltpu.make_async_copy(xhat_all.at[shard], xhat_out.at[shard], out_sem.at[0, shard]).wait()
-        pltpu.make_async_copy(
-            both.at[shard, pl.ds(rows, rows)], cot_out.at[shard], out_sem.at[1, shard]
-        ).wait()
-        pltpu.make_async_copy(heads_buf.at[shard], heads_out.at[shard], out_sem.at[2, shard]).wait()
-        pltpu.make_async_copy(units_buf.at[shard], units_out.at[shard], out_sem.at[3, shard]).wait()
+                passing(what, shard, 0).wait_send()
+
+                @pl.when(jnp.logical_and(shard_z <= z, here.has_above))
+                def _():
+                    passing(what, shard, 2).wait_send()
+
+                @pl.when(jnp.logical_and(shard_z >= z, here.has_below))
+                def _():
+                    passing(what, shard, 3).wait_send()
+
+        for at in range(4):
+            copy_out(at, shard).wait()
         return carry
 
     lax.fori_loop(0, count, finish, 0)
     for at, (source, place) in enumerate(shared):
         remote(source, place, at).wait_send()
+    prm_copy.wait_send()
 
     @pl.when(is_owner)
     def _():
@@ -758,12 +889,15 @@
             remote(source, place, 5 + at).wait_send()
 
 
-def gather_call(depth, tok, cot, prm, turn, w_qkv, w_out, w_up, w_down):
+def gather_call(depth, lengths, dealing, tok, cot, gains, w_qkv, w_out, w_up, w_down):
     count = depth * 4
     rows = tok.shape[0]
+    groups = dealing.shape[0]
+    spans, span = count // 2, 2 * BLK
     units = w_up.shape[1] // count
     any_spec = pl.BlockSpec(memory_space=pl.ANY)
     vmem = pl.BlockSpec(memory_space=pltpu.VMEM)
+    smem = pl.BlockSpec(memory_space=pltpu.SMEM)
     shape = jax.ShapeDtypeStruct
     return pl.pallas_call(
         functools.partial(gather_kernel, depth),
@@ -772,6 +906,8 @@
             shape((count, rows, 2 * units), NARROW),
             shape((count, rows, D), NARROW),
             shape((count, rows, D), NARROW),
+            shape((groups, count, HD, BLK), WIDE),
+            shape((groups, spans, 8, span), WIDE),
             shape((units, D), WIDE),
             shape((units, D), WIDE),
             shape((8, units), WIDE),
@@ -781,214 +917,53 @@
             shape((HD, D), NARROW),
             shape((8, D), WIDE),
         ),
-        in_specs=[any_spec, any_spec, any_spec, vmem] + [any_spec] * 4,
-        out_specs=(any_spec,) * 4 + (vmem,) * 8,
+        in_specs=[smem, smem, any_spec, any_spec] + [vmem] * 4 + [any_spec] * 4,
+        out_specs=(any_spec,) * 4 + (vmem,) * 10,
         scratch_shapes=[
-            pltpu.VMEM((count, 2 * rows, D), NARROW),
+            pltpu.VMEM((2, count, rows, D), NARROW),
             pltpu.VMEM((count, rows, D), NARROW),
             pltpu.VMEM((count, 4 * HD, rows), NARROW),
             pltpu.VMEM((count, rows, 2 * units), NARROW),
+            pltpu.VMEM((count, rows, units), WIDE),
+            pltpu.VMEM((groups, spans, 2 * HD, span), NARROW),
+            pltpu.VMEM((groups, spans, span, HD), NARROW),
             pltpu.VMEM((2, 3, D // 2, 128), NARROW),
             pltpu.VMEM((2, 8, D // 2), WIDE),
+            pltpu.SMEM((groups, count), jnp.int32),
             pltpu.SemaphoreType.DMA((2,)),
             pltpu.SemaphoreType.DMA((7,)),
             pltpu.SemaphoreType.DMA((7,)),
             pltpu.SemaphoreType.DMA((7,)),
-            pltpu.SemaphoreType.DMA((4, count)),
-            pltpu.SemaphoreType.DMA((count,)),
+            pltpu.SemaphoreType.DMA((2, 4, count)),
+            pltpu.SemaphoreType.DMA((2, count)),
             pltpu.SemaphoreType.DMA((4, count)),
         ],
-        name="gather_and_units",
+        name="gather_and_forward",
         compiler_params=pltpu.CompilerParams(
             collective_id=1, has_side_effects=True, vmem_limit_bytes=VMEM_LIMIT
         ),
-    )(tok, cot, prm, turn, w_qkv, w_out, w_up, w_down)
-
-
-def attention_kernel(
-    lengths_ref,
-    dealing_ref,
-    heads_ref,
-    turn_ref,
-    turned_out,
-    tokens_out,
-    wide,
-    q_rows,
-    k_rows,
-    v_rows,
-    g_rows,
-    scores,
-    probs,
-    g_query,
-    attended,
-    g_key,
-    g_value,
-    turn_wide,
-    found,
-):
-    blocks = heads_ref.shape[0]
-    groups = heads_ref.shape[2] // BLK
-    spans = blocks // 2
-    span = 2 * BLK
-    scale = HD ** (-0.5)
-
-    for group in range(groups):
-        lanes = slice(group * BLK, (group + 1) * BLK)
-
-        def note(block, carry):
-            found[dealing_ref[group, block]] = block
-            return carry
-
-        lax.fori_loop(0, blocks, note, 0)
-        starts = [jnp.int32(0)]
-        for piece in range(lengths_ref.shape[1] - 1):
-            starts.append(starts[-1] + lengths_ref[group, piece])
-
-        def bring(at, carry):
-            for side in range(2):
-                source = found[2 * at + side]
-                part = heads_ref[source, :, lanes]
-                to = slice(side * BLK, (side + 1) * BLK)
-                wide[at, :, to] = part
-                turn_wide[at, :, to] = turn_ref[source, :, lanes]
-                part = part.astype(WIDE)
-                row = pl.ds(pl.multiple_of(side * BLK, BLK), BLK)
-                q_rows[at, row, :] = part[0:HD].T.astype(NARROW)
-                k_rows[at, row, :] = part[HD : 2 * HD].T.astype(NARROW)
-                v_rows[at, row, :] = part[2 * HD : 3 * HD].T.astype(NARROW)
-                g_rows[at, row, :] = part[3 * HD : 4 * HD].T.astype(NARROW)
-            g_key[at] = jnp.zeros((span, HD), WIDE)
-            g_value[at] = jnp.zeros((span, HD), WIDE)
-            return carry
-
-        lax.fori_loop(0, spans, bring, 0)
-
-        def one_span(at, carry):
-            natural = at * span + lax.broadcasted_iota(jnp.int32, (1, span), 1)
-            opening = jnp.zeros((1, span), jnp.int32)
-            first = jnp.int32(0)
-            for start in starts[1:]:
-                opening = jnp.where(natural >= start, start, opening)
-                first = jnp.where(at * span >= start, start, first)
-            low = first // span
-            queries_t = wide[at, 0:HD, :]
-            g_attended_t = wide[at, 3 * HD : 4 * HD, :]
-            key_in = lax.broadcasted_iota(jnp.int32, (span, span), 0)
-
-            def score(keys_at, top):
-                raw = dot(k_rows[keys_at], queries_t) * scale
-                place = key_in + keys_at * span
-                allowed = jnp.logical_and(place <= natural, place >= opening)
-                kept = jnp.where(allowed, raw, MASKED)
-                scores[keys_at] = kept
-                return jnp.maximum(top, jnp.max(kept.reshape(span // 8, 8, span), axis=0))
-
-            top = lax.fori_loop(low, at + 1, score, jnp.full((8, span), MASKED, WIDE))
-            top = jnp.max(top, axis=0, keepdims=True)
-
-            def power(keys_at, total):
-                risen = jnp.exp(scores[keys_at] - top)
-                scores[keys_at] = risen
-                return total + jnp.sum(risen.reshape(span // 8, 8, span), axis=0)
-
-            total = lax.fori_loop(low, at + 1, power, jnp.zeros((8, span), WIDE))
-            share = 1.0 / jnp.sum(total, axis=0, keepdims=True)
-            attended[...] = jnp.zeros_like(attended)
-            g_query[...] = jnp.zeros_like(g_query)
-
-            def weigh(keys_at, carry):
-                part = scores[keys_at] * share
-                scores[keys_at] = part
-                low_part = part.astype(NARROW)
-                probs[keys_at] = low_part
-                attended[...] += dot(wide[keys_at, 2 * HD : 3 * HD, :], low_part)
-                return carry
-
-            lax.fori_loop(low, at + 1, weigh, 0)
-            row_dot = jnp.sum(attended[...] * g_attended_t.astype(WIDE), axis=0, keepdims=True)
-
-            def back(keys_at, carry):
-                g_probs = dot(v_rows[keys_at], g_attended_t)
-                g_scores = (scores[keys_at] * (g_probs - row_dot)).astype(NARROW)
-                g_query[...] += dot(wide[keys_at, HD : 2 * HD, :], g_scores)
-                g_key[keys_at] += dot(g_scores, q_rows[at])
-                g_value[keys_at] += dot(probs[keys_at], g_rows[at])
-                return carry
-
-            lax.fori_loop(low, at + 1, back, 0)
-            wide[at, 0:HD, :] = (unturn(g_query[...] * scale, turn_wide[at])).astype(NARROW)
-            wide[at, 3 * HD : 4 * HD, :] = attended[...].astype(NARROW)
-            return carry
-
-        lax.fori_loop(0, spans, one_span, 0)
-
-        def give(at, carry):
-            keys_t = unturn(g_key[at].T * scale, turn_wide[at]).astype(NARROW)
-            values_t = g_value[at].T.astype(NARROW)
-            whole = jnp.concatenate(
-                [wide[at, 3 * HD : 4 * HD, :], wide[at, 0:HD, :], keys_t, values_t], axis=0
-            )
-            for side in range(2):
-                to = found[2 * at + side]
-                part = whole[:, side * BLK : (side + 1) * BLK]
-                turned_out[to, :, lanes] = part
-                tokens_out[to, lanes, :] = part.astype(WIDE).T.astype(NARROW)
-            return carry
-
-        lax.fori_loop(0, spans, give, 0)
-
-
-def unturn(rows, turn):
-    cosine, sine = turn[0:8], turn[8:16]
+    )(lengths, dealing, tok, cot, *gains, w_qkv, w_out, w_up, w_down)
+
+
+def far_first(depth):
+    return [list(reversed(row)) for row in near_first(depth)]
+
+
+def unturn(rows, cosine, sine):
     first, second = rows[0:8], rows[8:16]
     return jnp.concatenate(
         [first * cosine + second * sine, second * cosine - first * sine, rows[16:]], axis=0
     )
 
 
-def attention_call(lengths, dealing, heads, turn):
-    blocks, _, rows = heads.shape
-    spans, span = blocks // 2, 2 * BLK
-    vmem = pl.BlockSpec(memory_space=pltpu.VMEM)
-    smem = pl.BlockSpec(memory_space=pltpu.SMEM)
-    shape = jax.ShapeDtypeStruct
-    return pl.pallas_call(
-        attention_kernel,
-        out_shape=(
-            shape((blocks, 4 * HD, rows), NARROW),
-            shape((blocks, rows, 4 * HD), NARROW),
-        ),
-        in_specs=[smem, smem, vmem, vmem],
-        out_specs=(vmem, vmem),
-        scratch_shapes=[
-            pltpu.VMEM((spans, 4 * HD, span), NARROW),
-            pltpu.VMEM((spans, span, HD), NARROW),
-            pltpu.VMEM((spans, span, HD), NARROW),
-            pltpu.VMEM((spans, span, HD), NARROW),
-            pltpu.VMEM((spans, span, HD), NARROW),
-            pltpu.VMEM((spans, span, span), WIDE),
-            pltpu.VMEM((spans, span, span), NARROW),
-            pltpu.VMEM((HD, span), WIDE),
-            pltpu.VMEM((HD, span), WIDE),
-            pltpu.VMEM((spans, span, HD), WIDE),
-            pltpu.VMEM((spans, span, HD), WIDE),
-            pltpu.VMEM((spans, 16, span), WIDE),
-            pltpu.SMEM((blocks,), jnp.int32),
-        ],
-        name="head_attention",
-        compiler_params=pltpu.CompilerParams(vmem_limit_bytes=VMEM_LIMIT),
-    )(lengths, dealing, heads, turn)
-
-
-def far_first(depth):
-    return [list(reversed(row)) for row in near_first(depth)]
-
-
 def reduce_kernel(
     depth,
-    tokens_in,
-    turned_in,
+    lengths_ref,
+    dealing_ref,
+    heads_in,
     units_in,
+    attended_in,
+    total_in,
     tok_ref,
     cot_ref,
     prm_all,
@@ -1008,12 +983,20 @@
     up_ref,
     down_ref,
     vec_ref,
-    w_heads_out,
     w_heads_back,
     give_buf,
     sum_buf,
     beside_buf,
     line_buf,
+    wide,
+    q_rows,
+    k_rows,
+    v_rows,
+    g_rows,
+    g_key,
+    g_value,
+    turned_all,
+    by_token,
     stream,
     g_heads,
     g_wout,
@@ -1025,6 +1008,7 @@
     inbox,
     wout_in,
     down_in,
+    found,
     send_sem,
     recv_twin,
     recv_beside,
@@ -1039,7 +1023,10 @@
     c, x, y, z, core = here.c, here.x, here.y, here.z, here.core
     rows = tok_ref.shape[0]
     units = wup_all.shape[1]
+    groups = dealing_ref.shape[0]
     count = 4 * depth
+    spans, span = count // 2, 2 * BLK
+    scale = HD ** (-0.5)
     piece = D // (2 * count)
     order = far_first(depth)
 
@@ -1056,8 +1043,6 @@
             pltpu.make_async_copy(cot_in.at[shard], stream.at[1, slot], stream_sem.at[1, slot]),
         )
 
-    for copy in load(0):
-        copy.start()
     here.greet_all()
 
     def crossing(source, place, at):
@@ -1077,14 +1062,157 @@
     send_grads = [crossing(grads.at[part, 1 - x], grads_in.at[part], 2 + part) for part in range(2)]
     send_down.start()
 
-    w_heads_out[0:HD, :] = wout_part[...]
-    w_heads_out[HD:, :] = jnp.zeros((3 * HD, D), NARROW)
-    w_heads_back[0:HD, :] = jnp.zeros((HD, D), NARROW)
-    w_heads_back[HD:, :] = wqkv_t[...]
-    g_heads[...] = jnp.zeros_like(g_heads)
-    g_wout[...] = jnp.zeros_like(g_wout)
-    sum_heads[...] = jnp.zeros_like(sum_heads)
-    sum_units = jnp.sum(g_sum[...], axis=0, keepdims=True)
+    def to_twin(what, slot):
+        return pltpu.make_async_remote_copy(
+            give_buf.at[slot],
+            sum_buf.at[what, slot],
+            send_sem.at[what, 0, slot],
+            recv_twin.at[what, slot],
+            device_id=here.twin,
+            device_id_type=MESH,
+        )
+
+    def to_beside(what, to_z):
+        return pltpu.make_async_remote_copy(
+            sum_buf.at[what, to_z],
+            beside_buf.at[what, to_z],
+            send_sem.at[what, 1, to_z],
+            recv_beside.at[what, to_z],
+            device_id=here.beside,
+            device_id_type=MESH,
+        )
+
+    def to_above(what, to_z):
+        return pltpu.make_async_remote_copy(
+            sum_buf.at[what, depth + to_z],
+            line_buf.at[what, to_z],
+            send_sem.at[what, 2, to_z],
+            recv_z.at[what, to_z],
+            device_id=here.above,
+            device_id_type=MESH,
+        )
+
+    def over_slot(to_z, at_z):
+        return jnp.where(to_z == at_z, depth, to_z)
+
+    def to_below(what, to_z):
+        slot = over_slot(to_z, z - 1)
+        return pltpu.make_async_remote_copy(
+            sum_buf.at[what, depth + to_z],
+            line_buf.at[what, slot],
+            send_sem.at[what, 2, to_z],
+            recv_z.at[what, slot],
+            device_id=here.below,
+            device_id_type=MESH,
+        )
+
+    def from_above(what, to_z):
+        slot = over_slot(to_z, z)
+        return pltpu.make_async_remote_copy(
+            sum_buf.at[what, depth + to_z],
+            line_buf.at[what, slot],
+            send_sem.at[what, 2, to_z],
+            recv_z.at[what, slot],
+            device_id=here.above,
+            device_id_type=MESH,
+        )
+
+    def pass_on(what, at, part):
+        to_z = pick2(z, at // 4, order)
+        kind = lax.rem(at, 4)
+        slot = lax.rem(kind, 2) * depth + to_z
+
+        @pl.when(kind < 2)
+        def _():
+            if what == 1:
+                to_twin(0, slot).wait_send()
+            give_buf[slot] = part.astype(NARROW)
+            to_twin(what, slot).start()
+
+        @pl.when(kind >= 2)
+        def _():
+            to_twin(what, slot).wait_recv()
+            sum_buf[what, slot] = (part + sum_buf[what, slot].astype(WIDE)).astype(NARROW)
+
+        @pl.when(kind == 2)
+        def _():
+            to_beside(what, to_z).start()
+
+    def chain(what, at):
+        to_z = pick2(z, at, order)
+        slot = depth + to_z
+        to_beside(what, to_z).wait_recv()
+
+        def add(incoming):
+            for part in range(2):
+                half = slice(part * rows // 2, (part + 1) * rows // 2)
+                total = sum_buf[what, slot, half, :].astype(WIDE)
+                total = total + beside_buf[what, to_z, half, :].astype(WIDE)
+                if incoming:
+                    total = total + line_buf[what, to_z, half, :].astype(WIDE)
+                sum_buf[what, slot, half, :] = total.astype(NARROW)
+
+        @pl.when(to_z > z)
+        def _():
+            @pl.when(here.has_below)
+            def _():
+                to_above(what, to_z).wait_recv()
+                add(True)
+
+            @pl.when(jnp.logical_not(here.has_below))
+            def _():
+                add(False)
+
+            to_above(what, to_z).start()
+
+        @pl.when(to_z < z)
+        def _():
+            @pl.when(here.has_above)
+            def _():
+                from_above(what, to_z).wait_recv()
+                add(True)
+
+            @pl.when(jnp.logical_not(here.has_above))
+            def _():
+                add(False)
+
+            to_below(what, to_z).start()
+
+    def gather_total(what):
+        @pl.when(here.has_below)
+        def _():
+            to_above(what, z).wait_recv()
+
+        @pl.when(jnp.logical_not(here.has_below))
+        def _():
+            line_buf[what, z] = jnp.zeros((rows, D), NARROW)
+
+        @pl.when(here.has_above)
+        def _():
+            from_above(what, z).wait_recv()
+
+        @pl.when(jnp.logical_not(here.has_above))
+        def _():
+            line_buf[what, depth] = jnp.zeros((rows, D), NARROW)
+
+        return (
+            sum_buf[what, depth + z].astype(WIDE)
+            + beside_buf[what, z].astype(WIDE)
+            + line_buf[what, z].astype(WIDE)
+            + line_buf[what, depth].astype(WIDE)
+        )
+
+    def give_out(at, carry):
+        shard = shard_of(at)
+        parts = []
+        for group in range(groups):
+            attended = attended_in[group, dealing_ref[group, shard]].astype(NARROW)
+            parts.append(dot(attended, wout_part[...], TN))
+        part = jnp.concatenate(parts, axis=0) + dot(units_in[shard, :, 0:units], wdown_part[...])
+        pass_on(0, at, part)
+        return carry
+
+    lax.fori_loop(0, count, give_out, 0)
 
     def settle(chunk, part, raw, weights, sums, column):
         scaled = raw * column[:, 2 - 2 * part : 3 - 2 * part] + sums * column[:, 3 - 2 * part : 4 - 2 * part]
@@ -1104,6 +1232,8 @@
         for at in range(per):
             grads[part, at % 2, chunk * (per // 2) + at // 2] = scaled[at * piece : (at + 1) * piece]
 
+    sum_units = jnp.sum(g_sum[...], axis=0, keepdims=True)
+
     def settle_up(chunk, carry):
         lanes = pl.ds(pl.multiple_of(chunk * 128, 128), 128)
         weights = wup_all[lanes, :].astype(WIDE)
@@ -1112,16 +1242,102 @@
 
     lax.fori_loop(0, D // 128, settle_up, 0)
     send_grads[0].start()
-
-    def partial(at):
+    find_blocks(dealing_ref, found)
+    w_heads_back[0:HD, :] = jnp.zeros((HD, D), NARROW)
+    w_heads_back[HD:, :] = wqkv_t[...]
+    g_heads[...] = jnp.zeros_like(g_heads)
+    g_wout[...] = jnp.zeros_like(g_wout)
+    sum_heads[...] = jnp.zeros_like(sum_heads)
+
+    for group in range(groups):
+        lanes = slice(group * BLK, (group + 1) * BLK)
+        starts = starts_of(lengths_ref, group)
+
+        def bring(at, carry, group=group, lanes=lanes):
+            for side in range(2):
+                source = found[group, 2 * at + side]
+                part = heads_in[source, :, lanes]
+                to = slice(side * BLK, (side + 1) * BLK)
+                queries = part[0:HD].astype(WIDE) * scale
+                keys = part[HD : 2 * HD]
+                grads_part = part[3 * HD : 4 * HD]
+                wide[at, 0:HD, to] = queries.astype(NARROW)
+                wide[at, HD : 2 * HD, to] = keys
+                wide[at, 2 * HD : 3 * HD, to] = grads_part
+                q_rows[at, to, :] = queries.T.astype(NARROW)
+                k_rows[at, to, :] = keys.astype(WIDE).T.astype(NARROW)
+                v_rows[at, to, :] = part[2 * HD : 3 * HD].astype(WIDE).T.astype(NARROW)
+                g_rows[at, to, :] = grads_part.astype(WIDE).T.astype(NARROW)
+            g_key[at] = jnp.zeros((span, HD), WIDE)
+            g_value[at] = jnp.zeros((span, HD), WIDE)
+            return carry
+
+        lax.fori_loop(0, spans, bring, 0)
+        chain(0, 2 * group)
+
+        def one_span(at, carry, group=group, starts=starts):
+            natural = at * span + lax.broadcasted_iota(jnp.int32, (1, span), 1)
+            opening = opening_of(natural, starts)
+            key_in = lax.broadcasted_iota(jnp.int32, (span, span), 0)
+            queries = wide[at, 0:HD, :]
+            g_attended = wide[at, 2 * HD : 3 * HD, :]
+            attended = jnp.concatenate(
+                [attended_in[group, 2 * at], attended_in[group, 2 * at + 1]], axis=1
+            )
+            row_dot = jnp.sum(attended * g_attended.astype(WIDE), axis=0, keepdims=True)
+            log_total = total_in[group, at, 0:1, :]
+
+            def add(keys_at, so_far, allowed):
+                scores = dot(k_rows[keys_at], queries)
+                probs = jnp.where(allowed, jnp.exp(scores - log_total), 0.0)
+                g_probs = dot(v_rows[keys_at], g_attended)
+                g_scores = (probs * (g_probs - row_dot)).astype(NARROW)
+                g_key[keys_at] += dot(g_scores, q_rows[at])
+                g_value[keys_at] += dot(probs.astype(NARROW), g_rows[at])
+                return so_far + dot(wide[keys_at, HD : 2 * HD, :], g_scores)
+
+            def earlier(keys_at, so_far):
+                return add(keys_at, so_far, key_in >= opening - keys_at * span)
+
+            so_far = lax.fori_loop(0, at, earlier, jnp.zeros((HD, span), WIDE))
+            place = key_in + at * span
+            so_far = add(at, so_far, jnp.logical_and(place <= natural, place >= opening))
+            cosine, sine = turning(natural - opening)
+            turned = jnp.concatenate([attended, unturn(so_far * scale, cosine, sine)], axis=0)
+            for side in range(2):
+                part = turned[:, side * BLK : (side + 1) * BLK]
+                turned_all[group, 2 * at + side, 0 : 2 * HD, :] = part.astype(NARROW)
+            return carry
+
+        lax.fori_loop(0, spans, one_span, 0)
+        chain(0, 2 * group + 1)
+
+        def give(at, carry, group=group, starts=starts):
+            natural = at * span + lax.broadcasted_iota(jnp.int32, (1, span), 1)
+            cosine, sine = turning(natural - opening_of(natural, starts))
+            keys = unturn(g_key[at].T, cosine, sine)
+            turned = jnp.concatenate([keys, g_value[at].T], axis=0)
+            for side in range(2):
+                part = turned[:, side * BLK : (side + 1) * BLK]
+                turned_all[group, 2 * at + side, 2 * HD : 4 * HD, :] = part.astype(NARROW)
+                whole = turned_all[group, 2 * at + side].astype(WIDE)
+                by_token[group, 2 * at + side] = whole.T.astype(NARROW)
+            return carry
+
+        lax.fori_loop(0, spans, give, 0)
+
+    for copy in load(0):
+        copy.start()
+
+    def give_back(at, carry):
         shard, slot = shard_of(at), lax.rem(at, 2)
-        heads = tokens_in[shard]
-        activated = units_in[shard, :, 0:units]
+        blocks = [dealing_ref[group, shard] for group in range(groups)]
+        heads = jnp.concatenate([by_token[group, blocks[group]] for group in range(groups)], axis=0)
         g_hidden = units_in[shard, :, units : 2 * units]
-        part_out = dot(heads, w_heads_out[...]) + dot(activated, wdown_part[...])
-        part_back = dot(heads, w_heads_back[...]) * prm_all[0:1, :] + dot(
+        part = dot(heads, w_heads_back[...]) * prm_all[0:1, :] + dot(
             g_hidden, wup_all[...], NT
         ) * prm_all[2:3, :]
+        pass_on(1, at, part)
 
         @pl.when(at + 1 < count)
         def _():
@@ -1130,95 +1346,13 @@
 
         for copy in load(at):
             copy.wait()
-        g_wout[...] += dot(turned_in[shard, 0:HD, :], stream[1, slot])
-        g_heads[HD:, :] += dot(turned_in[shard, HD:, :], stream[0, slot])
+        turned = jnp.concatenate([turned_all[group, blocks[group]] for group in range(groups)], axis=1)
+        g_wout[...] += dot(turned[0:HD], stream[1, slot])
+        g_heads[HD:, :] += dot(turned[HD:], stream[0, slot])
         sum_heads[...] += jnp.sum(heads.astype(WIDE).reshape(rows // 8, 8, 4 * HD), axis=0)
-        return part_out, part_back
-
-    def to_twin(slot):
-        return pltpu.make_async_remote_copy(
-            give_buf.at[slot],
-            sum_buf.at[slot],
-            send_sem.at[0, slot],
-            recv_twin.at[slot],
-            device_id=here.twin,
-            device_id_type=MESH,
-        )
-
-    def to_beside(to_z):
-        return pltpu.make_async_remote_copy(
-            sum_buf.at[to_z],
-            beside_buf.at[to_z],
-            send_sem.at[1, to_z],
-            recv_beside.at[to_z],
-            device_id=here.beside,
-            device_id_type=MESH,
-        )
-
-    def to_above(to_z):
-        return pltpu.make_async_remote_copy(
-            sum_buf.at[depth + to_z],
-            line_buf.at[to_z],
-            send_sem.at[2, to_z],
-            recv_z.at[to_z],
-            device_id=here.above,
-            device_id_type=MESH,
-        )
-
-    def over_slot(to_z, at_z):
-        return jnp.where(to_z == at_z, depth, to_z)
-
-    def to_below(to_z):
-        return pltpu.make_async_remote_copy(
-            sum_buf.at[depth + to_z],
-            line_buf.at[over_slot(to_z, z - 1)],
-            send_sem.at[2, to_z],
-            recv_z.at[over_slot(to_z, z - 1)],
-            device_id=here.below,
-            device_id_type=MESH,
-        )
-
-    def from_above(to_z):
-        slot = over_slot(to_z, z)
-        return pltpu.make_async_remote_copy(
-            sum_buf.at[depth + to_z],
-            line_buf.at[slot],
-            send_sem.at[2, to_z],
-            recv_z.at[slot],
-            device_id=here.above,
-            device_id_type=MESH,
-        )
-
-    def produce(at, carry):
-        to_z = pick2(z, at // 4, order)
-        kind = lax.rem(at, 4)
-        home = lax.rem(kind, 2)
-        slot = home * depth + to_z
-        part_out, part_back = partial(at)
-
-        @pl.when(kind < 2)
-        def _():
-            give_buf[slot, 0:rows, :] = part_out.astype(NARROW)
-            give_buf[slot, rows : 2 * rows, :] = part_back.astype(NARROW)
-            to_twin(slot).start()
-
-        @pl.when(kind >= 2)
-        def _():
-            to_twin(slot).wait_recv()
-            sum_buf[slot, 0:rows, :] = (
-                part_out + sum_buf[slot, 0:rows, :].astype(WIDE)
-            ).astype(NARROW)
-            sum_buf[slot, rows : 2 * rows, :] = (
-                part_back + sum_buf[slot, rows : 2 * rows, :].astype(WIDE)
-            ).astype(NARROW)
-
-        @pl.when(kind == 2)
-        def _():
-            to_beside(to_z).start()
-
         return carry
 
-    lax.fori_loop(0, 4 * depth, produce, 0)
+    lax.fori_loop(0, count, give_back, 0)
     send_wout.start()
     sum_row = jnp.sum(sum_heads[...], axis=0, keepdims=True)
 
@@ -1268,105 +1402,16 @@
         inbox[part, c] = mail[part, c]
 
     mail_out(0)
-
-    def chain(at, carry):
-        to_z = pick2(z, at, order)
-        slot = depth + to_z
-        to_beside(to_z).wait_recv()
-
-        def add(incoming):
-            for part in range(4):
-                span = slice(part * rows // 2, (part + 1) * rows // 2)
-                total = sum_buf[slot, span, :].astype(WIDE) + beside_buf[to_z, span, :].astype(WIDE)
-                if incoming:
-                    total = total + line_buf[to_z, span, :].astype(WIDE)
-                sum_buf[slot, span, :] = total.astype(NARROW)
-
-        @pl.when(to_z > z)
-        def _():
-            @pl.when(here.has_below)
-            def _():
-                to_above(to_z).wait_recv()
-                add(True)
-
-            @pl.when(jnp.logical_not(here.has_below))
-            def _():
-                add(False)
-
-            to_above(to_z).start()
-
-        @pl.when(to_z < z)
-        def _():
-            @pl.when(here.has_above)
-            def _():
-                from_above(to_z).wait_recv()
-                add(True)
-
-            @pl.when(jnp.logical_not(here.has_above))
-            def _():
-                add(False)
-
-            to_below(to_z).start()
-
+    chain(1, 0)
+    mail_out(1)
+
+    def rest(at, carry):
+        chain(1, at)
         return carry
 
-    lax.fori_loop(0, 1, chain, 0)
-    mail_out(1)
-    lax.fori_loop(1, depth, chain, 0)
-
-    @pl.when(here.has_below)
-    def _():
-        to_above(z).wait_recv()
-
-    @pl.when(jnp.logical_not(here.has_below))
-    def _():
-        line_buf[z] = jnp.zeros((2 * rows, D), NARROW)
-
-    @pl.when(here.has_above)
-    def _():
-        from_above(z).wait_recv()
-
-    @pl.when(jnp.logical_not(here.has_above))
-    def _():
-        line_buf[depth] = jnp.zeros((2 * rows, D), NARROW)
-
-    def total(span):
-        return (
-            sum_buf[depth + z, span, :].astype(WIDE)
-            + beside_buf[z, span, :].astype(WIDE)
-            + line_buf[z, span, :].astype(WIDE)
-            + line_buf[depth, span, :].astype(WIDE)
-        )
-
-    tokens = tok_ref[...].astype(WIDE)
-    out_ref[...] = (tokens + total(slice(0, rows))).astype(NARROW)
-    average = jnp.mean(tokens, axis=-1, keepdims=True)
-    centred = tokens - average
-    variance = jnp.mean(centred * centred, axis=-1, keepdims=True)
-    rise = lax.rsqrt(variance + EPSILON)
-    xhat = centred * rise
-    g_xhat = total(slice(rows, 2 * rows))
-    along = jnp.mean(g_xhat * xhat, axis=-1, keepdims=True)
-    level = jnp.mean(g_xhat, axis=-1, keepdims=True)
-    grad_ref[...] = cot_ref[...].astype(WIDE) + rise * (g_xhat - level - xhat * along)
-
-    def finish(to_z, carry):
-        to_twin(to_z).wait_send()
-        to_twin(depth + to_z).wait_send()
-        to_beside(to_z).wait_send()
-
-        @pl.when(to_z > z)
-        def _():
-            to_above(to_z).wait_send()
-
-        @pl.when(to_z < z)
-        def _():
-            to_below(to_z).wait_send()
-
-        return carry
-
-    lax.fori_loop(0, depth, finish, 0)
-
+    lax.fori_loop(1, depth, rest, 0)
+
+    out_ref[...] = (tok_ref[...].astype(WIDE) + gather_total(0)).astype(NARROW)
     send_down.wait()
     down_ref[...] = g_down[pl.ds(x * half_down, half_down), :] + down_in[...]
     send_wout.wait()
@@ -1395,16 +1440,49 @@
             to = part * D + pair * 128
             qkv_ref[:, to : to + 128] = jnp.concatenate([left[:, lanes], right[:, lanes]], axis=1)
 
-
-def reduce_call(depth, tokens_in, turned_in, units_in, tok, cot, rest, xhat, cot_all):
+    tokens = tok_ref[...].astype(WIDE)
+    average = jnp.mean(tokens, axis=-1, keepdims=True)
+    centred = tokens - average
+    variance = jnp.mean(centred * centred, axis=-1, keepdims=True)
+    rise = lax.rsqrt(variance + EPSILON)
+    xhat = centred * rise
+    g_xhat = gather_total(1)
+    along = jnp.mean(g_xhat * xhat, axis=-1, keepdims=True)
+    level = jnp.mean(g_xhat, axis=-1, keepdims=True)
+    grad_ref[...] = cot_ref[...].astype(WIDE) + rise * (g_xhat - level - xhat * along)
+
+    def finish(to_z, carry):
+        to_twin(1, to_z).wait_send()
+        to_twin(1, depth + to_z).wait_send()
+        for what in range(2):
+            to_beside(what, to_z).wait_send()
+
+            @pl.when(to_z > z)
+            def _():
+                to_above(what, to_z).wait_send()
+
+            @pl.when(to_z < z)
+            def _():
+                to_below(what, to_z).wait_send()
+
+        return carry
+
+    lax.fori_loop(0, depth, finish, 0)
+
+
+def reduce_call(depth, lengths, dealing, heads, units_in, attended, total, tok, cot, rest, xhat, cot_all):
     rows = tok.shape[0]
     count = depth * 4
+    groups = dealing.shape[0]
+    spans, span = count // 2, 2 * BLK
     piece = D // (2 * count)
     units = rest[2].shape[1]
     vmem = pl.BlockSpec(memory_space=pltpu.VMEM)
+    smem = pl.BlockSpec(memory_space=pltpu.SMEM)
     any_spec = pl.BlockSpec(memory_space=pl.ANY)
     shape = jax.ShapeDtypeStruct
-    message = (2 * rows, D)
+    message = (rows, D)
+    row_form = pltpu.VMEM((spans, span, HD), NARROW)
     return pl.pallas_call(
         functools.partial(reduce_kernel, depth),
         out_shape=(
@@ -1416,15 +1494,23 @@
             shape((units // 2, D), WIDE),
             shape((8, piece), WIDE),
         ),
-        in_specs=[vmem] * 13 + [any_spec] * 2,
+        in_specs=[smem] * 2 + [vmem] * 14 + [any_spec] * 2,
         out_specs=(vmem,) * 7,
         scratch_shapes=[
             pltpu.VMEM((4 * HD, D), NARROW),
-            pltpu.VMEM((4 * HD, D), NARROW),
             pltpu.VMEM((2 * depth,) + message, NARROW),
-            pltpu.VMEM((2 * depth,) + message, NARROW),
-            pltpu.VMEM((depth,) + message, NARROW),
-            pltpu.VMEM((depth + 1,) + message, NARROW),
+            pltpu.VMEM((2, 2 * depth) + message, NARROW),
+            pltpu.VMEM((2, depth) + message, NARROW),
+            pltpu.VMEM((2, depth + 1) + message, NARROW),
+            pltpu.VMEM((spans, 3 * HD, span), NARROW),
+            row_form,
+            row_form,
+            row_form,
+            row_form,
+            pltpu.VMEM((spans, span, HD), WIDE),
+            pltpu.VMEM((spans, span, HD), WIDE),
+            pltpu.VMEM((groups, count, 4 * HD, BLK), NARROW),
+            pltpu.VMEM((groups, count, BLK, 4 * HD), NARROW),
             pltpu.VMEM((2, 2, rows, D), NARROW),
             pltpu.VMEM((4 * HD, D), WIDE),
             pltpu.VMEM((HD, D), WIDE),
@@ -1436,51 +1522,36 @@
             pltpu.VMEM((2, count, piece, 256), NARROW),
             pltpu.VMEM((HD // 2, D), WIDE),
             pltpu.VMEM((units // 2, D), WIDE),
-            pltpu.SemaphoreType.DMA((3, 2 * depth)),
-            pltpu.SemaphoreType.DMA((2 * depth,)),
-            pltpu.SemaphoreType.DMA((depth,)),
-            pltpu.SemaphoreType.DMA((depth + 1,)),
+            pltpu.SMEM((groups, count), jnp.int32),
+            pltpu.SemaphoreType.DMA((2, 3, 2 * depth)),
+            pltpu.SemaphoreType.DMA((2, 2 * depth)),
+            pltpu.SemaphoreType.DMA((2, depth)),
+            pltpu.SemaphoreType.DMA((2, depth + 1)),
             pltpu.SemaphoreType.DMA((2, 2)),
             pltpu.SemaphoreType.DMA((4,)),
             pltpu.SemaphoreType.DMA((4,)),
             pltpu.SemaphoreType.DMA((2, count)),
             pltpu.SemaphoreType.DMA((2, count)),
         ],
-        name="reduce_rows",
+        name="backward_and_reduce",
         compiler_params=pltpu.CompilerParams(
             collective_id=2, has_side_effects=True, vmem_limit_bytes=VMEM_LIMIT
         ),
-    )(tokens_in, turned_in, units_in, tok, cot, *rest, xhat, cot_all)
+    )(lengths, dealing, heads, units_in, attended, total, tok, cot, *rest, xhat, cot_all)
 
 
 def fast_shards(depth, *arguments):
-    (tokens, cotangent, lengths, dealing, gain_one, bias_one, gain_two, bias_two) = arguments[:8]
-    w_qkv, w_out, w_up, w_down = arguments[8:]
-    groups, local_rows, _ = tokens.shape
-    rows = groups * local_rows
-    count = depth * 4
+    tokens, cotangent, lengths, dealing = arguments[:4]
+    gains = [vector.reshape(1, -1) for vector in arguments[4:8]]
+    rows = tokens.shape[0] * tokens.shape[1]
     tok = tokens.reshape(rows, D)
     cot = cotangent.reshape(rows, D)
-    prm = jnp.stack([gain_one, bias_one, gain_two, bias_two] * 2).astype(WIDE)
-
-    openings = jnp.cumsum(lengths, axis=1) - lengths
-    natural = (dealing.T[:, :, None] * BLK + jnp.arange(BLK, dtype=jnp.int32)[None, None, :]).reshape(
-        count, rows
-    )
-    start_rows = jnp.repeat(openings.T, BLK, axis=1)[:, None, :]
-    opening = jnp.max(jnp.where(start_rows <= natural[None], start_rows, 0), axis=0)
-    place = (natural - opening).astype(WIDE)
-    frequency = 10000.0 ** (-2.0 * jnp.arange(ROT // 2, dtype=WIDE) / ROT)
-    angles = place[:, None, :] * frequency[None, :, None]
-    turn = jnp.concatenate([jnp.cos(angles), jnp.sin(angles)], axis=1)
-
-    (heads, units, xhat, cot_all, g_up, g_down, g_sum, wqkv_t, wup_all, wdown_part, wout_part, prm_all) = (
-        gather_call(depth, tok, cot, prm, turn, w_qkv, w_out, w_up, w_down)
-    )
-    turned, by_token = attention_call(lengths, dealing, heads, turn)
+    forward = gather_call(depth, lengths, dealing, tok, cot, gains, *arguments[8:])
+    heads, units, xhat, cot_all, attended, total, g_up, g_down, g_sum = forward[:9]
+    wqkv_t, wup_all, wdown_part, wout_part, prm_all = forward[9:]
     rest = (prm_all, wqkv_t, wup_all, wdown_part, wout_part, g_up, g_down, g_sum)
     out, grad_tokens, qkv_part, out_part, up_part, down_part, vector_part = reduce_call(
-        depth, by_token, turned, units, tok, cot, rest, xhat, cot_all
+        depth, lengths, dealing, heads, units, attended, total, tok, cot, rest, xhat, cot_all
     )
     return (
         out.reshape(tokens.shape),

time: 320 us -> 291 us (0.909)
  Pallas kernels: 302 us -> 274 us
  other arithmetic: 4.13 us -> 0 us
    pallas_call x1 -> x0, Pallas kernels: 58.2 us -> none  [attention_call(): pl.pallas_call(attention_kernel, out_shape=(shape((blocks, 4 * HD, rows),...]
    pallas_call x1, Pallas kernels: 121 us -> 137 us  [reduce_call(): pl.pallas_call(functools.partial(reduce_kernel, depth), out_shape=(shape(...]
    pallas_call x1, Pallas kernels: 122 us -> 137 us  [gather_call(): pl.pallas_call(functools.partial(gather_kernel, depth), out_shape=(shape(...]
    reshape x0 -> x4, local copies, waits for them, and re-layouts: none -> 5.04 us  [fast_shards(): gains = [vector.reshape(1, -1) for vector in arguments[4:8]]]
    unnamed x12 -> x10, local copies, waits for them, and re-layouts: 9.18 us -> 9.1 us
where the time goes in v3:
time: 291 us
  Pallas kernels  274 us (94%)
  local copies, waits for them, and re-layouts  15.5 us (5%)
    pallas_call x1, Pallas kernels, gather_call(): pl.pallas_call(functools.partial(gather_kernel, depth), out_shape=(shape(...  137 us
    pallas_call x1, Pallas kernels, reduce_call(): pl.pallas_call(functools.partial(reduce_kernel, depth), out_shape=(shape(...  137 us
    unnamed x10, local copies, waits for them, and re-layouts  9.1 us

profile of v3, /device:TPU:0, one launch (start us, length us, event | category | flops | bytes accessed | tf_op | source)
XLA Modules:
  0.0 290.7 jit_solution(6894229708224644577)
XLA Ops:
  0.6 1.3 reshape.46.gain_one_ref
  1.9 1.3 reshape.47.bias_one_ref
  3.2 1.3 reshape.48.gain_two_ref
  4.4 1.3 reshape.49.bias_two_ref
  5.7 137.5 %gather_and_forward.1 = (bf16[16,256,256]{2,1,0:T(8,128)(2,1)}, bf16[16,256,512]{2,1,0:T(8,128)(2,1)}, bf16[16,256,1024]{2,1,0:T(8,128)(2,1)}, bf16[16,256,1024]...) custom-call(s32[2,4]{1,0:T(2,128)} %lengths_ref.3, ...), custom_call_target="tpu_custom_call" | custom-call | tf_op jit(solution)/shard_map/gather_and_forward/pallas_call | solution.py:902
  143.1 137.0 %backward_and_reduce.1 = (bf16[256,1024]{1,0:T(8,128)(2,1)}, f32[256,1024]{1,0:T(8,128)}, f32[32,3072]{1,0:T(8,128)}, f32[32,1024]{1,0:T(8,128)}, f32[32,4096]{1...) custom-call(s32[2,4]{1,0:T(2,128)} %lengths_ref.3, s32[2,16]{1,0:T(2,128)} %dealing_ref.3, ...), custom_call_target="tpu_custom_call" | custom-call | tf_op jit(solution)/shard_map/backward_and_reduce/pallas_call | solution.py:1486
  280.2 0.0 copy-start.1
  280.2 0.0 copy-start
  280.2 1.4 slice_bitcast_fusion
  281.6 1.9 copy.28
  283.4 2.3 copy.29
  285.7 1.8 copy.30
  287.5 1.6 copy.31
  289.1 0.0 copy-done.1
  289.1 0.8 copy.32
  289.9 0.0 copy-done
  289.9 0.8 copy.33
Async XLA Ops:
  280.2 8.9 %copy-start.1 = (f32[32,4096]{1,0:T(8,128)S(1)}, f32[32,4096]{1,0:T(8,128)}, u32[]{:S(2)}) copy-start(f32[32,4096]{1,0:T(8,128)} %get-tuple-element.74) | copy-start | bytes 1572868
  280.2 9.7 %copy-start = (f32[128,1024]{1,0:T(8,128)S(1)}, f32[128,1024]{1,0:T(8,128)}, u32[]{:S(2)}) copy-start(f32[128,1024]{1,0:T(8,128)} %get-tuple-element.75) | copy-start | bytes 1572868

commit v4 on v3

--- a/solution.py
+++ b/solution.py
@@ -570,7 +570,7 @@
     for copy in own_in:
         copy.start()
     prm_rows = [
-        ref[...].astype(WIDE) for ref in (gain_one_ref, bias_one_ref, gain_two_ref, bias_two_ref)
+        ref[...].astype(WIDE).reshape(1, half) for ref in (gain_one_ref, bias_one_ref, gain_two_ref, bias_two_ref)
     ]
     prm_buf[x] = jnp.concatenate(prm_rows + prm_rows, axis=0)
 
@@ -622,11 +622,6 @@
     for at, (source, place) in enumerate(shared):
         remote(source, place, at).start()
 
-    @pl.when(is_owner)
-    def _():
-        for at, (source, place) in enumerate(held):
-            remote(source, place, 5 + at).start()
-
     def passing(what, shard, way):
         device = (here.beside, here.twin, here.above, here.below)[way]
         return pltpu.make_async_remote_copy(
@@ -654,6 +649,7 @@
     own_in[0].wait()
     onward(0, c, z)
     own_in[1].wait()
+    onward(1, c, z)
     find_blocks(dealing_ref, found)
 
     for at, (source, place) in enumerate(shared):
@@ -664,12 +660,7 @@
     @pl.when(is_owner)
     def _():
         for at, (source, place) in enumerate(held):
-            pltpu.make_async_copy(source, place, w_sem.at[5 + at]).wait()
-
-    @pl.when(jnp.logical_not(is_owner))
-    def _():
-        for at, (source, place) in enumerate(held):
-            remote(source, place, 5 + at).wait_recv()
+            remote(source, place, 5 + at).start()
 
     odd = lax.rem(c, 2) == 1
     for side in range(2):
@@ -783,12 +774,17 @@
 
         lax.fori_loop(0, 4 * depth + 4, step, 0)
 
-    def cotangent_too(at):
-        @pl.when(at == 4 * (depth - 1) + 1)
-        def _():
-            onward(1, c, z)
-
-    sweep(0, ahead, cotangent_too)
+    sweep(0, ahead, lambda at: None)
+
+    @pl.when(is_owner)
+    def _():
+        for at, (source, place) in enumerate(held):
+            pltpu.make_async_copy(source, place, w_sem.at[5 + at]).wait()
+
+    @pl.when(jnp.logical_not(is_owner))
+    def _():
+        for at, (source, place) in enumerate(held):
+            remote(source, place, 5 + at).wait_recv()
 
     spans = count // 2
     span = 2 * BLK
@@ -814,17 +810,20 @@
         mine = jnp.where(lax.rem(turn_no, 2) == 0, spans - 1 - turn_no // 2, turn_no // 2)
         natural = mine * span + lax.broadcasted_iota(jnp.int32, (1, span), 1)
         opening = opening_of(natural, [jnp.where(group == 0, *pair) for pair in zip(*openings)])
-        key_in = lax.broadcasted_iota(jnp.int32, (span, span), 0)
+        key_in = lax.broadcasted_iota(jnp.int32, (2 * span, span), 0)
         queries = wide[group, mine, 0:HD, :]
 
         def add(keys_at, state, allowed):
             top, total, so_far = state
-            raw = jnp.where(allowed, dot(k_rows[group, keys_at], queries), MASKED)
+            keys = k_rows[group, pl.ds(2 * keys_at, 2)].reshape(2 * span, HD)
+            raw = jnp.where(allowed, dot(keys, queries), MASKED)
             new_top = jnp.maximum(top, jnp.max(raw, axis=0, keepdims=True))
             risen = jnp.exp(raw - new_top)
             fade = jnp.exp(top - new_top)
             total = total * fade + jnp.sum(risen, axis=0, keepdims=True)
-            values = wide[group, keys_at, HD : 2 * HD, :]
+            values = jnp.concatenate(
+                [wide[group, 2 * keys_at + side, HD : 2 * HD, :] for side in range(2)], axis=1
+            )
             return new_top, total, so_far * fade + dot(values, risen.astype(NARROW))
 
         state = (
@@ -832,14 +831,15 @@
             jnp.zeros((1, span), WIDE),
             jnp.zeros((HD, span), WIDE),
         )
-        place = key_in + mine * span
-        state = add(mine, state, jnp.logical_and(place <= natural, place >= opening))
+        last = mine // 2
+        place = key_in + last * (2 * span)
+        state = add(last, state, jnp.logical_and(place <= natural, place >= opening))
 
         def earlier(back, state):
-            keys_at = mine - 1 - back
-            return add(keys_at, state, key_in >= opening - keys_at * span)
-
-        top, total, so_far = lax.fori_loop(0, mine, earlier, state)
+            keys_at = last - 1 - back
+            return add(keys_at, state, key_in >= opening - keys_at * (2 * span))
+
+        top, total, so_far = lax.fori_loop(0, last, earlier, state)
         attended = so_far / total
         for side in range(2):
             attended_out[group, 2 * mine + side] = attended[:, side * BLK : (side + 1) * BLK]
@@ -960,29 +960,35 @@
     depth,
     lengths_ref,
     dealing_ref,
-    heads_in,
-    units_in,
-    attended_in,
     total_in,
-    tok_ref,
-    cot_ref,
     prm_all,
-    wqkv_t,
-    wup_all,
-    wdown_part,
-    wout_part,
-    g_up,
-    g_down,
     g_sum,
+    attended_hbm,
+    wout_hbm,
+    wdown_hbm,
+    units_hbm,
+    g_up_hbm,
+    wup_hbm,
+    wqkv_hbm,
+    g_down_hbm,
+    heads_hbm,
     xhat_in,
     cot_in,
-    out_ref,
-    grad_ref,
-    qkv_ref,
+    sum_out,
+    sum_back,
+    inbox,
     wout_ref,
-    up_ref,
     down_ref,
     vec_ref,
+    attended_in,
+    wout_part,
+    wdown_part,
+    units_in,
+    g_up,
+    wup_all,
+    wqkv_t,
+    g_down,
+    heads_in,
     w_heads_back,
     give_buf,
     sum_buf,
@@ -1005,10 +1011,10 @@
     grads,
     grads_in,
     mail,
-    inbox,
     wout_in,
     down_in,
     found,
+    first_sem,
     send_sem,
     recv_twin,
     recv_beside,
@@ -1021,10 +1027,28 @@
 ):
     here = Place(depth)
     c, x, y, z, core = here.c, here.x, here.y, here.z, here.core
-    rows = tok_ref.shape[0]
+    rows = sum_out.shape[0]
     units = wup_all.shape[1]
     groups = dealing_ref.shape[0]
     count = 4 * depth
+    brought = [
+        pltpu.make_async_copy(source, place, first_sem.at[at])
+        for at, (source, place) in enumerate(
+            (
+                (attended_hbm, attended_in),
+                (wout_hbm, wout_part),
+                (wdown_hbm, wdown_part),
+                (units_hbm, units_in),
+                (g_up_hbm, g_up),
+                (wup_hbm, wup_all),
+                (wqkv_hbm, wqkv_t),
+                (g_down_hbm, g_down),
+                (heads_hbm, heads_in),
+            )
+        )
+    ]
+    for copy in brought:
+        copy.start()
     spans, span = count // 2, 2 * BLK
     scale = HD ** (-0.5)
     piece = D // (2 * count)
@@ -1060,7 +1084,6 @@
     send_down = crossing(g_down.at[pl.ds((1 - x) * half_down, half_down)], down_in, 0)
     send_wout = crossing(g_wout.at[pl.ds((1 - x) * half_wout, half_wout)], wout_in, 1)
     send_grads = [crossing(grads.at[part, 1 - x], grads_in.at[part], 2 + part) for part in range(2)]
-    send_down.start()
 
     def to_twin(what, slot):
         return pltpu.make_async_remote_copy(
@@ -1212,7 +1235,12 @@
         pass_on(0, at, part)
         return carry
 
+    for copy in brought[:4]:
+        copy.wait()
     lax.fori_loop(0, count, give_out, 0)
+    for copy in brought[4:]:
+        copy.wait()
+    send_down.start()
 
     def settle(chunk, part, raw, weights, sums, column):
         scaled = raw * column[:, 2 - 2 * part : 3 - 2 * part] + sums * column[:, 3 - 2 * part : 4 - 2 * part]
@@ -1278,7 +1306,7 @@
         def one_span(at, carry, group=group, starts=starts):
             natural = at * span + lax.broadcasted_iota(jnp.int32, (1, span), 1)
             opening = opening_of(natural, starts)
-            key_in = lax.broadcasted_iota(jnp.int32, (span, span), 0)
+            key_in = lax.broadcasted_iota(jnp.int32, (2 * span, span), 0)
             queries = wide[at, 0:HD, :]
             g_attended = wide[at, 2 * HD : 3 * HD, :]
             attended = jnp.concatenate(
@@ -1287,21 +1315,27 @@
             row_dot = jnp.sum(attended * g_attended.astype(WIDE), axis=0, keepdims=True)
             log_total = total_in[group, at, 0:1, :]
 
-            def add(keys_at, so_far, allowed):
-                scores = dot(k_rows[keys_at], queries)
+            def add(pair, so_far, allowed):
+                two = pl.ds(2 * pair, 2)
+                keys = k_rows[two].reshape(2 * span, HD)
+                values = v_rows[two].reshape(2 * span, HD)
+                scores = dot(keys, queries)
                 probs = jnp.where(allowed, jnp.exp(scores - log_total), 0.0)
-                g_probs = dot(v_rows[keys_at], g_attended)
-                g_scores = (probs * (g_probs - row_dot)).astype(NARROW)
-                g_key[keys_at] += dot(g_scores, q_rows[at])
-                g_value[keys_at] += dot(probs.astype(NARROW), g_rows[at])
-                return so_far + dot(wide[keys_at, HD : 2 * HD, :], g_scores)
-
-            def earlier(keys_at, so_far):
-                return add(keys_at, so_far, key_in >= opening - keys_at * span)
-
-            so_far = lax.fori_loop(0, at, earlier, jnp.zeros((HD, span), WIDE))
-            place = key_in + at * span
-            so_far = add(at, so_far, jnp.logical_and(place <= natural, place >= opening))
+                g_scores = (probs * (dot(values, g_attended) - row_dot)).astype(NARROW)
+                g_key[two] += dot(g_scores, q_rows[at]).reshape(2, span, HD)
+                g_value[two] += dot(probs.astype(NARROW), g_rows[at]).reshape(2, span, HD)
+                keys_t = jnp.concatenate(
+                    [wide[2 * pair + side, HD : 2 * HD, :] for side in range(2)], axis=1
+                )
+                return so_far + dot(keys_t, g_scores)
+
+            def earlier(pair, so_far):
+                return add(pair, so_far, key_in >= opening - pair * (2 * span))
+
+            last = at // 2
+            so_far = lax.fori_loop(0, last, earlier, jnp.zeros((HD, span), WIDE))
+            place = key_in + last * (2 * span)
+            so_far = add(last, so_far, jnp.logical_and(place <= natural, place >= opening))
             cosine, sine = turning(natural - opening)
             turned = jnp.concatenate([attended, unturn(so_far * scale, cosine, sine)], axis=0)
             for side in range(2):
@@ -1350,6 +1384,11 @@
         g_wout[...] += dot(turned[0:HD], stream[1, slot])
         g_heads[HD:, :] += dot(turned[HD:], stream[0, slot])
         sum_heads[...] += jnp.sum(heads.astype(WIDE).reshape(rows // 8, 8, 4 * HD), axis=0)
+
+        @pl.when(at == count - 4)
+        def _():
+            chain(1, 0)
+
         return carry
 
     lax.fori_loop(0, count, give_back, 0)
@@ -1402,16 +1441,16 @@
         inbox[part, c] = mail[part, c]
 
     mail_out(0)
-    chain(1, 0)
+    chain(1, 1)
     mail_out(1)
 
     def rest(at, carry):
         chain(1, at)
         return carry
 
-    lax.fori_loop(1, depth, rest, 0)
-
-    out_ref[...] = (tok_ref[...].astype(WIDE) + gather_total(0)).astype(NARROW)
+    lax.fori_loop(2, depth, rest, 0)
+
+    sum_out[...] = gather_total(0)
     send_down.wait()
     down_ref[...] = g_down[pl.ds(x * half_down, half_down), :] + down_in[...]
     send_wout.wait()
@@ -1429,27 +1468,9 @@
         send_grads[part].wait_send()
     together = jnp.zeros((piece, 128), WIDE)
     for from_c in range(count):
-        up_ref[:, from_c * units : (from_c + 1) * units] = inbox[0, from_c].astype(WIDE)
         together = together + inbox[1, from_c, :, 0:128].astype(WIDE)
     vec_ref[...] = together.T[0:8]
-    for pair in range(count // 2):
-        left = inbox[1, 2 * pair].astype(WIDE)
-        right = inbox[1, 2 * pair + 1].astype(WIDE)
-        for part in range(3):
-            lanes = slice((part + 1) * HD, (part + 2) * HD)
-            to = part * D + pair * 128
-            qkv_ref[:, to : to + 128] = jnp.concatenate([left[:, lanes], right[:, lanes]], axis=1)
-
-    tokens = tok_ref[...].astype(WIDE)
-    average = jnp.mean(tokens, axis=-1, keepdims=True)
-    centred = tokens - average
-    variance = jnp.mean(centred * centred, axis=-1, keepdims=True)
-    rise = lax.rsqrt(variance + EPSILON)
-    xhat = centred * rise
-    g_xhat = gather_total(1)
-    along = jnp.mean(g_xhat * xhat, axis=-1, keepdims=True)
-    level = jnp.mean(g_xhat, axis=-1, keepdims=True)
-    grad_ref[...] = cot_ref[...].astype(WIDE) + rise * (g_xhat - level - xhat * along)
+    sum_back[...] = gather_total(1)
 
     def finish(to_z, carry):
         to_twin(1, to_z).wait_send()
@@ -1470,13 +1491,12 @@
     lax.fori_loop(0, depth, finish, 0)
 
 
-def reduce_call(depth, lengths, dealing, heads, units_in, attended, total, tok, cot, rest, xhat, cot_all):
-    rows = tok.shape[0]
+def reduce_call(depth, scalars, small, large, rows):
     count = depth * 4
-    groups = dealing.shape[0]
+    groups = scalars[0].shape[0]
     spans, span = count // 2, 2 * BLK
     piece = D // (2 * count)
-    units = rest[2].shape[1]
+    units = large[5].shape[1]
     vmem = pl.BlockSpec(memory_space=pltpu.VMEM)
     smem = pl.BlockSpec(memory_space=pltpu.SMEM)
     any_spec = pl.BlockSpec(memory_space=pl.ANY)
@@ -1486,17 +1506,17 @@
     return pl.pallas_call(
         functools.partial(reduce_kernel, depth),
         out_shape=(
-            shape((rows, D), NARROW),
             shape((rows, D), WIDE),
-            shape((piece, 3 * D), WIDE),
+            shape((rows, D), WIDE),
+            shape((2, count, piece, 256), NARROW),
             shape((HD // 2, D), WIDE),
-            shape((piece, count * units), WIDE),
             shape((units // 2, D), WIDE),
             shape((8, piece), WIDE),
         ),
-        in_specs=[smem] * 2 + [vmem] * 14 + [any_spec] * 2,
-        out_specs=(vmem,) * 7,
-        scratch_shapes=[
+        in_specs=[smem] * 2 + [vmem] * 3 + [any_spec] * 11,
+        out_specs=(vmem,) * 6,
+        scratch_shapes=[pltpu.VMEM(array.shape, array.dtype) for array in large[:9]]
+        + [
             pltpu.VMEM((4 * HD, D), NARROW),
             pltpu.VMEM((2 * depth,) + message, NARROW),
             pltpu.VMEM((2, 2 * depth) + message, NARROW),
@@ -1519,10 +1539,10 @@
             pltpu.VMEM((2, 2, count, piece, 256), WIDE),
             pltpu.VMEM((2, count, piece, 256), WIDE),
             pltpu.VMEM((2, count, piece, 256), NARROW),
-            pltpu.VMEM((2, count, piece, 256), NARROW),
             pltpu.VMEM((HD // 2, D), WIDE),
             pltpu.VMEM((units // 2, D), WIDE),
             pltpu.SMEM((groups, count), jnp.int32),
+            pltpu.SemaphoreType.DMA((9,)),
             pltpu.SemaphoreType.DMA((2, 3, 2 * depth)),
             pltpu.SemaphoreType.DMA((2, 2 * depth)),
             pltpu.SemaphoreType.DMA((2, depth)),
@@ -1537,29 +1557,109 @@
         compiler_params=pltpu.CompilerParams(
             collective_id=2, has_side_effects=True, vmem_limit_bytes=VMEM_LIMIT
         ),
-    )(lengths, dealing, heads, units_in, attended, total, tok, cot, *rest, xhat, cot_all)
+    )(*scalars, *small, *large)
+
+
+def last_kernel(
+    tok_ref,
+    cot_ref,
+    sum_out,
+    sum_back,
+    inbox,
+    wout_in,
+    down_in,
+    vec_in,
+    out_ref,
+    grad_ref,
+    qkv_ref,
+    wout_ref,
+    up_ref,
+    down_ref,
+    vec_a,
+    vec_b,
+    vec_c,
+    vec_d,
+):
+    tokens = tok_ref[...].astype(WIDE)
+    out_ref[...] = (tokens + sum_out[...]).astype(NARROW)
+    average = jnp.mean(tokens, axis=-1, keepdims=True)
+    centred = tokens - average
+    variance = jnp.mean(centred * centred, axis=-1, keepdims=True)
+    rise = lax.rsqrt(variance + EPSILON)
+    xhat = centred * rise
+    g_xhat = sum_back[...]
+    along = jnp.mean(g_xhat * xhat, axis=-1, keepdims=True)
+    level = jnp.mean(g_xhat, axis=-1, keepdims=True)
+    grad_ref[...] = cot_ref[...].astype(WIDE) + rise * (g_xhat - level - xhat * along)
+    count = inbox.shape[1]
+    units = up_ref.shape[1] // count
+    for from_c in range(count):
+        up_ref[:, from_c * units : (from_c + 1) * units] = inbox[0, from_c].astype(WIDE)
+    for pair in range(count // 2):
+        left = inbox[1, 2 * pair].astype(WIDE)
+        right = inbox[1, 2 * pair + 1].astype(WIDE)
+        for part in range(3):
+            lanes = slice((part + 1) * HD, (part + 2) * HD)
+            to = part * D + pair * 128
+            qkv_ref[:, to : to + 128] = jnp.concatenate([left[:, lanes], right[:, lanes]], axis=1)
+    wout_ref[...] = wout_in[...]
+    down_ref[...] = down_in[...]
+    for at, ref in enumerate((vec_a, vec_b, vec_c, vec_d)):
+        ref[...] = vec_in[at]
+
+
+def last_call(tok, cot, sum_out, sum_back, inbox, wout_in, down_in, vec_in):
+    rows = tok.shape[0]
+    _, count, piece, units = inbox.shape
+    shape = jax.ShapeDtypeStruct
+    steps = 2
+
+    def cut(array_shape):
+        return pl.BlockSpec((array_shape[0] // steps,) + array_shape[1:], lambda at: (at, 0))
+
+    whole = pl.BlockSpec((8, piece), lambda at: (0, 0))
+    vector = pl.BlockSpec((piece,), lambda at: (0,))
+    letters = pl.BlockSpec((2, count, piece // steps, units), lambda at: (0, 0, at, 0))
+    outs = (
+        shape((rows, D), NARROW),
+        shape((rows, D), WIDE),
+        shape((piece, 3 * D), WIDE),
+        shape(wout_in.shape, WIDE),
+        shape((piece, count * units), WIDE),
+        shape(down_in.shape, WIDE),
+    )
+    return pl.pallas_call(
+        last_kernel,
+        grid=(steps,),
+        out_shape=outs + (shape((piece,), WIDE),) * 4,
+        in_specs=[cut(array.shape) for array in (tok, cot, sum_out, sum_back)]
+        + [letters, cut(wout_in.shape), cut(down_in.shape), whole],
+        out_specs=tuple(cut(array.shape) for array in outs) + (vector,) * 4,
+        name="last_rows",
+        compiler_params=pltpu.CompilerParams(vmem_limit_bytes=VMEM_LIMIT),
+    )(tok, cot, sum_out, sum_back, inbox, wout_in, down_in, vec_in)
 
 
 def fast_shards(depth, *arguments):
     tokens, cotangent, lengths, dealing = arguments[:4]
-    gains = [vector.reshape(1, -1) for vector in arguments[4:8]]
+    gains = arguments[4:8]
     rows = tokens.shape[0] * tokens.shape[1]
     tok = tokens.reshape(rows, D)
     cot = cotangent.reshape(rows, D)
     forward = gather_call(depth, lengths, dealing, tok, cot, gains, *arguments[8:])
     heads, units, xhat, cot_all, attended, total, g_up, g_down, g_sum = forward[:9]
     wqkv_t, wup_all, wdown_part, wout_part, prm_all = forward[9:]
-    rest = (prm_all, wqkv_t, wup_all, wdown_part, wout_part, g_up, g_down, g_sum)
-    out, grad_tokens, qkv_part, out_part, up_part, down_part, vector_part = reduce_call(
-        depth, lengths, dealing, heads, units, attended, total, tok, cot, rest, xhat, cot_all
+    small = (total, prm_all, g_sum)
+    large = (
+        attended, wout_part, wdown_part, units, g_up, wup_all, wqkv_t, g_down, heads, xhat, cot_all
+    )
+    out, grad_tokens, qkv_part, out_part, up_part, down_part, *vectors = last_call(
+        tok, cot, *reduce_call(depth, (lengths, dealing), small, large, rows)
     )
     return (
         out.reshape(tokens.shape),
         grad_tokens.reshape(tokens.shape),
-        vector_part[0],
-        vector_part[1],
-        vector_part[2],
-        vector_part[3],
+        *vectors,
         qkv_part,
         out_part,
         up_part,

time: 291 us -> 254 us (0.87)
  Pallas kernels: 274 us -> 253 us
  local copies, waits for them, and re-layouts: 15.5 us -> 0 us
    pallas_call x1, Pallas kernels: 137 us -> 124 us  [gather_call(): pl.pallas_call(functools.partial(gather_kernel, depth), out_shape=(shape(...]
    pallas_call x1, Pallas kernels: 137 us -> 125 us  [reduce_call(): pl.pallas_call(functools.partial(reduce_kernel, depth), out_shape=(shape(...]
    unnamed x10 -> x0, local copies, waits for them, and re-layouts: 9.1 us -> none
    reshape x4 -> x0, local copies, waits for them, and re-layouts: 5.04 us -> none  [fast_shards(): gains = [vector.reshape(1, -1) for vector in arguments[4:8]]]
    pallas_call x0 -> x1, Pallas kernels: none -> 3.71 us  [last_call(): pl.pallas_call(last_kernel, grid=(steps,), out_shape=outs + (shape((piece...]
where the time goes in v4:
time: 254 us
  Pallas kernels  253 us (100%)
    pallas_call x1, Pallas kernels, reduce_call(): pl.pallas_call(functools.partial(reduce_kernel, depth), out_shape=(shape(...  125 us
    pallas_call x1, Pallas kernels, gather_call(): pl.pallas_call(functools.partial(gather_kernel, depth), out_shape=(shape(...  124 us

profile of v4, /device:TPU:0, one launch (start us, length us, event | category | flops | bytes accessed | tf_op | source)
XLA Modules:
  0.0 253.6 jit_solution(11142142655366238571)
XLA Ops:
  0.6 124.4 %gather_and_forward.1 = (bf16[16,256,256]{2,1,0:T(8,128)(2,1)}, bf16[16,256,512]{2,1,0:T(8,128)(2,1)}, bf16[16,256,1024]{2,1,0:T(8,128)(2,1)}, bf16[16,256,1024]...) custom-call(s32[2,4]{1,0:T(2,128)} %lengths_ref.3, ...), custom_call_target="tpu_custom_call" | custom-call | tf_op jit(solution)/shard_map/gather_and_forward/pallas_call | solution.py:902
  125.0 124.7 %backward_and_reduce.1 = (f32[256,1024]{1,0:T(8,128)}, f32[256,1024]{1,0:T(8,128)}, bf16[2,16,32,256]{3,2,1,0:T(8,128)(2,1)}, f32[32,1024]{1,0:T(8,128)}, f32[128,1024]{1,0:T(8,128)}, /*index=5*/f32[8,32]{1,0:T(8,128)}) custom-call(s32[2,4]{1,0:T(2,128)} %lengths_ref.3, s32[2,16]{1,0:T(2,128)} %dealing_ref.3, f32[2,8,8,256]{3,2,1,0:T(8,128)} %get-tuple-element.40.total_in, ...), custom_call_target="tpu_custom_call" | custom-call | tf_op jit(solution)/shard_map/backward_and_reduce/pallas_call | solution.py:1506
  249.8 3.7 %last_rows.1 = (bf16[256,1024]{1,0:T(8,128)(2,1)}, f32[256,1024]{1,0:T(8,128)}, f32[32,3072]{1,0:T(8,128)}, f32[32,1024]{1,0:T(8,128)}, f32[32,4096]{1,0:T(8,128...) custom-call(bf16[256,1024]{1,0:T(8,128)(2,1)} %bitcast.5, ...), custom_call_target="tpu_custom_call" | custom-call | tf_op jit(solution)/shard_map/last_rows/pallas_call | solution.py:1631

commit v5 on v4

--- a/solution.py
+++ b/solution.py
@@ -476,6 +476,16 @@
         frequency = jnp.where(row == at, FREQUENCY[at], frequency)
     angles = place.astype(WIDE) * frequency
     return jnp.cos(angles), jnp.sin(angles)
+
+
+ALONG = (16, 16)
+
+
+def cut(rows, what, piece):
+    rest = rows - ALONG[what]
+    first = (rest // 2 + 15) // 16 * 16
+    begin = (0, first, rest, rows)
+    return pl.ds(begin[piece], begin[piece + 1] - begin[piece])
 
 
 def starts_of(lengths_ref, group):
@@ -536,6 +546,7 @@
     wdown_part,
     wout_part,
     prm_all,
+    found,
     both,
     xhat_all,
     heads_buf,
@@ -545,7 +556,6 @@
     k_rows,
     wq_buf,
     prm_buf,
-    found,
     in_sem,
     w_sem,
     wsend_sem,
@@ -622,34 +632,45 @@
     for at, (source, place) in enumerate(shared):
         remote(source, place, at).start()
 
-    def passing(what, shard, way):
+    def passing(what, piece, shard, way):
         device = (here.beside, here.twin, here.above, here.below)[way]
         return pltpu.make_async_remote_copy(
-            both.at[what, shard],
-            both.at[what, shard],
-            send_sem.at[what, way, shard],
-            recv_sem.at[what, shard],
+            both.at[what, shard, cut(rows, what, piece)],
+            both.at[what, shard, cut(rows, what, piece)],
+            send_sem.at[what, piece, way, shard],
+            recv_sem.at[what, piece, shard],
             device_id=device,
             device_id_type=MESH,
         )
 
-    def onward(what, shard, from_z):
-        passing(what, shard, 0).start()
+    def onward(what, piece, shard, from_z, cross):
+        if cross:
+            passing(what, piece, shard, 0).start()
 
         @pl.when(jnp.logical_and(from_z <= z, here.has_above))
         def _():
-            passing(what, shard, 2).start()
+            passing(what, piece, shard, 2).start()
 
         @pl.when(jnp.logical_and(from_z >= z, here.has_below))
         def _():
-            passing(what, shard, 3).start()
-
-        passing(what, shard, 1).start()
+            passing(what, piece, shard, 3).start()
+
+        passing(what, piece, shard, 1).start()
+
+    def arrived(what, piece, shard):
+        passing(what, piece, shard, 1).wait_recv()
+
+    def relay(what, shard, from_z):
+        for piece in range(3):
+            arrived(what, piece, shard)
+            onward(what, piece, shard, from_z, piece < 2)
 
     own_in[0].wait()
-    onward(0, c, z)
+    for piece in range(3):
+        onward(0, piece, c, z, True)
     own_in[1].wait()
-    onward(1, c, z)
+    for piece in range(3):
+        onward(1, piece, c, z, True)
     find_blocks(dealing_ref, found)
 
     for at, (source, place) in enumerate(shared):
@@ -730,7 +751,9 @@
 
     inner = jnp.logical_and(here.has_above, here.has_below)
 
-    def sweep(what, work, beside_work):
+    def sweep(what, work, beside_work, first=0):
+        relays = what == 0
+
         def step(at, carry):
             turn_no = at // 4
             kind = lax.rem(at, 4)
@@ -746,23 +769,30 @@
             is_own = jnp.logical_and(kind == 0, turn_no == 0)
             done = jnp.logical_or(is_own, jnp.logical_and(kind == 0, early))
 
-            @pl.when(jnp.logical_and(live, jnp.logical_not(done)))
+            @pl.when(jnp.logical_and(lax.rem(kind, 2) == 1, live))
             def _():
-                passing(what, shard, 1).wait_recv()
-
-            @pl.when(jnp.logical_and(jnp.logical_and(kind == 0, live), jnp.logical_not(done)))
-            def _():
-                onward(what, shard, from_z)
+                for piece in range(3):
+                    arrived(what, piece, shard)
+
+            if relays:
+
+                @pl.when(jnp.logical_and(jnp.logical_and(kind == 0, live), jnp.logical_not(done)))
+                def _():
+                    relay(what, shard, from_z)
 
             @pl.when(jnp.logical_and(kind == 2, live))
             def _():
-                passing(what, shard, 1).start()
-
-            @pl.when(jnp.logical_and(jnp.logical_and(kind == 1, turn_no == 1), inner))
-            def _():
-                following = here.at(next_z, y, core)
-                passing(what, following, 1).wait_recv()
-                onward(what, following, next_z)
+                arrived(what, 2, shard)
+                onward(what, 2, shard, from_z, False)
+                for piece in range(2):
+                    arrived(what, piece, shard)
+                    passing(what, piece, shard, 1).start()
+
+            if relays:
+
+                @pl.when(jnp.logical_and(jnp.logical_and(kind == 1, turn_no == 1), inner))
+                def _():
+                    relay(what, here.at(next_z, y, core), next_z)
 
             beside_work(at)
 
@@ -772,19 +802,44 @@
 
             return carry
 
-        lax.fori_loop(0, 4 * depth + 4, step, 0)
-
-    sweep(0, ahead, lambda at: None)
-
-    @pl.when(is_owner)
-    def _():
-        for at, (source, place) in enumerate(held):
-            pltpu.make_async_copy(source, place, w_sem.at[5 + at]).wait()
-
-    @pl.when(jnp.logical_not(is_owner))
-    def _():
-        for at, (source, place) in enumerate(held):
-            remote(source, place, 5 + at).wait_recv()
+        lax.fori_loop(first, 4 * depth + 4, step, 0)
+
+    def relay_next(at, wanted, index, which):
+        @pl.when(jnp.logical_and(at == wanted, which))
+        def _():
+            from_z = pick2(z, jnp.int32(index), order)
+            relay(1, here.at(from_z, y, core), from_z)
+
+    outer = jnp.logical_not(inner)
+
+    def late_weights():
+        @pl.when(is_owner)
+        def _():
+            for at, (source, place) in enumerate(held):
+                pltpu.make_async_copy(source, place, w_sem.at[5 + at]).wait()
+
+        @pl.when(jnp.logical_not(is_owner))
+        def _():
+            for at, (source, place) in enumerate(held):
+                remote(source, place, 5 + at).wait_recv()
+
+    def cotangents_start(at):
+        relay_next(at, 4 * depth, 1, at >= 0)
+        relay_next(at, 4 * depth + 1, 2, inner)
+
+        @pl.when(at == 4 * depth)
+        def _():
+            late_weights()
+            behind(c)
+
+        @pl.when(at == 4 * depth + 1)
+        def _():
+            twin = here.at(z, y, 1 - core)
+            for piece in range(3):
+                arrived(1, piece, twin)
+            behind(twin)
+
+    sweep(0, ahead, cotangents_start)
 
     spans = count // 2
     span = 2 * BLK
@@ -846,11 +901,15 @@
         total_out[group, mine] = jnp.broadcast_to(top + jnp.log(total), (8, span))
 
     def attend_too(at):
-        @pl.when(at < groups * spans)
-        def _():
-            attend(at)
-
-    sweep(1, behind, attend_too)
+        relay_next(at, 4, 2, outer)
+        relay_next(at, 4, 3, inner)
+        relay_next(at, 7, 3, outer)
+
+        @pl.when(at < groups * spans + 4)
+        def _():
+            attend(at - 4)
+
+    sweep(1, behind, attend_too, first=4)
 
     def finish(shard, carry):
         shard_z = shard // 4
@@ -860,19 +919,25 @@
 
             @pl.when(mine)
             def _():
-                passing(what, shard, 1).wait_send()
-
-            @pl.when(jnp.logical_and(mine, column))
-            def _():
-                passing(what, shard, 0).wait_send()
-
-                @pl.when(jnp.logical_and(shard_z <= z, here.has_above))
+                for piece in range(3):
+                    passing(what, piece, shard, 1).wait_send()
+
+            for piece in range(3):
+                along = mine if piece == 2 else jnp.logical_and(mine, column)
+
+                @pl.when(jnp.logical_and(along, jnp.logical_and(shard_z <= z, here.has_above)))
                 def _():
-                    passing(what, shard, 2).wait_send()
-
-                @pl.when(jnp.logical_and(shard_z >= z, here.has_below))
+                    passing(what, piece, shard, 2).wait_send()
+
+                @pl.when(jnp.logical_and(along, jnp.logical_and(shard_z >= z, here.has_below)))
                 def _():
-                    passing(what, shard, 3).wait_send()
+                    passing(what, piece, shard, 3).wait_send()
+
+                crossed = shard == c if piece == 2 else jnp.logical_and(mine, column)
+
+                @pl.when(crossed)
+                def _():
+                    passing(what, piece, shard, 0).wait_send()
 
         for at in range(4):
             copy_out(at, shard).wait()
@@ -916,9 +981,10 @@
             shape((units, D), NARROW),
             shape((HD, D), NARROW),
             shape((8, D), WIDE),
+            shape((groups, count), jnp.int32),
         ),
         in_specs=[smem, smem, any_spec, any_spec] + [vmem] * 4 + [any_spec] * 4,
-        out_specs=(any_spec,) * 4 + (vmem,) * 10,
+        out_specs=(any_spec,) * 4 + (vmem,) * 10 + (smem,),
         scratch_shapes=[
             pltpu.VMEM((2, count, rows, D), NARROW),
             pltpu.VMEM((count, rows, D), NARROW),
@@ -929,13 +995,12 @@
             pltpu.VMEM((groups, spans, span, HD), NARROW),
             pltpu.VMEM((2, 3, D // 2, 128), NARROW),
             pltpu.VMEM((2, 8, D // 2), WIDE),
-            pltpu.SMEM((groups, count), jnp.int32),
             pltpu.SemaphoreType.DMA((2,)),
             pltpu.SemaphoreType.DMA((7,)),
             pltpu.SemaphoreType.DMA((7,)),
             pltpu.SemaphoreType.DMA((7,)),
-            pltpu.SemaphoreType.DMA((2, 4, count)),
-            pltpu.SemaphoreType.DMA((2, count)),
+            pltpu.SemaphoreType.DMA((2, 3, 4, count)),
+            pltpu.SemaphoreType.DMA((2, 3, count)),
             pltpu.SemaphoreType.DMA((4, count)),
         ],
         name="gather_and_forward",
@@ -960,6 +1025,7 @@
     depth,
     lengths_ref,
     dealing_ref,
+    found,
     total_in,
     prm_all,
     g_sum,
@@ -994,6 +1060,7 @@
     sum_buf,
     beside_buf,
     line_buf,
+    other_line,
     wide,
     q_rows,
     k_rows,
@@ -1013,12 +1080,15 @@
     mail,
     wout_in,
     down_in,
-    found,
     first_sem,
-    send_sem,
+    send_twin,
+    send_beside,
     recv_twin,
     recv_beside,
     recv_z,
+    send_z,
+    send_last,
+    recv_last,
     stream_sem,
     across_send,
     across_recv,
@@ -1089,54 +1159,60 @@
         return pltpu.make_async_remote_copy(
             give_buf.at[slot],
             sum_buf.at[what, slot],
-            send_sem.at[what, 0, slot],
+            send_twin.at[what, slot],
             recv_twin.at[what, slot],
             device_id=here.twin,
             device_id_type=MESH,
         )
 
-    def to_beside(what, to_z):
+    def to_beside(what, piece, to_z):
         return pltpu.make_async_remote_copy(
-            sum_buf.at[what, to_z],
-            beside_buf.at[what, to_z],
-            send_sem.at[what, 1, to_z],
-            recv_beside.at[what, to_z],
+            sum_buf.at[what, to_z, cut(rows, what, piece)],
+            beside_buf.at[what, to_z, cut(rows, what, piece)],
+            send_beside.at[what, piece, to_z],
+            recv_beside.at[what, piece, to_z],
             device_id=here.beside,
             device_id_type=MESH,
         )
 
-    def to_above(what, to_z):
-        return pltpu.make_async_remote_copy(
-            sum_buf.at[what, depth + to_z],
-            line_buf.at[what, to_z],
-            send_sem.at[what, 2, to_z],
-            recv_z.at[what, to_z],
-            device_id=here.above,
-            device_id_type=MESH,
-        )
-
     def over_slot(to_z, at_z):
         return jnp.where(to_z == at_z, depth, to_z)
 
-    def to_below(what, to_z):
-        slot = over_slot(to_z, z - 1)
+    def along(what, piece, home, to_z, place, device):
+        here_rows = cut(rows, what, piece)
+        if piece == 2:
+            target = other_line.at[what, place, pl.ds(0, ALONG[what])]
+            if home == 1:
+                target = line_buf.at[what, place, here_rows]
+        else:
+            target = line_buf.at[what, place, here_rows]
+        lane = piece + (home if piece == 2 else 0)
         return pltpu.make_async_remote_copy(
-            sum_buf.at[what, depth + to_z],
-            line_buf.at[what, slot],
-            send_sem.at[what, 2, to_z],
-            recv_z.at[what, slot],
-            device_id=here.below,
+            sum_buf.at[what, home * depth + to_z, here_rows],
+            target,
+            send_z.at[what, lane, to_z],
+            recv_z.at[what, lane, place],
+            device_id=device,
             device_id_type=MESH,
         )
 
-    def from_above(what, to_z):
-        slot = over_slot(to_z, z)
+    def to_above(what, piece, home, to_z):
+        return along(what, piece, home, to_z, to_z, here.above)
+
+    def to_below(what, piece, home, to_z):
+        return along(what, piece, home, to_z, over_slot(to_z, z - 1), here.below)
+
+    def from_above(what, piece, home, to_z):
+        return along(what, piece, home, to_z, over_slot(to_z, z), here.above)
+
+    def cross_last(what):
+        here_rows = cut(rows, what, 2)
         return pltpu.make_async_remote_copy(
-            sum_buf.at[what, depth + to_z],
-            line_buf.at[what, slot],
-            send_sem.at[what, 2, to_z],
-            recv_z.at[what, slot],
-            device_id=here.above,
+            sum_buf.at[what, z, here_rows],
+            beside_buf.at[what, z, here_rows],
+            send_last.at[what],
+            recv_last.at[what],
+            device_id=here.beside,
             device_id_type=MESH,
         )
 
@@ -1159,52 +1235,93 @@
 
         @pl.when(kind == 2)
         def _():
-            to_beside(what, to_z).start()
-
-    def chain(what, at):
+            for piece in range(2):
+                to_beside(what, piece, to_z).start()
+
+    def chain_piece(what, at, piece, home):
         to_z = pick2(z, at, order)
-        slot = depth + to_z
-        to_beside(what, to_z).wait_recv()
+        slot = home * depth + to_z
+        here_rows = cut(rows, what, piece)
+        if piece < 2:
+            to_beside(what, piece, to_z).wait_recv()
 
         def add(incoming):
-            for part in range(2):
-                half = slice(part * rows // 2, (part + 1) * rows // 2)
-                total = sum_buf[what, slot, half, :].astype(WIDE)
-                total = total + beside_buf[what, to_z, half, :].astype(WIDE)
-                if incoming:
-                    total = total + line_buf[what, to_z, half, :].astype(WIDE)
-                sum_buf[what, slot, half, :] = total.astype(NARROW)
+            total = sum_buf[what, slot, here_rows, :].astype(WIDE)
+            if piece < 2:
+                total = total + beside_buf[what, to_z, here_rows, :].astype(WIDE)
+            if incoming:
+                if piece == 2 and home == 0:
+                    came = other_line[what, to_z, 0 : ALONG[what], :]
+                else:
+                    came = line_buf[what, to_z, here_rows, :]
+                total = total + came.astype(WIDE)
+            sum_buf[what, slot, here_rows, :] = total.astype(NARROW)
 
         @pl.when(to_z > z)
         def _():
             @pl.when(here.has_below)
             def _():
-                to_above(what, to_z).wait_recv()
+                to_above(what, piece, home, to_z).wait_recv()
                 add(True)
 
-            @pl.when(jnp.logical_not(here.has_below))
-            def _():
-                add(False)
-
-            to_above(what, to_z).start()
+            if piece < 2:
+
+                @pl.when(jnp.logical_not(here.has_below))
+                def _():
+                    add(False)
+
+            to_above(what, piece, home, to_z).start()
 
         @pl.when(to_z < z)
         def _():
             @pl.when(here.has_above)
             def _():
-                from_above(what, to_z).wait_recv()
+                from_above(what, piece, home, to_z).wait_recv()
                 add(True)
 
-            @pl.when(jnp.logical_not(here.has_above))
-            def _():
-                add(False)
-
-            to_below(what, to_z).start()
+            if piece < 2:
+
+                @pl.when(jnp.logical_not(here.has_above))
+                def _():
+                    add(False)
+
+            to_below(what, piece, home, to_z).start()
+
+    def chain(what, at):
+        for home in range(2):
+            chain_piece(what, at, 2, home)
+        for piece in range(2):
+            chain_piece(what, at, piece, 1)
+
+    def cross_over(what):
+        here_rows = cut(rows, what, 2)
+        came = slice(0, ALONG[what])
+
+        @pl.when(here.has_below)
+        def _():
+            to_above(what, 2, 0, z).wait_recv()
+            total = sum_buf[what, z, here_rows, :].astype(WIDE)
+            total = total + other_line[what, z, came, :].astype(WIDE)
+            sum_buf[what, z, here_rows, :] = total.astype(NARROW)
+
+        @pl.when(here.has_above)
+        def _():
+            from_above(what, 2, 0, z).wait_recv()
+            total = sum_buf[what, z, here_rows, :].astype(WIDE)
+            total = total + other_line[what, depth, came, :].astype(WIDE)
+            sum_buf[what, z, here_rows, :] = total.astype(NARROW)
+
+        cross_last(what).start()
 
     def gather_total(what):
+        for piece in range(2):
+            to_beside(what, piece, z).wait_recv()
+        cross_last(what).wait_recv()
+
         @pl.when(here.has_below)
         def _():
-            to_above(what, z).wait_recv()
+            for piece in range(3):
+                to_above(what, piece, 1, z).wait_recv()
 
         @pl.when(jnp.logical_not(here.has_below))
         def _():
@@ -1212,7 +1329,8 @@
 
         @pl.when(here.has_above)
         def _():
-            from_above(what, z).wait_recv()
+            for piece in range(3):
+                from_above(what, piece, 1, z).wait_recv()
 
         @pl.when(jnp.logical_not(here.has_above))
         def _():
@@ -1258,7 +1376,7 @@
             scaled = jnp.where(lane == 3, vectors[row, 1:2], scaled)
         per = 128 // piece
         for at in range(per):
-            grads[part, at % 2, chunk * (per // 2) + at // 2] = scaled[at * piece : (at + 1) * piece]
+            grads[part, at % 2, chunk * (per // 2) + at // 2] = scaled[at * piece : (at + 1) * piece].astype(NARROW)
 
     sum_units = jnp.sum(g_sum[...], axis=0, keepdims=True)
 
@@ -1270,7 +1388,6 @@
 
     lax.fori_loop(0, D // 128, settle_up, 0)
     send_grads[0].start()
-    find_blocks(dealing_ref, found)
     w_heads_back[0:HD, :] = jnp.zeros((HD, D), NARROW)
     w_heads_back[HD:, :] = wqkv_t[...]
     g_heads[...] = jnp.zeros_like(g_heads)
@@ -1344,7 +1461,10 @@
             return carry
 
         lax.fori_loop(0, spans, one_span, 0)
-        chain(0, 2 * group + 1)
+        if group == 0:
+            chain(0, 1)
+        else:
+            cross_over(0)
 
         def give(at, carry, group=group, starts=starts):
             natural = at * span + lax.broadcasted_iota(jnp.int32, (1, span), 1)
@@ -1363,46 +1483,20 @@
     for copy in load(0):
         copy.start()
 
+    def tokens_of(shard):
+        blocks = [by_token[group, dealing_ref[group, shard]] for group in range(groups)]
+        return jnp.concatenate(blocks, axis=0)
+
     def give_back(at, carry):
-        shard, slot = shard_of(at), lax.rem(at, 2)
-        blocks = [dealing_ref[group, shard] for group in range(groups)]
-        heads = jnp.concatenate([by_token[group, blocks[group]] for group in range(groups)], axis=0)
+        shard = shard_of(at)
         g_hidden = units_in[shard, :, units : 2 * units]
-        part = dot(heads, w_heads_back[...]) * prm_all[0:1, :] + dot(
+        part = dot(tokens_of(shard), w_heads_back[...]) * prm_all[0:1, :] + dot(
             g_hidden, wup_all[...], NT
         ) * prm_all[2:3, :]
         pass_on(1, at, part)
-
-        @pl.when(at + 1 < count)
-        def _():
-            for copy in load(at + 1):
-                copy.start()
-
-        for copy in load(at):
-            copy.wait()
-        turned = jnp.concatenate([turned_all[group, blocks[group]] for group in range(groups)], axis=1)
-        g_wout[...] += dot(turned[0:HD], stream[1, slot])
-        g_heads[HD:, :] += dot(turned[HD:], stream[0, slot])
-        sum_heads[...] += jnp.sum(heads.astype(WIDE).reshape(rows // 8, 8, 4 * HD), axis=0)
-
-        @pl.when(at == count - 4)
-        def _():
-            chain(1, 0)
-
         return carry
 
     lax.fori_loop(0, count, give_back, 0)
-    send_wout.start()
-    sum_row = jnp.sum(sum_heads[...], axis=0, keepdims=True)
-
-    def settle_qkv(chunk, carry):
-        lanes = pl.ds(pl.multiple_of(chunk * 128, 128), 128)
-        weights = w_heads_back[:, lanes].astype(WIDE).T
-        settle(chunk, 1, g_heads[:, lanes].T, weights, sum_row, prm_all[:, lanes].T)
-        return carry
-
-    lax.fori_loop(0, D // 128, settle_qkv, 0)
-    send_grads[1].start()
 
     def post(part, to_c):
         return pltpu.make_async_remote_copy(
@@ -1428,7 +1522,9 @@
         send_grads[part].wait_recv()
 
         def fold(to_c, carry):
-            mail[part, to_c] = (grads[part, x, to_c] + grads_in[part, to_c]).astype(NARROW)
+            mail[part, to_c] = (
+                grads[part, x, to_c].astype(WIDE) + grads_in[part, to_c].astype(WIDE)
+            ).astype(NARROW)
             return carry
 
         lax.fori_loop(0, count, fold, 0)
@@ -1441,14 +1537,68 @@
         inbox[part, c] = mail[part, c]
 
     mail_out(0)
-    chain(1, 1)
+
+    def weigh(at, carry):
+        shard, slot = shard_of(at), lax.rem(at, 2)
+
+        @pl.when(at + 1 < count)
+        def _():
+            for copy in load(at + 1):
+                copy.start()
+
+        for copy in load(at):
+            copy.wait()
+        turned = jnp.concatenate(
+            [turned_all[group, dealing_ref[group, shard]] for group in range(groups)], axis=1
+        )
+        g_wout[...] += dot(turned[0:HD], stream[1, slot])
+        g_heads[HD:, :] += dot(turned[HD:], stream[0, slot])
+        sum_heads[...] += jnp.sum(
+            tokens_of(shard).astype(WIDE).reshape(rows // 8, 8, 4 * HD), axis=0
+        )
+        return carry
+
+    inner = jnp.logical_and(here.has_above, here.has_below)
+    outer = jnp.logical_not(inner)
+    early, middle = count // 4, count * 5 // 8
+    lax.fori_loop(0, early, weigh, 0)
+
+    @pl.when(outer)
+    def _():
+        chain(1, 0)
+
+    lax.fori_loop(early, middle, weigh, 0)
+
+    @pl.when(outer)
+    def _():
+        chain(1, 1)
+
+    @pl.when(inner)
+    def _():
+        chain(1, 0)
+
+    lax.fori_loop(middle, count, weigh, 0)
+    send_wout.start()
+    sum_row = jnp.sum(sum_heads[...], axis=0, keepdims=True)
+
+    def settle_qkv(chunk, carry):
+        lanes = pl.ds(pl.multiple_of(chunk * 128, 128), 128)
+        weights = w_heads_back[:, lanes].astype(WIDE).T
+        settle(chunk, 1, g_heads[:, lanes].T, weights, sum_row, prm_all[:, lanes].T)
+        return carry
+
+    lax.fori_loop(0, D // 128, settle_qkv, 0)
+    send_grads[1].start()
+
+    @pl.when(inner)
+    def _():
+        chain(1, 1)
+
     mail_out(1)
-
-    def rest(at, carry):
+    for at in range(2, depth - 1):
         chain(1, at)
-        return carry
-
-    lax.fori_loop(2, depth, rest, 0)
+    cross_over(1)
+
 
     sum_out[...] = gather_total(0)
     send_down.wait()
@@ -1476,24 +1626,31 @@
         to_twin(1, to_z).wait_send()
         to_twin(1, depth + to_z).wait_send()
         for what in range(2):
-            to_beside(what, to_z).wait_send()
+            for piece in range(2):
+                to_beside(what, piece, to_z).wait_send()
 
             @pl.when(to_z > z)
             def _():
-                to_above(what, to_z).wait_send()
+                to_above(what, 2, 0, to_z).wait_send()
+                for piece in range(3):
+                    to_above(what, piece, 1, to_z).wait_send()
 
             @pl.when(to_z < z)
             def _():
-                to_below(what, to_z).wait_send()
+                to_below(what, 2, 0, to_z).wait_send()
+                for piece in range(3):
+                    to_below(what, piece, 1, to_z).wait_send()
 
         return carry
 
     lax.fori_loop(0, depth, finish, 0)
+    for what in range(2):
+        cross_last(what).wait_send()
 
 
 def reduce_call(depth, scalars, small, large, rows):
     count = depth * 4
-    groups = scalars[0].shape[0]
+    groups = scalars[1].shape[0]
     spans, span = count // 2, 2 * BLK
     piece = D // (2 * count)
     units = large[5].shape[1]
@@ -1513,7 +1670,7 @@
             shape((units // 2, D), WIDE),
             shape((8, piece), WIDE),
         ),
-        in_specs=[smem] * 2 + [vmem] * 3 + [any_spec] * 11,
+        in_specs=[smem] * 3 + [vmem] * 3 + [any_spec] * 11,
         out_specs=(vmem,) * 6,
         scratch_shapes=[pltpu.VMEM(array.shape, array.dtype) for array in large[:9]]
         + [
@@ -1522,6 +1679,7 @@
             pltpu.VMEM((2, 2 * depth) + message, NARROW),
             pltpu.VMEM((2, depth) + message, NARROW),
             pltpu.VMEM((2, depth + 1) + message, NARROW),
+            pltpu.VMEM((2, depth + 1, max(ALONG), D), NARROW),
             pltpu.VMEM((spans, 3 * HD, span), NARROW),
             row_form,
             row_form,
@@ -1536,17 +1694,20 @@
             pltpu.VMEM((HD, D), WIDE),
             pltpu.VMEM((8, 4 * HD), WIDE),
             pltpu.VMEM((D, 128), WIDE),
-            pltpu.VMEM((2, 2, count, piece, 256), WIDE),
-            pltpu.VMEM((2, count, piece, 256), WIDE),
+            pltpu.VMEM((2, 2, count, piece, 256), NARROW),
+            pltpu.VMEM((2, count, piece, 256), NARROW),
             pltpu.VMEM((2, count, piece, 256), NARROW),
             pltpu.VMEM((HD // 2, D), WIDE),
             pltpu.VMEM((units // 2, D), WIDE),
-            pltpu.SMEM((groups, count), jnp.int32),
             pltpu.SemaphoreType.DMA((9,)),
-            pltpu.SemaphoreType.DMA((2, 3, 2 * depth)),
             pltpu.SemaphoreType.DMA((2, 2 * depth)),
-            pltpu.SemaphoreType.DMA((2, depth)),
-            pltpu.SemaphoreType.DMA((2, depth + 1)),
+            pltpu.SemaphoreType.DMA((2, 2, depth)),
+            pltpu.SemaphoreType.DMA((2, 2 * depth)),
+            pltpu.SemaphoreType.DMA((2, 2, depth)),
+            pltpu.SemaphoreType.DMA((2, 4, depth + 1)),
+            pltpu.SemaphoreType.DMA((2, 4, depth)),
+            pltpu.SemaphoreType.DMA((2,)),
+            pltpu.SemaphoreType.DMA((2,)),
             pltpu.SemaphoreType.DMA((2, 2)),
             pltpu.SemaphoreType.DMA((4,)),
             pltpu.SemaphoreType.DMA((4,)),
@@ -1648,13 +1809,13 @@
     cot = cotangent.reshape(rows, D)
     forward = gather_call(depth, lengths, dealing, tok, cot, gains, *arguments[8:])
     heads, units, xhat, cot_all, attended, total, g_up, g_down, g_sum = forward[:9]
-    wqkv_t, wup_all, wdown_part, wout_part, prm_all = forward[9:]
+    wqkv_t, wup_all, wdown_part, wout_part, prm_all, found = forward[9:]
     small = (total, prm_all, g_sum)
     large = (
         attended, wout_part, wdown_part, units, g_up, wup_all, wqkv_t, g_down, heads, xhat, cot_all
     )
     out, grad_tokens, qkv_part, out_part, up_part, down_part, *vectors = last_call(
-        tok, cot, *reduce_call(depth, (lengths, dealing), small, large, rows)
+        tok, cot, *reduce_call(depth, (lengths, dealing, found), small, large, rows)
     )
     return (
         out.reshape(tokens.shape),

time: 254 us -> 238 us (0.937)
  Pallas kernels: 253 us -> 237 us
    pallas_call x1, Pallas kernels: 124 us -> 115 us  [gather_call(): pl.pallas_call(functools.partial(gather_kernel, depth), out_shape=(shape(...]
    pallas_call x1, Pallas kernels: 125 us -> 118 us  [reduce_call(): pl.pallas_call(functools.partial(reduce_kernel, depth), out_shape=(shape(...]
where the time goes in v5:
time: 238 us
  Pallas kernels  237 us (100%)
    pallas_call x1, Pallas kernels, reduce_call(): pl.pallas_call(functools.partial(reduce_kernel, depth), out_shape=(shape(...  118 us
    pallas_call x1, Pallas kernels, gather_call(): pl.pallas_call(functools.partial(gather_kernel, depth), out_shape=(shape(...  115 us

profile of v5, /device:TPU:0, one launch (start us, length us, event | category | flops | bytes accessed | tf_op | source)
XLA Modules:
  0.0 238.1 jit_solution(14757824471995491925)
XLA Ops:
  0.6 115.3 %gather_and_forward.1 = (bf16[16,256,256]{2,1,0:T(8,128)(2,1)}, bf16[16,256,512]{2,1,0:T(8,128)(2,1)}, bf16[16,256,1024]{2,1,0:T(8,128)(2,1)}, bf16[16,256,1024]...) custom-call(s32[2,4]{1,0:T(2,128)} %lengths_ref.3, ...), custom_call_target="tpu_custom_call" | custom-call | tf_op jit(solution)/shard_map/gather_and_forward/pallas_call | solution.py:967
  115.9 118.3 %backward_and_reduce.1 = (f32[256,1024]{1,0:T(8,128)}, f32[256,1024]{1,0:T(8,128)}, bf16[2,16,32,256]{3,2,1,0:T(8,128)(2,1)}, f32[32,1024]{1,0:T(8,128)}, f32[128,1024]{1,0:T(8,128)}, /*index=5*/f32[8,32]{1,0:T(8,128)}) custom-call(s32[2,4]{1,0:T(2,128)} %lengths_ref.3, s32[2,16]{1,0:T(2,128)} %dealing_ref.3, s32[2,16]{1,0:T(2,128)} %get-tuple-element.41.found, ...), custom_call_target="tpu_custom_call" | custom-call | tf_op jit(solution)/shard_map/backward_and_reduce/pallas_call | solution.py:1663
  234.2 3.7 %last_rows.1 = (bf16[256,1024]{1,0:T(8,128)(2,1)}, f32[256,1024]{1,0:T(8,128)}, f32[32,3072]{1,0:T(8,128)}, f32[32,1024]{1,0:T(8,128)}, f32[32,4096]{1,0:T(8,128...) custom-call(bf16[256,1024]{1,0:T(8,128)(2,1)} %bitcast.5, ...), custom_call_target="tpu_custom_call" | custom-call | tf_op jit(solution)/shard_map/last_rows/pallas_call | solution.py:1792

commit v6 on v5

--- a/solution.py
+++ b/solution.py
@@ -865,19 +865,22 @@
         mine = jnp.where(lax.rem(turn_no, 2) == 0, spans - 1 - turn_no // 2, turn_no // 2)
         natural = mine * span + lax.broadcasted_iota(jnp.int32, (1, span), 1)
         opening = opening_of(natural, [jnp.where(group == 0, *pair) for pair in zip(*openings)])
-        key_in = lax.broadcasted_iota(jnp.int32, (2 * span, span), 0)
         queries = wide[group, mine, 0:HD, :]
 
-        def add(keys_at, state, allowed):
+        def add(first, width, state, diagonal):
             top, total, so_far = state
-            keys = k_rows[group, pl.ds(2 * keys_at, 2)].reshape(2 * span, HD)
+            keys = k_rows[group, pl.ds(first, width)].reshape(width * span, HD)
+            place = lax.broadcasted_iota(jnp.int32, (width * span, span), 0)
+            allowed = place >= opening - first * span
+            if diagonal:
+                allowed = jnp.logical_and(allowed, place <= natural - first * span)
             raw = jnp.where(allowed, dot(keys, queries), MASKED)
             new_top = jnp.maximum(top, jnp.max(raw, axis=0, keepdims=True))
             risen = jnp.exp(raw - new_top)
             fade = jnp.exp(top - new_top)
             total = total * fade + jnp.sum(risen, axis=0, keepdims=True)
             values = jnp.concatenate(
-                [wide[group, 2 * keys_at + side, HD : 2 * HD, :] for side in range(2)], axis=1
+                [wide[group, first + side, HD : 2 * HD, :] for side in range(width)], axis=1
             )
             return new_top, total, so_far * fade + dot(values, risen.astype(NARROW))
 
@@ -887,12 +890,15 @@
             jnp.zeros((HD, span), WIDE),
         )
         last = mine // 2
-        place = key_in + last * (2 * span)
-        state = add(last, state, jnp.logical_and(place <= natural, place >= opening))
+        state = lax.cond(
+            lax.rem(mine, 2) == 1,
+            lambda state: add(mine - 1, 2, state, True),
+            lambda state: add(mine, 1, state, True),
+            state,
+        )
 
         def earlier(back, state):
-            keys_at = last - 1 - back
-            return add(keys_at, state, key_in >= opening - keys_at * (2 * span))
+            return add(2 * (last - 1 - back), 2, state, False)
 
         top, total, so_far = lax.fori_loop(0, last, earlier, state)
         attended = so_far / total
@@ -1423,7 +1429,6 @@
         def one_span(at, carry, group=group, starts=starts):
             natural = at * span + lax.broadcasted_iota(jnp.int32, (1, span), 1)
             opening = opening_of(natural, starts)
-            key_in = lax.broadcasted_iota(jnp.int32, (2 * span, span), 0)
             queries = wide[at, 0:HD, :]
             g_attended = wide[at, 2 * HD : 3 * HD, :]
             attended = jnp.concatenate(
@@ -1432,27 +1437,34 @@
             row_dot = jnp.sum(attended * g_attended.astype(WIDE), axis=0, keepdims=True)
             log_total = total_in[group, at, 0:1, :]
 
-            def add(pair, so_far, allowed):
-                two = pl.ds(2 * pair, 2)
-                keys = k_rows[two].reshape(2 * span, HD)
-                values = v_rows[two].reshape(2 * span, HD)
+            def add(first, width, so_far, diagonal):
+                some = pl.ds(first, width)
+                keys = k_rows[some].reshape(width * span, HD)
+                values = v_rows[some].reshape(width * span, HD)
+                place = lax.broadcasted_iota(jnp.int32, (width * span, span), 0)
+                allowed = place >= opening - first * span
+                if diagonal:
+                    allowed = jnp.logical_and(allowed, place <= natural - first * span)
                 scores = dot(keys, queries)
                 probs = jnp.where(allowed, jnp.exp(scores - log_total), 0.0)
                 g_scores = (probs * (dot(values, g_attended) - row_dot)).astype(NARROW)
-                g_key[two] += dot(g_scores, q_rows[at]).reshape(2, span, HD)
-                g_value[two] += dot(probs.astype(NARROW), g_rows[at]).reshape(2, span, HD)
+                g_key[some] += dot(g_scores, q_rows[at]).reshape(width, span, HD)
+                g_value[some] += dot(probs.astype(NARROW), g_rows[at]).reshape(width, span, HD)
                 keys_t = jnp.concatenate(
-                    [wide[2 * pair + side, HD : 2 * HD, :] for side in range(2)], axis=1
+                    [wide[first + side, HD : 2 * HD, :] for side in range(width)], axis=1
                 )
                 return so_far + dot(keys_t, g_scores)
 
             def earlier(pair, so_far):
-                return add(pair, so_far, key_in >= opening - pair * (2 * span))
-
-            last = at // 2
-            so_far = lax.fori_loop(0, last, earlier, jnp.zeros((HD, span), WIDE))
-            place = key_in + last * (2 * span)
-            so_far = add(last, so_far, jnp.logical_and(place <= natural, place >= opening))
+                return add(2 * pair, 2, so_far, False)
+
+            so_far = lax.fori_loop(0, at // 2, earlier, jnp.zeros((HD, span), WIDE))
+            so_far = lax.cond(
+                lax.rem(at, 2) == 1,
+                lambda so_far: add(at - 1, 2, so_far, True),
+                lambda so_far: add(at, 1, so_far, True),
+                so_far,
+            )
             cosine, sine = turning(natural - opening)
             turned = jnp.concatenate([attended, unturn(so_far * scale, cosine, sine)], axis=0)
             for side in range(2):
@@ -1594,9 +1606,9 @@
     def _():
         chain(1, 1)
 
-    mail_out(1)
     for at in range(2, depth - 1):
         chain(1, at)
+    mail_out(1)
     cross_over(1)
 
 

time: 238 us -> 236 us (level)
  no operation moved by 1% of the time
where the time goes in v6:
time: 236 us; the launch traced here: 235 us
  Pallas kernels  235 us (100%)
    pallas_call x1, Pallas kernels, reduce_call(): pl.pallas_call(functools.partial(reduce_kernel, depth), out_shape=(shape(...  116 us
    pallas_call x1, Pallas kernels, gather_call(): pl.pallas_call(functools.partial(gather_kernel, depth), out_shape=(shape(...  115 us

profile of v6, /device:TPU:0, one launch (start us, length us, event | category | flops | bytes accessed | tf_op | source)
XLA Modules:
  0.0 235.4 jit_solution(1072927400183159665)
XLA Ops:
  0.6 114.9 %gather_and_forward.1 = (bf16[16,256,256]{2,1,0:T(8,128)(2,1)}, bf16[16,256,512]{2,1,0:T(8,128)(2,1)}, bf16[16,256,1024]{2,1,0:T(8,128)(2,1)}, bf16[16,256,1024]...) custom-call(s32[2,4]{1,0:T(2,128)} %lengths_ref.3, ...), custom_call_target="tpu_custom_call" | custom-call | tf_op jit(solution)/shard_map/gather_and_forward/pallas_call | solution.py:973
  115.5 116.0 %backward_and_reduce.1 = (f32[256,1024]{1,0:T(8,128)}, f32[256,1024]{1,0:T(8,128)}, bf16[2,16,32,256]{3,2,1,0:T(8,128)(2,1)}, f32[32,1024]{1,0:T(8,128)}, f32[128,1024]{1,0:T(8,128)}, /*index=5*/f32[8,32]{1,0:T(8,128)}) custom-call(s32[2,4]{1,0:T(2,128)} %lengths_ref.3, s32[2,16]{1,0:T(2,128)} %dealing_ref.3, s32[2,16]{1,0:T(2,128)} %get-tuple-element.41.found, ...), custom_call_target="tpu_custom_call" | custom-call | tf_op jit(solution)/shard_map/backward_and_reduce/pallas_call | solution.py:1675
  231.5 3.7 %last_rows.1 = (bf16[256,1024]{1,0:T(8,128)(2,1)}, f32[256,1024]{1,0:T(8,128)}, f32[32,3072]{1,0:T(8,128)}, f32[32,1024]{1,0:T(8,128)}, f32[32,4096]{1,0:T(8,128...) custom-call(bf16[256,1024]{1,0:T(8,128)(2,1)} %bitcast.5, ...), custom_call_target="tpu_custom_call" | custom-call | tf_op jit(solution)/shard_map/last_rows/pallas_call | solution.py:1804

commit v7 on v6

--- a/solution.py
+++ b/solution.py
@@ -1608,8 +1608,8 @@
 
     for at in range(2, depth - 1):
         chain(1, at)
+    cross_over(1)
     mail_out(1)
-    cross_over(1)
 
 
     sum_out[...] = gather_total(0)

time: 236 us -> 236 us (level)
  no operation moved by 1% of the time
where the time goes in v7:
time: 236 us; the launch traced here: 235 us
  Pallas kernels  235 us (100%)
    pallas_call x1, Pallas kernels, reduce_call(): pl.pallas_call(functools.partial(reduce_kernel, depth), out_shape=(shape(...  116 us
    pallas_call x1, Pallas kernels, gather_call(): pl.pallas_call(functools.partial(gather_kernel, depth), out_shape=(shape(...  115 us

profile of v7, /device:TPU:0, one launch (start us, length us, event | category | flops | bytes accessed | tf_op | source)
XLA Modules:
  0.0 235.4 jit_solution(12593824721824082999)
XLA Ops:
  0.6 114.9 %gather_and_forward.1 = (bf16[16,256,256]{2,1,0:T(8,128)(2,1)}, bf16[16,256,512]{2,1,0:T(8,128)(2,1)}, bf16[16,256,1024]{2,1,0:T(8,128)(2,1)}, bf16[16,256,1024]...) custom-call(s32[2,4]{1,0:T(2,128)} %lengths_ref.3, ...), custom_call_target="tpu_custom_call" | custom-call | tf_op jit(solution)/shard_map/gather_and_forward/pallas_call | solution.py:973
  115.5 116.0 %backward_and_reduce.1 = (f32[256,1024]{1,0:T(8,128)}, f32[256,1024]{1,0:T(8,128)}, bf16[2,16,32,256]{3,2,1,0:T(8,128)(2,1)}, f32[32,1024]{1,0:T(8,128)}, f32[128,1024]{1,0:T(8,128)}, /*index=5*/f32[8,32]{1,0:T(8,128)}) custom-call(s32[2,4]{1,0:T(2,128)} %lengths_ref.3, s32[2,16]{1,0:T(2,128)} %dealing_ref.3, s32[2,16]{1,0:T(2,128)} %get-tuple-element.41.found, ...), custom_call_target="tpu_custom_call" | custom-call | tf_op jit(solution)/shard_map/backward_and_reduce/pallas_call | solution.py:1675
  231.5 3.7 %last_rows.1 = (bf16[256,1024]{1,0:T(8,128)(2,1)}, f32[256,1024]{1,0:T(8,128)}, f32[32,3072]{1,0:T(8,128)}, f32[32,1024]{1,0:T(8,128)}, f32[32,4096]{1,0:T(8,128...) custom-call(bf16[256,1024]{1,0:T(8,128)(2,1)} %bitcast.5, ...), custom_call_target="tpu_custom_call" | custom-call | tf_op jit(solution)/shard_map/last_rows/pallas_call | solution.py:1804
